TPU v7x, 512 devices: a whole 4x4x16 slice. The times are simulated.
512 devices in a mesh: ctx: 32 (over z, core), fsdp: 16 (over x, y).
Axes of the slice: x: 4, y: 4, z: 16, core: 2. Of those that a mesh axis runs over, the one named last changes fastest.
Arguments:
- tokens: bfloat16 [8192, 4096], P('ctx', 'fsdp'), may hold values from -6 to 6
- w_xz: bfloat16 [4096, 32, 256], P('ctx', 'fsdp'), may hold values from -0.09375 to 0.09375
- w_bc: bfloat16 [4096, 256], P('ctx'), may hold values from -0.09375 to 0.09375
- gain: float32 [32, 128], P('fsdp'), may hold values from 0.5 to 1.5
- skip: float32 [32], P('fsdp'), may hold values from 0.5 to 2
- decays: float32 [32, 8192], P('fsdp', 'ctx'), may hold values from 0.4 to 1
- boundaries: int32 [8192], P('ctx'), may hold values 0 or 1
Outputs:
- mixed: bfloat16 [8192, 32, 128], P('ctx', 'fsdp')
All inputs are finite; a program needn't handle non-finite values. No bound on the sum of `boundaries` on one device may be relied on, other than what follows from the above.
Results may differ from a plain program's by a relative error of at most 0.013.
Values may be sent and summed in bfloat16 or wider, within the bound.
No kernel may reach another device: no remote copies, remote signals or barrier semaphores. Data moves between devices by JAX's collectives and lax.ppermute only.
A program may use at most 64 MiB of HBM per device.

v0:
```python
import jax
import jax.numpy as jnp
from jax import lax
from jax.sharding import PartitionSpec as P

GROUP = 256


def carried_in(value, axis, join, neutral):
    count, mine = (lax.axis_size(axis), lax.axis_index(axis))
    pieces = jax.tree.map(lambda part: lax.all_gather(part, axis), value)
    so_far = jax.tree.map(
        lambda part, zero: jnp.full_like(part, 0) + jnp.asarray(zero, part.dtype), value, neutral
    )

    def hop(position, so_far):
        longer = join(so_far, jax.tree.map(lambda part: part[position], pieces))
        return jax.tree.map(lambda new, old: jnp.where(position < mine, new, old), longer, so_far)

    return lax.fori_loop(0, count - 1, hop, so_far)


def combine(earlier, later):
    return (earlier[0] * later[0], later[0][:, None, None] * earlier[1] + later[1])


def per_device(tokens, w_xz, w_bc, gain, skip, decays, boundaries):
    tok_rows = tokens.shape[0]
    head_count = w_xz.shape[1]
    head_width = w_xz.shape[2] // 2
    state_width = w_bc.shape[1] // 2
    fsdp_count = lax.axis_size("fsdp")
    whole = lax.all_gather(tokens, "fsdp", axis=1, tiled=True)
    pieces = (
        lax.all_gather(w_xz, "ctx", axis=0, tiled=True),
        lax.all_gather(w_bc, "ctx", axis=0, tiled=True),
    )
    count = pieces[0].shape[0]
    first = jnp.dot(whole, pieces[0].reshape(count, -1), preferred_element_type=jnp.float32)
    second = jnp.dot(whole, pieces[1], preferred_element_type=jnp.float32)
    proj = first
    map_local = jax.nn.silu(second).astype(jnp.bfloat16)
    proj = proj.reshape(tok_rows, head_count, 2, head_width)
    values = jax.nn.silu(proj[:, :, 0]).astype(jnp.bfloat16)
    gate = proj[:, :, 1].astype(jnp.bfloat16)
    blocks = tok_rows // GROUP
    block_values = values.reshape(blocks, GROUP, head_count, head_width)
    b_proj = map_local[:, :state_width].reshape(blocks, GROUP, state_width)
    c_proj = map_local[:, state_width:].reshape(blocks, GROUP, state_width)
    shrink_exponent = jnp.log(decays).reshape(head_count, blocks, GROUP).transpose(1, 0, 2)
    position = jnp.arange(GROUP)
    causal = position[:, None] >= position[None, :]
    lower_ones = causal.astype(jnp.float32)
    cumulative = jnp.einsum(
        "khj,ij->khi", shrink_exponent, lower_ones, precision=lax.Precision.HIGHEST
    )
    segment_ids = jnp.cumsum(boundaries.reshape(blocks, GROUP), axis=1)
    allowed = (segment_ids[:, :, None] == segment_ids[:, None, :]) & causal[None]
    decay_mat = jnp.where(
        allowed[:, None], jnp.exp(cumulative[:, :, :, None] - cumulative[:, :, None, :]), 0.0
    )
    scores = jnp.einsum("kin,kjn->kij", c_proj, b_proj, preferred_element_type=jnp.float32)
    weights = (decay_mat * scores[:, None]).astype(jnp.bfloat16)
    diagonal = jnp.einsum(
        "khij,kjhp->kihp", weights, block_values, preferred_element_type=jnp.float32
    )
    last_total = cumulative[:, :, -1]
    last_segment = segment_ids[:, -1]
    to_end = jnp.where(
        (segment_ids == last_segment[:, None])[:, None, :],
        jnp.exp(last_total[:, :, None] - cumulative),
        0.0,
    )
    scaled = (to_end.transpose(0, 2, 1)[:, :, :, None] * block_values.astype(jnp.float32)).astype(
        jnp.bfloat16
    )
    local_states = jnp.einsum("kjhp,kjn->khpn", scaled, b_proj, preferred_element_type=jnp.float32)
    carry_in = jnp.where((segment_ids == 0)[:, None, :], jnp.exp(cumulative), 0.0)
    carry_gate = jnp.where((last_segment == 0)[:, None], jnp.exp(last_total), 0.0)
    device_gate = carry_gate[0]
    device_state = local_states[0]
    identity = (jnp.ones_like(device_gate), jnp.zeros_like(device_state))
    incoming = carried_in((device_gate, device_state), "ctx", combine, identity)[1]
    offdiag = jnp.einsum(
        "in,hpn->ihp", c_proj[0].astype(jnp.float32), incoming, precision=lax.Precision.HIGHEST
    )
    pieces_out = diagonal[0] + offdiag * carry_in[0].T[:, :, None]
    output = pieces_out
    output = output + skip[None, :, None] * values.astype(jnp.float32)
    gated = output * jax.nn.silu(gate.astype(jnp.float32))
    squares = lax.psum(jnp.sum(gated * gated, axis=(1, 2)), "fsdp")
    mean_square = squares / (head_count * head_width * fsdp_count)
    normed = gated * lax.rsqrt(mean_square + 1e-05)[:, None, None] * gain[None]
    return normed.astype(jnp.bfloat16)


def solution(mesh):
    in_specs = (
        P("ctx", "fsdp"),
        P("ctx", "fsdp", None),
        P("ctx", None),
        P("fsdp", None),
        P("fsdp"),
        P("fsdp", "ctx"),
        P("ctx"),
    )
    out_specs = P("ctx", "fsdp", None)
    return jax.shard_map(
        per_device, mesh=mesh, in_specs=in_specs, out_specs=out_specs, check_vma=False
    )
```

profile of v0, /device:TPU:1, one launch (start us, length us, event | category | flops | bytes accessed | tf_op | source)
XLA Modules:
  0.0 385.4 jit_solution(9632781573677594797)
XLA Ops:
  14.0 63.8 %all-gather.7.cloned.1.call-done = bf16[256,4096]{1,0:T(8,128)(2,1)} async-done(((bf16[256,256]{1,0:T(8,128)(2,1)}), bf16[256,4096]{1,0:T(8,128)(2,1)}) %all-gather.7.cloned.1.call-update) | async-done | bytes 2097168 | tf_op jit(solution)/shard_map/all_gather | solution.py:33
  77.8 74.7 %all-gather.11.cloned.1.call-done = bf16[4096,256]{1,0:T(8,128)(2,1)} async-done(((bf16[128,256]{1,0:T(8,128)(2,1)}), bf16[4096,256]{1,0:T(8,128)(2,1)}) %all-gather.11.cloned.1.call-update) | async-done | bytes 2097168 | tf_op jit(solution)/shard_map/all_gather | solution.py:36
  152.5 2.9 multiply_convert_fusion.4
  155.5 69.9 %all-gather.9.cloned.1.call-done = bf16[4096,2,256]{2,1,0:T(2,128)(2,1)} async-done(((bf16[128,2,256]{2,1,0:T(2,128)(2,1)}), bf16[4096,2,256]{2,1,0:T(2,128)(2,1)}) %all-gather.9.cloned.1.call-update) | async-done | bytes 4194320 | tf_op jit(solution)/shard_map/all_gather | solution.py:35
  225.3 11.2 %copy.25 = bf16[4096,2,256]{0,2,1:T(8,128)(2,1)} copy(bf16[4096,2,256]{2,1,0:T(2,128)(2,1)} %all-gather.9.cloned.1.call-done) | data formatting | bytes 8388608 | tf_op jit(solution)/shard_map/reshape | solution.py:39
  236.5 3.6 fusion.1
  241.2 29.3 %all-gather = f32[32,2,1]{1,2,0:T(1,128)S(1)} all-gather(f32[1,2,1]{1,2,0:T(1,128)S(1)} %copy.20), channel_id=2, replica_groups=mesh['ctx'=32,'fsdp'=16] {'ctx'}, dimensions={0}, use_global_device_ids=true | all-gather | bytes 264 | tf_op jit(solution)/shard_map/all_gather | solution.py:11
  271.2 41.0 %all-gather.13.cloned.1.call-done = f32[64,128,128]{2,1,0:T(8,128)} async-done(((f32[2,128,128]{2,1,0:T(8,128)}), f32[64,128,128]{2,1,0:T(8,128)}) %all-gather.13.cloned.1.call-update) | async-done | bytes 4194320 | tf_op jit(solution)/shard_map/all_gather | solution.py:11
  312.2 32.1 %while.14 = (s32[]{:T(128)}, f32[2,128,128]{2,1,0:T(8,128)S(1)}, s32[]{:T(128)}, f32[32,2]{1,0:T(8,128)S(1)}, f32[32,2,128,128]{3,2,1,0:T(8,128)}, /*index=5*/s32[]{:T(128)}, s32[]{:T(128)}) while((s32[]{:T(128)}, f32[2,128,128]{2,1,0:T(8,128)S(1)}, s32[]{:T(128)}, f32[32,2]{1,0:T(8,128)S(1)}, f32[32,2,128,128]{3,2,1,0:T(8,128)}, ...), condition=%wide.region_3.4_spmd.clone, body=%wide.region_2.3_spmd.clone.sunk | while | flops 131076 | bytes 393353 | solution.py:20
  312.2 1.0 fusion.46
  313.2 1.0 fusion.46
  314.3 1.0 fusion.46
  315.3 1.0 fusion.46
  316.3 1.0 fusion.46
  317.4 1.0 fusion.46
  318.4 1.0 fusion.46
  319.5 1.0 fusion.46
  320.5 1.0 fusion.46
  322.6 1.0 fusion.46
  323.6 1.0 fusion.46
  324.6 1.0 fusion.46
  326.7 1.0 fusion.46
  327.8 1.0 fusion.46
  344.7 33.3 %psum.7 = f32[256]{0:T(256)S(1)} all-reduce(f32[256]{0:T(256)S(1)} %get-tuple-element.149), channel_id=1, replica_groups=mesh['ctx'=32,'fsdp'=16] {'fsdp'}, use_global_device_ids=true, to_apply=%region_5.6 | all-reduce | flops 256 | bytes 2048 | tf_op jit(solution)/shard_map/psum | solution.py:91
  (84 shorter events, 26.2 us)
Async XLA Ops:
  6.5 71.2 %all-gather.7.cloned.1.call-start = ((), (), s32[]{:S(2)}) async-start(), calls=%async_computation | async-start | bytes 2228224 | tf_op jit(solution)/shard_map/all_gather | solution.py:33
  7.3 145.2 %all-gather.11.cloned.1.call-start = ((), (), s32[]{:S(2)}) async-start(), calls=%async_computation.2 | async-start | bytes 2162688 | tf_op jit(solution)/shard_map/all_gather | solution.py:36
  8.0 217.3 %all-gather.9.cloned.1.call-start = ((), (), s32[]{:S(2)}) async-start(), calls=%async_computation.1 | async-start | bytes 4325376 | tf_op jit(solution)/shard_map/all_gather | solution.py:35
  8.7 303.4 %all-gather.13.cloned.1.call-start = ((), (), s32[]{:S(2)}) async-start(), calls=%async_computation.3 | async-start | bytes 4325376 | tf_op jit(solution)/shard_map/all_gather | solution.py:11
  155.5 81.1 %copy-start.1 = (bf16[256,4096]{1,0:T(8,128)(2,1)S(1)}, bf16[256,4096]{1,0:T(8,128)(2,1)}, u32[]{:S(2)}) copy-start(bf16[256,4096]{1,0:T(8,128)(2,1)} %all-gather.7.cloned.1.call-done) | copy-start | bytes 6291460
  270.8 73.5 %copy-start.2 = (f32[2]{0:T(128)S(1)}, f32[2]{0:T(128)}, u32[]{:S(2)}) copy-start(f32[2]{0:T(128)} %param.13) | copy-start | bytes 28
  312.2 65.8 %copy-start = (f32[2,128]{1,0:T(2,128)S(1)}, f32[2,128]{1,0:T(2,128)}, u32[]{:S(2)}) copy-start(f32[2,128]{1,0:T(2,128)} %param.12) | copy-start | bytes 3076
Sparse Core Ops, SparseCore 0:
  10.3 67.3 all-gather.6
  79.9 72.5 all-gather.10
  154.6 70.6 all-gather.8
  241.2 70.9 all-gather.12
where the time goes:
time: 392 us; the launch traced here: 385 us
  waiting for transfers between devices  251 us (64%)
  blocking collectives  62.6 us (16%)
  other arithmetic  32.6 us (8%)
  between operations  14.5 us (4%)
  local copies, waits for them, and re-layouts  13.8 us (4%)
  matrix products  9.24 us (2%)
    all_gather x1, waiting for transfers between devices, per_device(): lax.all_gather(w_bc, 'ctx', axis=0, tiled=True)  74.7 us
    all_gather x1, waiting for transfers between devices, per_device(): lax.all_gather(w_xz, 'ctx', axis=0, tiled=True)  69.9 us
    all_gather x1, waiting for transfers between devices, per_device(): whole = lax.all_gather(tokens, 'fsdp', axis=1, tiled=True)  63.8 us
    all_gather x1, waiting for transfers between devices, carried_in(): pieces = jax.tree.map(lambda part: lax.all_gather(part, axis), value)  41 us
    psum x1, blocking collectives, per_device(): squares = lax.psum(jnp.sum(gated * gated, axis=(1, 2)), 'fsdp')  33.3 us
    select_n x31, other arithmetic, hop(): jnp.where(position < mine, new, old)  30.8 us
    all_gather x1, blocking collectives, carried_in(): pieces = jax.tree.map(lambda part: lax.all_gather(part, axis), value)  29.3 us
    reshape x1, local copies, waits for them, and re-layouts, per_device(): pieces[0].reshape(count, -1)  11.2 us
  transfers between devices with their start and end apart: 4, of which 4 were waited for; matrix products, arithmetic and copies ran while one was open for 2% of the time, Pallas kernels for 0%

commit v1 on v0

v1 whole, which is shorter than its diff:
```python
import jax
import jax.numpy as jnp
from jax import lax
from jax.sharding import PartitionSpec as P

F32 = jnp.float32
BF16 = jnp.bfloat16


def swap_cores(x, count):
    return lax.ppermute(x, "ctx", [(i, i ^ 1) for i in range(count)])


def to_all(x, axis):
    size = lax.axis_size(axis)
    return lax.all_to_all(jnp.broadcast_to(x[None], (size,) + x.shape), axis, 0, 0)


def per_device(tokens, w_xz, w_bc, gain, skip, decays, boundaries):
    rows = tokens.shape[0]
    heads = w_xz.shape[1]
    width = w_xz.shape[2] // 2
    n_state = w_bc.shape[1] // 2
    n_ctx, n_fsdp = lax.axis_size("ctx"), lax.axis_size("fsdp")
    n_chip = n_ctx // 2
    ctx, fsdp = lax.axis_index("ctx"), lax.axis_index("fsdp")
    core, chip = ctx % 2, ctx // 2
    same_core = [[2 * z + c for z in range(n_chip)] for c in range(2)]

    w_all = lax.all_gather(w_xz.reshape(w_xz.shape[0], -1), "ctx", axis=0, tiled=True)
    tok = to_all(tokens, "fsdp")
    share = w_bc.shape[1] // n_fsdp
    part = lax.dynamic_slice_in_dim(w_bc.T, fsdp * share, share, axis=0)
    part = lax.all_gather(part, "ctx", axis=0, axis_index_groups=same_core)
    other = swap_cores(part, n_ctx)
    even, odd = jnp.where(core == 0, part, other), jnp.where(core == 0, other, part)
    part = jnp.stack([even, odd], axis=1)
    part = part.transpose(2, 0, 1, 3).reshape(share, n_fsdp, -1)
    maps_t = jnp.einsum("sfk,fik->si", part, tok, preferred_element_type=F32)
    maps_t = jax.nn.silu(maps_t).astype(BF16)
    maps_t = to_all(maps_t, "fsdp").reshape(2, n_state, rows)
    b_t, c_t = maps_t[0], maps_t[1]

    position = jnp.arange(rows)
    causal = position[:, None] >= position[None, :]
    cum = jnp.einsum(
        "hj,ij->hi", jnp.log(decays), causal.astype(F32), precision=lax.Precision.HIGHEST
    )
    seg = jnp.cumsum(boundaries)
    allowed = (seg[:, None] == seg[None, :]) & causal
    decay = jnp.where(allowed[None], jnp.exp(cum[:, :, None] - cum[:, None, :]), 0.0)
    scores = jnp.einsum("ni,nj->ij", c_t, b_t, preferred_element_type=F32)
    weights = (decay * scores[None]).astype(BF16)
    total, last = cum[:, -1], seg[-1]
    to_end = jnp.where((seg == last)[None], jnp.exp(total[:, None] - cum), 0.0)
    carry_in = jnp.where((seg == 0)[None], jnp.exp(cum), 0.0)
    gate_end = jnp.where(last == 0, jnp.exp(total), 0.0)

    proj = jnp.einsum(
        "fik,fkn->in", tok, w_all.reshape(n_fsdp, -1, w_all.shape[1]), preferred_element_type=F32
    )
    proj = proj.reshape(rows, heads, 2, width)
    values = jax.nn.silu(proj[:, :, 0]).astype(BF16)
    gate = proj[:, :, 1].astype(BF16)
    value_f = values.astype(F32)
    scaled = (to_end.T[:, :, None] * value_f).astype(BF16)
    local = jnp.einsum("jhp,nj->hpn", scaled, b_t, preferred_element_type=F32)

    tail = jnp.broadcast_to(gate_end[:, None, None], (heads, 8, n_state))
    mine = jnp.concatenate([local, tail], axis=1)
    keep = jnp.where(core == 0, mine[0], mine[1])
    got = swap_cores(jnp.where(core == 0, mine[1], mine[0]), n_ctx)
    first, second = jnp.where(core == 0, keep, got), jnp.where(core == 0, got, keep)
    s0, g0, s1, g1 = first[:width], first[width, 0], second[:width], second[width, 0]
    s_chip, g_chip = g1 * s0 + s1, g0 * g1
    g_hi = g_chip.astype(BF16)
    g_mid = (g_chip - g_hi.astype(F32)).astype(BF16)
    g_lo = (g_chip - g_hi.astype(F32) - g_mid.astype(F32)).astype(BF16)
    g_row = jnp.stack([g_hi, g_mid, g_lo] + [jnp.zeros_like(g_hi)] * 13)
    packed = jnp.concatenate(
        [s_chip.astype(BF16), jnp.broadcast_to(g_row[:, None], (16, n_state))], axis=0
    )
    everyone = lax.all_gather(packed, "ctx", axis=0, axis_index_groups=same_core)
    g_all = everyone[:, width : width + 3, 0].astype(F32)
    g_all = g_all[:, 0] + g_all[:, 1] + g_all[:, 2]
    at = jnp.arange(n_chip)
    between = (at[None, :] > at[:, None]) & (at[None, :] < chip)
    coef = jnp.prod(jnp.where(between, g_all[None, :], 1.0), axis=1)
    coef = jnp.where(at < chip, coef, 0.0)
    e0 = jnp.sum(coef[:, None, None] * everyone[:, :width].astype(F32), axis=0)
    e1 = g0 * e0 + s0
    kept = jnp.where(core == 0, e0, e1)
    came = swap_cores(jnp.where(core == 0, e1, e0), n_ctx)
    incoming = jnp.stack([jnp.where(core == 0, kept, came), jnp.where(core == 0, came, kept)])

    diagonal = jnp.einsum("hij,jhp->ihp", weights, values, preferred_element_type=F32)
    in_hi = incoming.astype(BF16)
    in_lo = (incoming - in_hi.astype(F32)).astype(BF16)
    offdiag = jnp.einsum("ni,hpn->ihp", c_t, in_hi, preferred_element_type=F32)
    offdiag = offdiag + jnp.einsum("ni,hpn->ihp", c_t, in_lo, preferred_element_type=F32)
    output = diagonal + offdiag * carry_in.T[:, :, None] + skip[None, :, None] * value_f
    gated = output * jax.nn.silu(gate.astype(F32))
    squares = jnp.sum(gated * gated, axis=(1, 2))
    squares = jnp.sum(to_all(squares, "fsdp"), axis=0)
    scale = lax.rsqrt(squares / (heads * width * n_fsdp) + 1e-05)
    return (gated * scale[:, None, None] * gain[None]).astype(BF16)


def solution(mesh):
    in_specs = (
        P("ctx", "fsdp"),
        P("ctx", "fsdp", None),
        P("ctx", None),
        P("fsdp", None),
        P("fsdp"),
        P("fsdp", "ctx"),
        P("ctx"),
    )
    out_specs = P("ctx", "fsdp", None)
    return jax.shard_map(
        per_device, mesh=mesh, in_specs=in_specs, out_specs=out_specs, check_vma=False
    )
```

time: 392 us -> 166 us (0.42); the launches traced: 385 us -> 166 us
  waiting for transfers between devices: 251 us -> 28.1 us
  starting transfers between devices: 0.12 us -> 33.9 us
  other arithmetic: 32.6 us -> 3.84 us
  blocking collectives: 62.6 us -> 67.8 us
  matrix products: 9.24 us -> 4.51 us
    all_gather x4 -> x1, waiting for transfers between devices: 249 us -> 20.2 us  [per_device(): lax.all_gather(w_xz.reshape(w_xz.shape[0], -1), 'ctx', axis=0, tiled=True)]
    psum x1 -> x0, blocking collectives: 33.3 us -> none  [per_device(): squares = lax.psum(jnp.sum(gated * gated, axis=(1, 2)), 'fsdp')]
    select_n x31 -> x6, other arithmetic: 30.8 us -> 0.82 us  [the longest x1 0.7 us: per_device(): came = swap_cores(jnp.where(core == 0, e1, e0), n_ctx)]
    all_gather x1 -> x2, blocking collectives: 29.3 us -> 55 us  [the longest x1 30.6 us: per_device(): part = lax.all_gather(part, 'ctx', axis=0, axis_index_groups=same_core)]
    ppermute x0 -> x3, starting transfers between devices: none -> 19.2 us  [swap_cores(): return lax.ppermute(x, 'ctx', [(i, i ^ 1) for i in range(count)])]
    all_to_all x0 -> x2, starting transfers between devices: none -> 14.6 us  [to_all(): lax.all_to_all(jnp.broadcast_to(x[None], (size,) + x.shape), axis, 0, 0)]
    all_to_all x0 -> x1, blocking collectives: none -> 12.7 us  [to_all(): lax.all_to_all(jnp.broadcast_to(x[None], (size,) + x.shape), axis, 0, 0)]
    reshape x1, local copies, waits for them, and re-layouts: 11.2 us -> 1.7 us  [per_device(): w_xz.reshape(w_xz.shape[0], -1)]
  transfers between devices with their start and end apart: 4 -> 6, of which waited for: 4 -> 4; matrix products, arithmetic and copies ran while one was open for 2% -> 4% of each run, Pallas kernels for 0% -> 0%
where the time goes in v1:
time: 166 us
  blocking collectives  67.8 us (41%)
  starting transfers between devices  33.9 us (20%)
  waiting for transfers between devices  28.1 us (17%)
  between operations  15.7 us (9%)
  local copies, waits for them, and re-layouts  11.8 us (7%)
  matrix products  4.51 us (3%)
  other arithmetic  3.84 us (2%)
    all_gather x1, blocking collectives, per_device(): part = lax.all_gather(part, 'ctx', axis=0, axis_index_groups=same_core)  30.6 us
    all_gather x1, blocking collectives, per_device(): lax.all_gather(packed, 'ctx', axis=0, axis_index_groups=same_core)  24.5 us
    all_gather x1, waiting for transfers between devices, per_device(): lax.all_gather(w_xz.reshape(w_xz.shape[0], -1), 'ctx', axis=0, tiled=True)  20.2 us
    ppermute x3, starting transfers between devices, swap_cores(): return lax.ppermute(x, 'ctx', [(i, i ^ 1) for i in range(count)])  19.2 us
    all_to_all x2, starting transfers between devices, to_all(): lax.all_to_all(jnp.broadcast_to(x[None], (size,) + x.shape), axis, 0, 0)  14.6 us
    all_to_all x1, blocking collectives, to_all(): lax.all_to_all(jnp.broadcast_to(x[None], (size,) + x.shape), axis, 0, 0)  12.7 us
    all_to_all x2, waiting for transfers between devices, to_all(): lax.all_to_all(jnp.broadcast_to(x[None], (size,) + x.shape), axis, 0, 0)  6.69 us
    unnamed x13, local copies, waits for them, and re-layouts  3.8 us
  transfers between devices with their start and end apart: 6, of which 4 were waited for; matrix products, arithmetic and copies ran while one was open for 4% of the time, Pallas kernels for 0%

profile of v1, /device:TPU:1, one launch (start us, length us, event | category | flops | bytes accessed | tf_op | source)
XLA Modules:
  0.0 165.6 jit_solution(5829619340590674381)
XLA Ops:
  6.5 1.7 %copy.39 = bf16[128,2,256]{0,2,1:T(8,128)(2,1)} copy(bf16[128,2,256]{2,1,0:T(2,128)(2,1)} %param.8) | data formatting | bytes 262144 | tf_op jit(solution)/shard_map/reshape | solution.py:30
  8.3 2.4 %broadcast_in_dim.60 = bf16[16,256,256]{2,1,0:T(8,128)(2,1)} broadcast(bf16[256,256]{1,0:T(8,128)(2,1)} %param.7), dimensions={1,2} | broadcast | bytes 2228224 | tf_op jit(solution)/shard_map/broadcast_in_dim | solution.py:16
  10.7 7.7 %all-to-all-start = ((bf16[16,256,256]{2,1,0:T(8,128)(2,1)}), bf16[16,256,256]{2,1,0:T(8,128)(2,1)S(1)}, u32[]{:S(2)}, u32[]{:S(2)}) async-start(bf16[16,256,256]{2,1,0:T(8,128)(2,1)} %broadcast_in_dim.60), calls=%async_computation | async-start | bytes 4194304 | tf_op jit(solution)/shard_map/all_to_all | solution.py:16
  18.6 30.6 %all-gather = bf16[256,128]{1,0:T(8,128)(2,1)S(1)} all-gather(bf16[16,128]{1,0:T(8,128)(2,1)S(1)} %bitcast.131), channel_id=2, replica_groups={{0,32,64,96,128,160,192,224,256,288,320,352,384,416,448,480},{16,48,80,..., dimensions={0}, use_global_device_ids=true | all-gather | bytes 69632 | tf_op jit(solution)/shard_map/all_gather | solution.py:34
  49.2 8.1 %collective-permute-start = (bf16[16,16,128]{2,1,0:T(8,128)(2,1)S(1)}, bf16[16,16,128]{2,1,0:T(8,128)(2,1)S(1)}, u32[]{:S(2)}, u32[]{:S(2)}) collective-permute-start(bf16[16,16,128]{2,1,0:T(8,128)(2,1)S(1)} %bitcast.128), channel_id=1, source_target_pairs={{0,16},{16,0},{32,48},{48,32},{64,80},{80,64},{96,112},{112,96},{1... | collective-permute-start | bytes 196616 | tf_op jit(solution)/shard_map/ppermute | solution.py:11
  57.8 0.6 slice.68
  58.9 0.6 broadcast_compare_fusion.1
  60.3 0.7 multiply_convert_fusion.4
  61.0 0.7 broadcast_in_dim.63
  61.6 6.9 %all-to-all-start.1 = ((bf16[16,16,256]{2,1,0:T(8,128)(2,1)}), bf16[16,16,256]{2,1,0:T(8,128)(2,1)S(1)}, u32[]{:S(2)}, u32[]{:S(2)}) async-start(bf16[16,16,256]{2,1,0:T(8,128)(2,1)} %broadcast_in_dim.63), calls=%async_computation.1 | async-start | bytes 262144 | tf_op jit(solution)/shard_map/all_to_all | solution.py:16
  68.6 6.7 %all-to-all-done.1 = bf16[16,16,256]{2,1,0:T(8,128)(2,1)S(1)} async-done(((bf16[16,16,256]{2,1,0:T(8,128)(2,1)}), bf16[16,16,256]{2,1,0:T(8,128)(2,1)S(1)}, u32[]{:S(2)}, u32[]{:S(2)}) %all-to-all-start.1) | async-done | bytes 131104 | tf_op jit(solution)/shard_map/all_to_all | solution.py:16
  75.3 20.2 %all-gather.4.cloned.1.call-done = bf16[4096,512]{0,1:T(8,128)(2,1)} async-done(((bf16[128,512]{0,1:T(8,128)(2,1)}), bf16[4096,512]{0,1:T(8,128)(2,1)}) %all-gather.4.cloned.1.call-update) | async-done | bytes 4194320 | tf_op jit(solution)/shard_map/all_gather | solution.py:30
  95.4 3.6 %copy.45 = bf16[64,8,16,256]{3,2,1,0:T(8,128)(2,1)S(1)} copy(bf16[64,8,16,256]{3,1,2,0:T(8,128)(2,1)} %bitcast.121) | data formatting | bytes 8388608
  99.1 2.4 %fusion.3 = f32[256,2,2,128]{0,3,2,1:T(8,128)S(1)} fusion(bf16[2,2,128,16,256]{4,3,2,1,0:T(8,128)(2,1)S(1)} %bitcast.122, bf16[16,256,256]{2,1,0:T(8,128)(2,1)S(1)} %all-to-all-done), kind=kOutput, calls=%fused_computation.3 | convolution fusion | flops 1073741824 | bytes 6815744 | tf_op jit(solution)/shard_map/fik,fkn->in/dot_general | solution.py:59
  101.8 2.2 %collective-permute-start.1 = (f32[136,128]{1,0:T(8,128)S(1)}, f32[136,128]{1,0:T(8,128)S(1)}, u32[]{:S(2)}, u32[]{:S(2)}) collective-permute-start(f32[136,128]{1,0:T(8,128)S(1)} %select_bitcast_fusion), channel_id=1, source_target_pairs={{0,16},{16,0},{32,48},{48,32},{64,80},{80,64},{96,112},{112,96},{1... | collective-permute-start | bytes 208904 | tf_op jit(solution)/shard_map/ppermute | solution.py:11
  104.2 0.8 collective-permute-done.1
  105.5 0.6 slice.91
  106.1 0.7 fusion.42
  108.4 24.5 %all-gather.1 = bf16[2304,128]{1,0:T(8,128)(2,1)S(1)} all-gather(bf16[144,128]{1,0:T(8,128)(2,1)S(1)} %pad_maximum_fusion.2), channel_id=3, replica_groups={{0,32,64,96,128,160,192,224,256,288,320,352,384,416,448,480},{16,48,80,..., dimensions={0}, use_global_device_ids=true | all-gather | bytes 626688 | tf_op jit(solution)/shard_map/all_gather | solution.py:83
  133.3 0.7 fusion.43
  134.0 9.0 %collective-permute-start.2 = (f32[128,128]{1,0:T(8,128)S(1)}, f32[128,128]{1,0:T(8,128)S(1)}, u32[]{:S(2)}, u32[]{:S(2)}) collective-permute-start(f32[128,128]{1,0:T(8,128)S(1)} %fusion.43), channel_id=1, source_target_pairs={{0,16},{16,0},{32,48},{48,32},{64,80},{80,64},{96,112},{112,96},{1... | collective-permute-start | bytes 196616 | tf_op jit(solution)/shard_map/ppermute | solution.py:11
  143.9 0.7 select_bitcast_fusion.2
  145.1 12.7 %all_to_all.16 = f32[16,1,256]{2,1,0:T(1,128)S(1)} all-to-all(f32[16,1,256]{2,1,0:T(1,128)S(1)} %broadcast_in_dim.113), channel_id=1, replica_groups=mesh['ctx'=32,'fsdp'=16] {'fsdp'}, dimensions={0} | all-to-all | bytes 32768 | tf_op jit(solution)/shard_map/all_to_all | solution.py:16
  157.9 0.8 copy.36
  (55 shorter events, 4.6 us)
Async XLA Ops:
  6.5 11.9 %copy-start = (bf16[128,256]{1,0:T(8,128)(2,1)S(1)}, bf16[128,256]{1,0:T(8,128)(2,1)}, u32[]{:S(2)}) copy-start(bf16[128,256]{1,0:T(8,128)(2,1)} %param.9) | copy-start | bytes 196612
  6.5 88.9 %all-gather.4.cloned.1.call-start = ((), (), s32[]{:S(2)}) async-start(), calls=%async_computation.3 | async-start | bytes 4325376 | tf_op jit(solution)/shard_map/all_gather | solution.py:30
  10.7 46.5 %copy-start.2 = (s32[256]{0:T(256)S(1)}, s32[256]{0:T(256)}, u32[]{:S(2)}) copy-start(s32[256]{0:T(256)} %param.13) | copy-start | bytes 3076
  10.7 47.7 %copy-start.3 = (f32[2,256]{1,0:T(2,128)S(1)}, f32[2,256]{1,0:T(2,128)}, u32[]{:S(2)}) copy-start(f32[2,256]{1,0:T(2,128)} %param.12) | copy-start | bytes 6148
  10.7 49.6 %all-to-all-start = ((bf16[16,256,256]{2,1,0:T(8,128)(2,1)}), bf16[16,256,256]{2,1,0:T(8,128)(2,1)S(1)}, u32[]{:S(2)}, u32[]{:S(2)}) async-start(bf16[16,256,256]{2,1,0:T(8,128)(2,1)} %broadcast_in_dim.60), calls=%async_computation | async-start | bytes 4194304 | tf_op jit(solution)/shard_map/all_to_all | solution.py:16
  49.2 11.1 %collective-permute-start = (bf16[16,16,128]{2,1,0:T(8,128)(2,1)S(1)}, bf16[16,16,128]{2,1,0:T(8,128)(2,1)S(1)}, u32[]{:S(2)}, u32[]{:S(2)}) collective-permute-start(bf16[16,16,128]{2,1,0:T(8,128)(2,1)S(1)} %bitcast.128), channel_id=1, source_target_pairs={{0,16},{16,0},{32,48},{48,32},{64,80},{80,64},{96,112},{112,96},{1... | collective-permute-start | bytes 196616 | tf_op jit(solution)/shard_map/ppermute | solution.py:11
  61.6 13.7 %all-to-all-start.1 = ((bf16[16,16,256]{2,1,0:T(8,128)(2,1)}), bf16[16,16,256]{2,1,0:T(8,128)(2,1)S(1)}, u32[]{:S(2)}, u32[]{:S(2)}) async-start(bf16[16,16,256]{2,1,0:T(8,128)(2,1)} %broadcast_in_dim.63), calls=%async_computation.1 | async-start | bytes 262144 | tf_op jit(solution)/shard_map/all_to_all | solution.py:16
  101.8 3.2 %collective-permute-start.1 = (f32[136,128]{1,0:T(8,128)S(1)}, f32[136,128]{1,0:T(8,128)S(1)}, u32[]{:S(2)}, u32[]{:S(2)}) collective-permute-start(f32[136,128]{1,0:T(8,128)S(1)} %select_bitcast_fusion), channel_id=1, source_target_pairs={{0,16},{16,0},{32,48},{48,32},{64,80},{80,64},{96,112},{112,96},{1... | collective-permute-start | bytes 208904 | tf_op jit(solution)/shard_map/ppermute | solution.py:11
  108.3 36.4 %copy-start.4 = (f32[2]{0:T(128)S(1)}, f32[2]{0:T(128)}, u32[]{:S(2)}) copy-start(f32[2]{0:T(128)} %param.11) | copy-start | bytes 28
  134.0 9.9 %collective-permute-start.2 = (f32[128,128]{1,0:T(8,128)S(1)}, f32[128,128]{1,0:T(8,128)S(1)}, u32[]{:S(2)}, u32[]{:S(2)}) collective-permute-start(f32[128,128]{1,0:T(8,128)S(1)} %fusion.43), channel_id=1, source_target_pairs={{0,16},{16,0},{32,48},{48,32},{64,80},{80,64},{96,112},{112,96},{1... | collective-permute-start | bytes 196616 | tf_op jit(solution)/shard_map/ppermute | solution.py:11
  143.3 14.5 %copy-start.1 = (f32[2,128]{1,0:T(2,128)S(1)}, f32[2,128]{1,0:T(2,128)}, u32[]{:S(2)}) copy-start(f32[2,128]{1,0:T(2,128)} %param.10) | copy-start | bytes 3076
Sparse Core Ops, SparseCore 0:
  9.4 85.9 all-gather.3

commit v2 on v1

v2 whole, which is shorter than its diff:
```python
import functools

import jax
import jax.numpy as jnp
from jax import lax
from jax.experimental import pallas as pl
from jax.experimental.pallas import tpu as pltpu
from jax.sharding import PartitionSpec as P

F32 = jnp.float32
BF16 = jnp.bfloat16
PARAMS = pltpu.CompilerParams(vmem_limit_bytes=48 * 1024 * 1024)


def swap_cores(x):
    return lax.ppermute(x, "ctx", [(i, i ^ 1) for i in range(lax.axis_size("ctx"))])


def to_all(x, axis, groups=None):
    size = lax.axis_size(axis) if groups is None else len(groups[0])
    copies = jnp.broadcast_to(x[None], (size,) + x.shape)
    return lax.all_to_all(copies, axis, 0, 0, axis_index_groups=groups)


def maps_kernel(tok_ref, bc_ref, out_ref):
    acc = jnp.zeros(out_ref.shape, F32)
    for f in range(0, tok_ref.shape[0], 2):
        tok = jnp.concatenate([tok_ref[f], tok_ref[f + 1]], axis=1)
        bc = jnp.concatenate([bc_ref[f], bc_ref[f + 1]], axis=1)
        acc += lax.dot_general(bc, tok, (((1,), (1,)), ((), ())), preferred_element_type=F32)
    out_ref[...] = acc


def proj_kernel(n_w, tok_ref, *refs):
    out_ref = refs[-1]
    acc = jnp.zeros(out_ref.shape, F32)
    for f in range(0, tok_ref.shape[0], 2):
        tok = jnp.concatenate([tok_ref[f], tok_ref[f + 1]], axis=1)
        w = jnp.concatenate([r[g] for g in (f, f + 1) for r in refs[:n_w]], axis=0)
        acc += jnp.dot(tok, w, preferred_element_type=F32)
    out_ref[...] = acc


def project(tok, *ws):
    return pl.pallas_call(
        functools.partial(proj_kernel, len(ws)),
        out_shape=jax.ShapeDtypeStruct((tok.shape[1], ws[0].shape[2]), F32),
        compiler_params=PARAMS,
    )(tok, *ws)


def per_device(tokens, w_xz, w_bc, gain, skip, decays, boundaries):
    rows = tokens.shape[0]
    heads = w_xz.shape[1]
    width = w_xz.shape[2] // 2
    n_state = w_bc.shape[1] // 2
    n_ctx, n_fsdp = lax.axis_size("ctx"), lax.axis_size("fsdp")
    n_chip = n_ctx // 2
    ctx, fsdp = lax.axis_index("ctx"), lax.axis_index("fsdp")
    core, chip = ctx % 2, ctx // 2
    same_core = [[2 * z + c for z in range(n_chip)] for c in range(2)]
    depth = w_xz.shape[0]

    def mine_other(a, b):
        return jnp.where(core == 0, a, b), jnp.where(core == 0, b, a)

    w_gate = w_xz[:, :, width:].reshape(depth, -1)
    w_gate = lax.all_gather(w_gate, "ctx", axis=0, axis_index_groups=same_core)

    tok_mine, tok_other = mine_other(tokens[:, :depth], tokens[:, depth:])
    tok = jnp.concatenate([tok_mine, swap_cores(tok_other)], axis=0)
    tok = to_all(tok, "fsdp")

    share = w_bc.shape[1] // n_fsdp
    w_val = w_xz[:, :, :width].reshape(depth, -1)
    n_rest = 16
    bc_part = lax.dynamic_slice_in_dim(w_bc.T, fsdp * share, share, axis=0)
    rest = w_val[depth - n_rest :]
    small = jnp.concatenate([bc_part] + [rest[:, h * width : (h + 1) * width] for h in range(heads)])
    small = to_all(small, "ctx", same_core)
    bc_all = small[:, :share]
    rest_all = jnp.concatenate(
        [small[:, share + h * n_rest : share + (h + 1) * n_rest] for h in range(heads)], axis=2
    )
    w_val_all = lax.all_gather(
        w_val[: depth - n_rest], "ctx", axis=0, axis_index_groups=same_core
    )

    maps_t = pl.pallas_call(
        maps_kernel,
        out_shape=jax.ShapeDtypeStruct((share, 2 * rows), F32),
        compiler_params=PARAMS,
    )(tok, bc_all)
    maps_t = maps_t[:, :rows] + swap_cores(maps_t[:, rows:])
    maps_t = jax.nn.silu(maps_t).astype(BF16)
    maps_t = to_all(maps_t, "fsdp").reshape(2, n_state, rows)
    b_t, c_t = maps_t[0], maps_t[1]

    proj_v = project(tok, w_val_all, rest_all)
    proj_v = proj_v[:rows] + swap_cores(proj_v[rows:])
    values = jax.nn.silu(proj_v).astype(BF16).reshape(rows, heads, width)

    position = jnp.arange(rows)
    causal = position[:, None] >= position[None, :]
    cum = jnp.einsum(
        "hj,ij->hi", jnp.log(decays), causal.astype(F32), precision=lax.Precision.HIGHEST
    )
    seg = jnp.cumsum(boundaries)
    allowed = (seg[:, None] == seg[None, :]) & causal
    decay = jnp.where(allowed[None], jnp.exp(cum[:, :, None] - cum[:, None, :]), 0.0)
    scores = jnp.einsum("ni,nj->ij", c_t, b_t, preferred_element_type=F32)
    weights = (decay * scores[None]).astype(BF16)
    total, last = cum[:, -1], seg[-1]
    to_end = jnp.where((seg == last)[None], jnp.exp(total[:, None] - cum), 0.0)
    carry_in = jnp.where((seg == 0)[None], jnp.exp(cum), 0.0)
    gate_end = jnp.where(last == 0, jnp.exp(total), 0.0)

    value_f = values.astype(F32)
    scaled = (to_end.T[:, :, None] * value_f).astype(BF16)
    local = jnp.einsum("nj,jhp->hnp", b_t, scaled, preferred_element_type=F32)

    tail = jnp.broadcast_to(gate_end[:, None, None], (heads, 8, width))
    mine = jnp.concatenate([local, tail], axis=1)
    keep, send = mine_other(mine[0], mine[1])
    first, second = mine_other(keep, swap_cores(send))
    s0, g0, s1, g1 = first[:n_state], first[n_state, 0], second[:n_state], second[n_state, 0]
    s_chip, g_chip = g1 * s0 + s1, g0 * g1
    g_hi = g_chip.astype(BF16)
    g_mid = (g_chip - g_hi.astype(F32)).astype(BF16)
    g_lo = (g_chip - g_hi.astype(F32) - g_mid.astype(F32)).astype(BF16)
    g_row = jnp.stack([g_hi, g_mid, g_lo] + [jnp.zeros_like(g_hi)] * 13)
    packed = jnp.concatenate(
        [s_chip.astype(BF16), jnp.broadcast_to(g_row[:, None], (16, width))], axis=0
    )
    everyone = lax.all_gather(packed, "ctx", axis=0, axis_index_groups=same_core)
    g_all = everyone[:, n_state : n_state + 3, 0].astype(F32)
    g_all = g_all[:, 0] + g_all[:, 1] + g_all[:, 2]
    at = jnp.arange(n_chip)
    between = (at[None, :] > at[:, None]) & (at[None, :] < chip)
    coef = jnp.prod(jnp.where(between, g_all[None, :], 1.0), axis=1)
    coef = jnp.where(at < chip, coef, 0.0)
    e0 = jnp.sum(coef[:, None, None] * everyone[:, :n_state].astype(F32), axis=0)
    e1 = g0 * e0 + s0
    kept, give = mine_other(e0, e1)
    incoming = jnp.stack(mine_other(kept, swap_cores(give)))

    w_gate, tok, everyone = lax.optimization_barrier((w_gate, tok, everyone))
    proj_g = project(tok, w_gate)
    gate = (proj_g[:rows] + swap_cores(proj_g[rows:])).astype(BF16).reshape(rows, heads, width)

    diagonal = jnp.einsum("hij,jhp->ihp", weights, values, preferred_element_type=F32)
    in_hi = incoming.astype(BF16)
    in_lo = (incoming - in_hi.astype(F32)).astype(BF16)
    offdiag = jnp.einsum("ni,hnp->ihp", c_t, in_hi, preferred_element_type=F32)
    offdiag = offdiag + jnp.einsum("ni,hnp->ihp", c_t, in_lo, preferred_element_type=F32)
    output = diagonal + offdiag * carry_in.T[:, :, None] + skip[None, :, None] * value_f
    gated = output * jax.nn.silu(gate.astype(F32))
    squares = jnp.sum(gated * gated, axis=(1, 2))
    squares = jnp.sum(to_all(squares, "fsdp"), axis=0)
    scale = lax.rsqrt(squares / (heads * width * n_fsdp) + 1e-05)
    return (gated * scale[:, None, None] * gain[None]).astype(BF16)


def solution(mesh):
    in_specs = (
        P("ctx", "fsdp"),
        P("ctx", "fsdp", None),
        P("ctx", None),
        P("fsdp", None),
        P("fsdp"),
        P("fsdp", "ctx"),
        P("ctx"),
    )
    out_specs = P("ctx", "fsdp", None)
    return jax.shard_map(
        per_device, mesh=mesh, in_specs=in_specs, out_specs=out_specs, check_vma=False
    )
```

time: 166 us -> 179 us (1.078)
  starting transfers between devices: 33.9 us -> 58.6 us
  waiting for transfers between devices: 28.1 us -> 12.8 us
  other arithmetic: 3.84 us -> 6.48 us
  matrix products: 4.51 us -> 1.96 us
  Pallas kernels: 0 us -> 2.04 us
    all_gather x1, waiting for transfers between devices: 20.2 us -> 0.02 us  [per_device(): w_gate = lax.all_gather(w_gate, 'ctx', axis=0, axis_index_groups=same_core)]
    all_to_all x2 -> x3, starting transfers between devices: 14.6 us -> 29.5 us  [to_all(): return lax.all_to_all(copies, axis, 0, 0, axis_index_groups=groups)]
    ppermute x3 -> x6, starting transfers between devices: 19.2 us -> 29 us  [swap_cores(): lax.ppermute(x, 'ctx', [(i, i ^ 1) for i in range(lax.axis_size('ctx'))])]
    all_to_all x2 -> x3, waiting for transfers between devices: 6.69 us -> 11.7 us  [to_all(): return lax.all_to_all(copies, axis, 0, 0, axis_index_groups=groups)]
    dot_general x5 -> x1, matrix products: 3.76 us -> 0.15 us  [per_device(): local = jnp.einsum('nj,jhp->hnp', b_t, scaled, preferred_element_type=F32)]
    all_to_all x1, blocking collectives: 12.7 us -> 9.56 us  [to_all(): return lax.all_to_all(copies, axis, 0, 0, axis_index_groups=groups)]
    slice x4 -> x12, local copies, waits for them, and re-layouts: 1.19 us -> 3.66 us  [the longest x1 0.89 us: per_device(): w_gate = w_xz[:, :, width:].reshape(depth, -1)]
    all_gather x1, blocking collectives: 30.6 us -> 32.7 us  [per_device(): lax.all_gather(w_val[:depth - n_rest], 'ctx', axis=0, axis_index_groups=s...]
  transfers between devices with their start and end apart: 6 -> 10, of which waited for: 4 -> 4; matrix products, arithmetic and copies ran while one was open for 4% -> 9% of each run, Pallas kernels for 0% -> 1%
where the time goes in v2:
time: 179 us; the launch traced here: 178 us
  blocking collectives  66.6 us (37%)
  starting transfers between devices  58.6 us (33%)
  between operations  15.9 us (9%)
  local copies, waits for them, and re-layouts  13.5 us (8%)
  waiting for transfers between devices  12.8 us (7%)
  other arithmetic  6.48 us (4%)
  Pallas kernels  2.04 us (1%)
  matrix products  1.96 us (1%)
    all_gather x1, blocking collectives, per_device(): lax.all_gather(w_val[:depth - n_rest], 'ctx', axis=0, axis_index_groups=s...  32.7 us
    all_to_all x3, starting transfers between devices, to_all(): return lax.all_to_all(copies, axis, 0, 0, axis_index_groups=groups)  29.5 us
    ppermute x6, starting transfers between devices, swap_cores(): lax.ppermute(x, 'ctx', [(i, i ^ 1) for i in range(lax.axis_size('ctx'))])  29 us
    all_gather x1, blocking collectives, per_device(): lax.all_gather(packed, 'ctx', axis=0, axis_index_groups=same_core)  24.3 us
    all_to_all x3, waiting for transfers between devices, to_all(): return lax.all_to_all(copies, axis, 0, 0, axis_index_groups=groups)  11.7 us
    all_to_all x1, blocking collectives, to_all(): return lax.all_to_all(copies, axis, 0, 0, axis_index_groups=groups)  9.56 us
  transfers between devices with their start and end apart: 10, of which 4 were waited for; matrix products, arithmetic and copies ran while one was open for 9% of the time, Pallas kernels for 1%

profile of v2, /device:TPU:1, one launch (start us, length us, event | category | flops | bytes accessed | tf_op | source)
XLA Modules:
  0.0 177.8 jit_solution(7610605308076542243)
XLA Ops:
  6.5 0.8 copy-done
  9.0 15.7 %all-to-all-start.1 = ((bf16[16,48,128]{2,1,0:T(8,128)(2,1)}), bf16[16,48,128]{2,1,0:T(8,128)(2,1)S(1)}, u32[]{:S(2)}, u32[]{:S(2)}) async-start(bf16[16,48,128]{2,1,0:T(8,128)(2,1)} %broadcast_in_dim.63), calls=%async_computation.1 | async-start | bytes 393216 | tf_op jit(solution)/shard_map/all_to_all | solution.py:22
  24.8 0.9 broadcast_select_fusion.1
  25.7 2.9 %collective-permute-start = (bf16[256,128]{1,0:T(8,128)(2,1)S(1)}, bf16[256,128]{1,0:T(8,128)(2,1)S(1)}, u32[]{:S(2)}, u32[]{:S(2)}) collective-permute-start(bf16[256,128]{1,0:T(8,128)(2,1)S(1)} %get-tuple-element.23), channel_id=1, source_target_pairs={{0,16},{16,0},{32,48},{48,32},{64,80},{80,64},{96,112},{112,96},{1... | collective-permute-start | bytes 196616 | tf_op jit(solution)/shard_map/ppermute | solution.py:16
  28.6 0.9 slice.140
  30.1 0.9 slice.111
  31.1 1.0 reduce-window.9
  32.2 5.1 %all-to-all-done.1 = bf16[16,48,128]{2,1,0:T(8,128)(2,1)S(1)} async-done(((bf16[16,48,128]{2,1,0:T(8,128)(2,1)}), bf16[16,48,128]{2,1,0:T(8,128)(2,1)S(1)}, u32[]{:S(2)}, u32[]{:S(2)}) %all-to-all-start.1) | async-done | bytes 196640 | tf_op jit(solution)/shard_map/all_to_all | solution.py:22
  37.3 1.7 broadcast_in_dim.61
  39.0 6.9 %all-to-all-start = ((bf16[16,512,128]{2,1,0:T(8,128)(2,1)}), bf16[16,512,128]{2,1,0:T(8,128)(2,1)S(1)}, u32[]{:S(2)}, u32[]{:S(2)}) async-start(bf16[16,512,128]{2,1,0:T(8,128)(2,1)} %broadcast_in_dim.61), calls=%async_computation | async-start | bytes 4194304 | tf_op jit(solution)/shard_map/all_to_all | solution.py:22
  48.7 32.7 %all_gather.16.refs_0_ = bf16[16,112,256]{2,1,0:T(8,128)(2,1)S(1)} all-gather(bf16[1,112,256]{2,1,0:T(8,128)(2,1)S(1)} %all_gather.15), channel_id=1, replica_groups={{0,32,64,96,128,160,192,224,256,288,320,352,384,416,448,480},{16,48,80,..., dimensions={0}, use_global_device_ids=true | all-gather | bytes 974848 | tf_op jit(solution)/shard_map/all_gather | solution.py:85
  82.1 9.3 %collective-permute-start.2 = (f32[16,256]{1,0:T(8,128)S(1)}, f32[16,256]{1,0:T(8,128)S(1)}, u32[]{:S(2)}, u32[]{:S(2)}) collective-permute-start(f32[16,256]{1,0:T(8,128)S(1)} %slice.151), channel_id=1, source_target_pairs={{0,16},{16,0},{32,48},{48,32},{64,80},{80,64},{96,112},{112,96},{1... | collective-permute-start | bytes 49160 | tf_op jit(solution)/shard_map/ppermute | solution.py:16
  92.9 1.9 %collective-permute-start.1 = (f32[256,256]{1,0:T(8,128)S(1)}, f32[256,256]{1,0:T(8,128)S(1)}, u32[]{:S(2)}, u32[]{:S(2)}) collective-permute-start(f32[256,256]{1,0:T(8,128)S(1)} %slice.148), channel_id=1, source_target_pairs={{0,16},{16,0},{32,48},{48,32},{64,80},{80,64},{96,112},{112,96},{1... | collective-permute-start | bytes 786440 | tf_op jit(solution)/shard_map/ppermute | solution.py:16
  95.5 6.9 %all-to-all-start.2 = ((bf16[16,16,256]{2,1,0:T(8,128)(2,1)}), bf16[16,16,256]{2,1,0:T(8,128)(2,1)S(1)}, u32[]{:S(2)}, u32[]{:S(2)}) async-start(bf16[16,16,256]{2,1,0:T(8,128)(2,1)} %broadcast_in_dim.66), calls=%async_computation.2 | async-start | bytes 262144 | tf_op jit(solution)/shard_map/all_to_all | solution.py:22
  102.6 6.6 %all-to-all-done.2 = bf16[16,16,256]{2,1,0:T(8,128)(2,1)S(1)} async-done(((bf16[16,16,256]{2,1,0:T(8,128)(2,1)}), bf16[16,16,256]{2,1,0:T(8,128)(2,1)S(1)}, u32[]{:S(2)}, u32[]{:S(2)}) %all-to-all-start.2) | async-done | bytes 131104 | tf_op jit(solution)/shard_map/all_to_all | solution.py:22
  109.6 1.0 fusion.13
  110.9 3.7 %collective-permute-start.3 = (f32[136,128]{1,0:T(8,128)S(1)}, f32[136,128]{1,0:T(8,128)S(1)}, u32[]{:S(2)}, u32[]{:S(2)}) collective-permute-start(f32[136,128]{1,0:T(8,128)S(1)} %select_bitcast_fusion), channel_id=1, source_target_pairs={{0,16},{16,0},{32,48},{48,32},{64,80},{80,64},{96,112},{112,96},{1... | collective-permute-start | bytes 208904 | tf_op jit(solution)/shard_map/ppermute | solution.py:16
  114.6 0.9 collective-permute-done.3
  118.7 24.3 %all-gather = bf16[2304,128]{1,0:T(8,128)(2,1)S(1)} all-gather(bf16[144,128]{1,0:T(8,128)(2,1)S(1)} %pad_maximum_fusion.4), channel_id=2, replica_groups={{0,32,64,96,128,160,192,224,256,288,320,352,384,416,448,480},{16,48,80,..., dimensions={0}, use_global_device_ids=true | all-gather | bytes 626688 | tf_op jit(solution)/shard_map/all_gather | solution.py:135
  144.1 9.2 %collective-permute-start.4 = (f32[128,128]{1,0:T(8,128)S(1)}, f32[128,128]{1,0:T(8,128)S(1)}, u32[]{:S(2)}, u32[]{:S(2)}) collective-permute-start(f32[128,128]{1,0:T(8,128)S(1)} %fusion.19), channel_id=1, source_target_pairs={{0,16},{16,0},{32,48},{48,32},{64,80},{80,64},{96,112},{112,96},{1... | collective-permute-start | bytes 196616 | tf_op jit(solution)/shard_map/ppermute | solution.py:16
  153.3 0.9 convolution_bitcast_fusion.1
  154.3 1.2 copy-done.2
  156.3 2.1 %collective-permute-start.5 = (f32[256,256]{1,0:T(8,128)S(1)}, f32[256,256]{1,0:T(8,128)S(1)}, u32[]{:S(2)}, u32[]{:S(2)}) collective-permute-start(f32[256,256]{1,0:T(8,128)S(1)} %slice.164), channel_id=1, source_target_pairs={{0,16},{16,0},{32,48},{48,32},{64,80},{80,64},{96,112},{112,96},{1... | collective-permute-start | bytes 786440 | tf_op jit(solution)/shard_map/ppermute | solution.py:16
  160.5 9.6 %all_to_all.21 = f32[16,1,256]{2,1,0:T(1,128)S(1)} all-to-all(f32[16,1,256]{2,1,0:T(1,128)S(1)} %broadcast_in_dim.120), channel_id=1, replica_groups=mesh['ctx'=32,'fsdp'=16] {'fsdp'}, dimensions={0} | all-to-all | bytes 32768 | tf_op jit(solution)/shard_map/all_to_all | solution.py:22
  (92 shorter events, 14.9 us)
Async XLA Ops:
  6.5 0.8 copy-start
  9.0 28.3 %all-to-all-start.1 = ((bf16[16,48,128]{2,1,0:T(8,128)(2,1)}), bf16[16,48,128]{2,1,0:T(8,128)(2,1)S(1)}, u32[]{:S(2)}, u32[]{:S(2)}) async-start(bf16[16,48,128]{2,1,0:T(8,128)(2,1)} %broadcast_in_dim.63), calls=%async_computation.1 | async-start | bytes 393216 | tf_op jit(solution)/shard_map/all_to_all | solution.py:22
  24.7 129.6 %all-gather.3.cloned.1.call-start = ((), (), s32[]{:S(2)}) async-start(), calls=%async_computation.4 | async-start | bytes 1114112 | tf_op jit(solution)/shard_map/all_gather | solution.py:68
  25.7 6.5 %collective-permute-start = (bf16[256,128]{1,0:T(8,128)(2,1)S(1)}, bf16[256,128]{1,0:T(8,128)(2,1)S(1)}, u32[]{:S(2)}, u32[]{:S(2)}) collective-permute-start(bf16[256,128]{1,0:T(8,128)(2,1)S(1)} %get-tuple-element.23), channel_id=1, source_target_pairs={{0,16},{16,0},{32,48},{48,32},{64,80},{80,64},{96,112},{112,96},{1... | collective-permute-start | bytes 196616 | tf_op jit(solution)/shard_map/ppermute | solution.py:16
  39.0 8.3 %copy-start.4 = (f32[2,256]{1,0:T(2,128)S(1)}, f32[2,256]{1,0:T(2,128)}, u32[]{:S(2)}) copy-start(f32[2,256]{1,0:T(2,128)} %param.12) | copy-start | bytes 6148
  39.0 42.4 %all-to-all-start = ((bf16[16,512,128]{2,1,0:T(8,128)(2,1)}), bf16[16,512,128]{2,1,0:T(8,128)(2,1)S(1)}, u32[]{:S(2)}, u32[]{:S(2)}) async-start(bf16[16,512,128]{2,1,0:T(8,128)(2,1)} %broadcast_in_dim.61), calls=%async_computation | async-start | bytes 4194304 | tf_op jit(solution)/shard_map/all_to_all | solution.py:22
  82.1 12.8 %collective-permute-start.2 = (f32[16,256]{1,0:T(8,128)S(1)}, f32[16,256]{1,0:T(8,128)S(1)}, u32[]{:S(2)}, u32[]{:S(2)}) collective-permute-start(f32[16,256]{1,0:T(8,128)S(1)} %slice.151), channel_id=1, source_target_pairs={{0,16},{16,0},{32,48},{48,32},{64,80},{80,64},{96,112},{112,96},{1... | collective-permute-start | bytes 49160 | tf_op jit(solution)/shard_map/ppermute | solution.py:16
  92.1 0.8 copy-start.1
  92.9 16.3 %collective-permute-start.1 = (f32[256,256]{1,0:T(8,128)S(1)}, f32[256,256]{1,0:T(8,128)S(1)}, u32[]{:S(2)}, u32[]{:S(2)}) collective-permute-start(f32[256,256]{1,0:T(8,128)S(1)} %slice.148), channel_id=1, source_target_pairs={{0,16},{16,0},{32,48},{48,32},{64,80},{80,64},{96,112},{112,96},{1... | collective-permute-start | bytes 786440 | tf_op jit(solution)/shard_map/ppermute | solution.py:16
  95.5 13.7 %all-to-all-start.2 = ((bf16[16,16,256]{2,1,0:T(8,128)(2,1)}), bf16[16,16,256]{2,1,0:T(8,128)(2,1)S(1)}, u32[]{:S(2)}, u32[]{:S(2)}) async-start(bf16[16,16,256]{2,1,0:T(8,128)(2,1)} %broadcast_in_dim.66), calls=%async_computation.2 | async-start | bytes 262144 | tf_op jit(solution)/shard_map/all_to_all | solution.py:22
  110.9 4.6 %collective-permute-start.3 = (f32[136,128]{1,0:T(8,128)S(1)}, f32[136,128]{1,0:T(8,128)S(1)}, u32[]{:S(2)}, u32[]{:S(2)}) collective-permute-start(f32[136,128]{1,0:T(8,128)S(1)} %select_bitcast_fusion), channel_id=1, source_target_pairs={{0,16},{16,0},{32,48},{48,32},{64,80},{80,64},{96,112},{112,96},{1... | collective-permute-start | bytes 208904 | tf_op jit(solution)/shard_map/ppermute | solution.py:16
  144.1 14.3 %collective-permute-start.4 = (f32[128,128]{1,0:T(8,128)S(1)}, f32[128,128]{1,0:T(8,128)S(1)}, u32[]{:S(2)}, u32[]{:S(2)}) collective-permute-start(f32[128,128]{1,0:T(8,128)S(1)} %fusion.19), channel_id=1, source_target_pairs={{0,16},{16,0},{32,48},{48,32},{64,80},{80,64},{96,112},{112,96},{1... | collective-permute-start | bytes 196616 | tf_op jit(solution)/shard_map/ppermute | solution.py:16
  154.3 1.2 copy-start.2
  156.3 3.8 %copy-start.5 = (f32[2]{0:T(128)S(1)}, f32[2]{0:T(128)}, u32[]{:S(2)}) copy-start(f32[2]{0:T(128)} %param.11) | copy-start | bytes 28
  156.3 3.8 %copy-start.6 = (f32[256,256]{1,0:T(8,128)S(1)}, f32[256,256]{1,0:T(8,128)}, u32[]{:S(2)}) copy-start(f32[256,256]{1,0:T(8,128)} %convolution_bitcast_fusion.1) | copy-start | bytes 786436
  156.3 3.6 %collective-permute-start.5 = (f32[256,256]{1,0:T(8,128)S(1)}, f32[256,256]{1,0:T(8,128)S(1)}, u32[]{:S(2)}, u32[]{:S(2)}) collective-permute-start(f32[256,256]{1,0:T(8,128)S(1)} %slice.164), channel_id=1, source_target_pairs={{0,16},{16,0},{32,48},{48,32},{64,80},{80,64},{96,112},{112,96},{1... | collective-permute-start | bytes 786440 | tf_op jit(solution)/shard_map/ppermute | solution.py:16
  159.5 10.6 %copy-start.3 = (f32[2,128]{1,0:T(2,128)S(1)}, f32[2,128]{1,0:T(2,128)}, u32[]{:S(2)}) copy-start(f32[2,128]{1,0:T(2,128)} %param.10) | copy-start | bytes 3076
Sparse Core Ops, SparseCore 0:
  30.3 63.5 all-gather.2

commit v3 on v1

v3 whole, which is shorter than its diff:
```python
import functools

import jax
import jax.numpy as jnp
from jax import lax
from jax.experimental import pallas as pl
from jax.experimental.pallas import tpu as pltpu
from jax.sharding import PartitionSpec as P

F32 = jnp.float32
BF16 = jnp.bfloat16
HIGH = lax.Precision.HIGHEST
PARAMS = pltpu.CompilerParams(vmem_limit_bytes=20 * 1024 * 1024)
NT = (((1,), (1,)), ((), ()))
TN = (((0,), (0,)), ((), ()))
VMEM = pl.BlockSpec(memory_space=pltpu.VMEM)
SMEM = pl.BlockSpec(memory_space=pltpu.SMEM)


def call(kernel, outs, *args, smem=0):
    shapes = [jax.ShapeDtypeStruct(s, t) for s, t in outs]
    got = pl.pallas_call(
        kernel,
        out_shape=shapes,
        in_specs=[SMEM] * smem + [VMEM] * (len(args) - smem),
        out_specs=[VMEM] * len(shapes),
        compiler_params=PARAMS,
    )(*args)
    return got[0] if len(shapes) == 1 else got


def silu(x):
    return x / (1.0 + jnp.exp(-x))


def shift(x, by):
    n = lax.axis_size("ctx")
    return lax.ppermute(x, "ctx", [(i, (i + by) % n) for i in range(n)])


def swap_cores(x):
    return lax.ppermute(x, "ctx", [(i, i ^ 1) for i in range(lax.axis_size("ctx"))])


def decay_kernel(decays_ref, starts_ref, cols_ref, decay_ref, ends_ref):
    heads, rows = decays_ref.shape
    i = lax.broadcasted_iota(jnp.int32, (rows, rows), 0)
    j = lax.broadcasted_iota(jnp.int32, (rows, rows), 1)
    causal = i >= j
    ones = causal.astype(F32)
    logs = jnp.log(decays_ref[...])
    starts = starts_ref[...].astype(F32)
    both = jnp.concatenate([logs, starts, jnp.zeros((8 - heads - 1, rows), F32)], axis=0)
    cum_row = lax.dot_general(both, ones, NT, precision=HIGH, preferred_element_type=F32)
    cum_col = lax.dot_general(ones, both, NT, precision=HIGH, preferred_element_type=F32)
    seg_row, seg_col = cum_row[heads : heads + 1], cum_col[:, heads : heads + 1]
    same = causal & (jnp.abs(seg_row - seg_col) < 0.5)
    last = cum_row[:, rows - 1 :]
    seg_last = last[heads : heads + 1]
    to_end, carry = [], []
    for h in range(heads):
        col = cum_col[:, h : h + 1]
        diff = col - cum_row[h : h + 1]
        decay_ref[h] = jnp.where(same, jnp.exp(diff), 0.0)
        total = last[h : h + 1]
        to_end.append(jnp.where(jnp.abs(seg_col - seg_last) < 0.5, jnp.exp(total - col), 0.0))
        carry.append(jnp.where(seg_col < 0.5, jnp.exp(col), 0.0))
        keep = jnp.where(seg_last < 0.5, jnp.exp(total), 0.0)
        ends_ref[h] = jnp.broadcast_to(keep, ends_ref.shape[1:])
    cols_ref[...] = jnp.concatenate(to_end + carry, axis=1)


def partial_kernel(steps, with_acc, chip_ref, tok_ref, *refs):
    n_out = 3
    blocks, outs = refs[: len(steps)], refs[-n_out:]
    n_chip, rows = tok_ref.shape[0], tok_ref.shape[1]
    half = rows // 2
    chip = chip_ref[0]
    edges = [0, outs[0].shape[1], outs[0].shape[1] + outs[2].shape[1]]
    if with_acc:
        acc = refs[len(steps)][...]
    else:
        acc = jnp.zeros((rows, edges[-1]), F32)
    order = list(zip(steps, blocks))
    for at in range(0, len(order), 2):
        part = order[at : at + 2]
        toks = [tok_ref[lax.rem(chip - s + 2 * n_chip, n_chip)] for s, _ in part]
        ws = [w[...] for _, w in part]
        tok = jnp.concatenate(toks, axis=1) if len(part) > 1 else toks[0]
        w = jnp.concatenate(ws, axis=0) if len(part) > 1 else ws[0]
        acc += jnp.dot(tok, w, preferred_element_type=F32)
    outs[0][...] = acc[:half, : edges[1]]
    outs[1][...] = acc[half:, : edges[1]]
    outs[2][...] = acc[:, edges[1] :]


def first_kernel(steps, chip_ref, tok_ref, *refs):
    blocks, out_ref = refs[: len(steps)], refs[-1]
    n_chip = tok_ref.shape[0]
    chip = chip_ref[0]
    acc = jnp.zeros(out_ref.shape, F32)
    order = list(zip(steps, blocks))
    for at in range(0, len(order), 2):
        part = order[at : at + 2]
        toks = [tok_ref[lax.rem(chip - s + 2 * n_chip, n_chip)] for s, _ in part]
        ws = [w[...] for _, w in part]
        tok = jnp.concatenate(toks, axis=1) if len(part) > 1 else toks[0]
        w = jnp.concatenate(ws, axis=0) if len(part) > 1 else ws[0]
        acc += jnp.dot(tok, w, preferred_element_type=F32)
    out_ref[...] = acc


def local_kernel(own_ref, got_ref, cols_ref, val_ref, maps_ref, local_ref):
    heads, n_state, width = local_ref.shape
    both = own_ref[...] + got_ref[...]
    act = silu(both).astype(BF16)
    values = act[:, : heads * width]
    maps = act[:, heads * width :]
    val_ref[...] = values
    maps_ref[...] = maps
    for h in range(heads):
        v = values[:, h * width : (h + 1) * width].astype(F32)
        scaled = (cols_ref[:, h : h + 1] * v).astype(BF16)
        local_ref[h] = lax.dot_general(maps[:, :n_state], scaled, TN, preferred_element_type=F32)


def diag_kernel(skip_ref, maps_ref, val_ref, decay_ref, out_ref):
    heads = decay_ref.shape[0]
    n_state = maps_ref.shape[1] // 2
    width = val_ref.shape[1] // heads
    scores = lax.dot_general(
        maps_ref[:, n_state:], maps_ref[:, :n_state], NT, preferred_element_type=F32
    )
    for h in range(heads):
        at = slice(h * width, (h + 1) * width)
        v = val_ref[:, at]
        weights = (decay_ref[h] * scores).astype(BF16)
        out = jnp.dot(weights, v, preferred_element_type=F32)
        out_ref[:, at] = out + skip_ref[h] * v.astype(F32)


def gated_kernel(heads, core_ref, diag_ref, kept_ref, came_ref, maps_ref, cols_ref, gate_ref, got_ref, out_ref, sum_ref):
    rows = diag_ref.shape[0]
    width = diag_ref.shape[1] // heads
    n_state = maps_ref.shape[1] // 2
    core = core_ref[0]
    c_map = maps_ref[:, n_state:]
    kept, came = kept_ref[...], came_ref[...]
    gate = (gate_ref[...] + got_ref[...]).astype(BF16).astype(F32)
    gate = silu(gate)
    total = jnp.zeros((rows, width), F32)
    for h in range(heads):
        at = slice(h * width, (h + 1) * width)
        state = jnp.where(core == h, kept, came)
        hi = state.astype(BF16)
        lo = (state - hi.astype(F32)).astype(BF16)
        off = jnp.dot(c_map, hi, preferred_element_type=F32)
        off += jnp.dot(c_map, lo, preferred_element_type=F32)
        out = diag_ref[:, at] + off * cols_ref[:, heads + h : heads + h + 1]
        gated = out * gate[:, at]
        out_ref[:, at] = gated
        total += gated * gated
    ones = jnp.ones((sum_ref.shape[0], width), F32)
    sum_ref[...] = lax.dot_general(ones, total, NT, precision=HIGH, preferred_element_type=F32)


def norm_kernel(count, sum_ref, gated_ref, gain_ref, out_ref):
    ones = jnp.ones((sum_ref.shape[0], gated_ref.shape[1]), F32)
    mean = lax.dot_general(sum_ref[...], ones, TN, precision=HIGH, preferred_element_type=F32)
    scale = lax.rsqrt(mean / count + 1e-05)
    out_ref[...] = (gated_ref[...] * scale * gain_ref[...]).astype(BF16)


def per_device(tokens, w_xz, w_bc, gain, skip, decays, boundaries):
    rows = tokens.shape[0]
    depth, heads = w_xz.shape[:2]
    width = w_xz.shape[2] // 2
    n_state = w_bc.shape[1] // 2
    n_ctx, n_fsdp = lax.axis_size("ctx"), lax.axis_size("fsdp")
    n_chip = n_ctx // 2
    ctx = lax.axis_index("ctx")
    core, chip = ctx % 2, ctx // 2
    same_core = [[2 * z + c for z in range(n_chip)] for c in range(2)]
    core_1, chip_1 = core.reshape(1), chip.reshape(1)

    def mine_other(a, b):
        return jnp.where(core == 0, a, b), jnp.where(core == 0, b, a)

    tok_mine, tok_other = mine_other(tokens[:, :depth], tokens[:, depth:])
    tok = jnp.concatenate([tok_mine, swap_cores(tok_other)], axis=0)
    copies = jnp.broadcast_to(tok[None], (n_fsdp,) + tok.shape)
    tok = lax.all_to_all(copies, "fsdp", 0, 0)

    block = jnp.concatenate(
        [w_xz[:, :, :width].reshape(depth, -1), w_bc, w_xz[:, :, width:].reshape(depth, -1)], axis=1
    )
    up = down = block
    steps, blocks = [0], [block]
    for s in range(1, n_chip // 2 + 1):
        up = shift(up, 2)
        steps.append(s)
        blocks.append(up)
        if s < n_chip // 2:
            down = shift(down, -2)
            steps.append(-s)
            blocks.append(down)
    early = n_chip - 4

    cols, decay, ends = call(
        decay_kernel,
        [((rows, 2 * heads), F32), ((heads, rows, rows), F32), ((heads, 8, width), F32)],
        decays,
        boundaries.reshape(1, rows),
    )

    n_first = heads * width + 2 * n_state
    acc = call(
        functools.partial(first_kernel, steps[:early]),
        [((2 * rows, block.shape[1]), F32)],
        chip_1,
        tok,
        *blocks[:early],
        smem=1,
    )
    own, other, gates = call(
        functools.partial(partial_kernel, steps[early:], True),
        [((rows, n_first), F32), ((rows, n_first), F32), ((2 * rows, heads * width), F32)],
        chip_1,
        tok,
        *blocks[early:],
        acc,
        smem=1,
    )
    got = swap_cores(other)
    gate_got = swap_cores(gates[rows:])
    values, maps, local = call(
        local_kernel,
        [((rows, heads * width), BF16), ((rows, 2 * n_state), BF16), ((heads, n_state, width), F32)],
        own,
        got,
        cols,
    )

    mine = jnp.concatenate([local, ends], axis=1)
    keep, send = mine_other(mine[0], mine[1])
    first, second = mine_other(keep, swap_cores(send))
    diag = call(diag_kernel, [((rows, heads * width), F32)], skip, maps, values, decay, smem=1)
    s0, g0, s1, g1 = first[:n_state], first[n_state, 0], second[:n_state], second[n_state, 0]
    s_chip, g_chip = g1 * s0 + s1, g0 * g1
    g_hi = g_chip.astype(BF16)
    g_mid = (g_chip - g_hi.astype(F32)).astype(BF16)
    g_lo = (g_chip - g_hi.astype(F32) - g_mid.astype(F32)).astype(BF16)
    g_row = jnp.stack([g_hi, g_mid, g_lo] + [jnp.zeros_like(g_hi)] * 13)
    packed = jnp.concatenate(
        [s_chip.astype(BF16), jnp.broadcast_to(g_row[:, None], (16, width))], axis=0
    )
    everyone = lax.all_gather(packed, "ctx", axis=0, axis_index_groups=same_core)
    g_all = everyone[:, n_state : n_state + 3, 0].astype(F32)
    g_all = g_all[:, 0] + g_all[:, 1] + g_all[:, 2]
    at = jnp.arange(n_chip)
    between = (at[None, :] > at[:, None]) & (at[None, :] < chip)
    coef = jnp.prod(jnp.where(between, g_all[None, :], 1.0), axis=1)
    coef = jnp.where(at < chip, coef, 0.0)
    e0 = jnp.sum(coef[:, None, None] * everyone[:, :n_state].astype(F32), axis=0)
    e1 = g0 * e0 + s0
    kept, give = mine_other(e0, e1)
    came = swap_cores(give)

    gated, sums = call(
        functools.partial(gated_kernel, heads),
        [((rows, heads * width), F32), ((n_fsdp, rows), F32)],
        core_1,
        diag,
        kept,
        came,
        maps,
        cols,
        gates[:rows],
        gate_got,
        smem=1,
    )
    sums = lax.all_to_all(sums, "fsdp", 0, 0, tiled=True)
    out = call(
        functools.partial(norm_kernel, heads * width * n_fsdp),
        [((rows, heads * width), BF16)],
        sums,
        gated,
        gain.reshape(1, -1),
    )
    return out.reshape(rows, heads, width)


def solution(mesh):
    in_specs = (
        P("ctx", "fsdp"),
        P("ctx", "fsdp", None),
        P("ctx", None),
        P("fsdp", None),
        P("fsdp"),
        P("fsdp", "ctx"),
        P("ctx"),
    )
    out_specs = P("ctx", "fsdp", None)
    return jax.shard_map(
        per_device, mesh=mesh, in_specs=in_specs, out_specs=out_specs, check_vma=False
    )
```

time: 166 us -> 159 us (0.958)
  starting transfers between devices: 33.9 us -> 88 us
  blocking collectives: 67.8 us -> 37.5 us
  waiting for transfers between devices: 28.1 us -> 8.33 us
  between operations: 15.7 us -> 1.84 us
  Pallas kernels: 0 us -> 6.38 us
  matrix products: 4.51 us -> 0 us
    ppermute x3 -> x20, starting transfers between devices: 19.2 us -> 84.2 us  [the longest x15 51.8 us: shift(): return lax.ppermute(x, 'ctx', [(i, (i + by) % n) for i in range(n)])]
    all_gather x1 -> x0, blocking collectives: 30.6 us -> none  [per_device(): part = lax.all_gather(part, 'ctx', axis=0, axis_index_groups=same_core)]
    all_gather x1 -> x0, waiting for transfers between devices: 20.2 us -> none  [per_device(): lax.all_gather(w_xz.reshape(w_xz.shape[0], -1), 'ctx', axis=0, tiled=True)]
    all_to_all x2 -> x1, starting transfers between devices: 14.6 us -> 3.85 us  [per_device(): tok = lax.all_to_all(copies, 'fsdp', 0, 0)]
    ppermute x3 -> x20, waiting for transfers between devices: 1.26 us -> 8.33 us  [the longest x15 7.93 us: shift(): return lax.ppermute(x, 'ctx', [(i, (i + by) % n) for i in range(n)])]
    all_to_all x2 -> x1, waiting for transfers between devices: 6.69 us -> 0.01 us  [per_device(): tok = lax.all_to_all(copies, 'fsdp', 0, 0)]
    pallas_call x0 -> x7, Pallas kernels: none -> 6.38 us  [call(): pl.pallas_call(kernel, out_shape=shapes, in_specs=[SMEM] * smem + [VMEM]...]
    dot_general x8 -> x0, matrix products: 4.51 us -> none  [the longest x1 2.45 us: per_device(): jnp.einsum('fik,fkn->in', tok, w_all.reshape(n_fsdp, -1, w_all.shape[1]),...]
  transfers between devices with their start and end apart: 6 -> 21, of which waited for: 4 -> 7; matrix products, arithmetic and copies ran while one was open for 4% -> 3% of each run, Pallas kernels for 0% -> 2%
where the time goes in v3:
time: 159 us; the launch traced here: 158 us
  starting transfers between devices  88 us (55%)
  blocking collectives  37.5 us (24%)
  local copies, waits for them, and re-layouts  12.9 us (8%)
  waiting for transfers between devices  8.33 us (5%)
  Pallas kernels  6.38 us (4%)
  other arithmetic  2.6 us (2%)
  between operations  1.84 us (1%)
    ppermute x15, starting transfers between devices, shift(): return lax.ppermute(x, 'ctx', [(i, (i + by) % n) for i in range(n)])  51.8 us
    ppermute x5, starting transfers between devices, swap_cores(): lax.ppermute(x, 'ctx', [(i, i ^ 1) for i in range(lax.axis_size('ctx'))])  32.4 us
    all_gather x1, blocking collectives, per_device(): lax.all_gather(packed, 'ctx', axis=0, axis_index_groups=same_core)  24.4 us
    all_to_all x1, blocking collectives, per_device(): sums = lax.all_to_all(sums, 'fsdp', 0, 0, tiled=True)  13 us
    unnamed x35, local copies, waits for them, and re-layouts  8.15 us
    ppermute x15, waiting for transfers between devices, shift(): return lax.ppermute(x, 'ctx', [(i, (i + by) % n) for i in range(n)])  7.93 us
    pallas_call x7, Pallas kernels, call(): pl.pallas_call(kernel, out_shape=shapes, in_specs=[SMEM] * smem + [VMEM]...  6.38 us
    all_to_all x1, starting transfers between devices, per_device(): tok = lax.all_to_all(copies, 'fsdp', 0, 0)  3.85 us
  transfers between devices with their start and end apart: 21, of which 7 were waited for; matrix products, arithmetic and copies ran while one was open for 3% of the time, Pallas kernels for 2%

profile of v3, /device:TPU:1, one launch (start us, length us, event | category | flops | bytes accessed | tf_op | source)
XLA Modules:
  0.0 157.6 jit_solution(1680094600792208882)
XLA Ops:
  0.9 8.8 %collective-permute-start = (bf16[256,128]{1,0:T(8,128)(2,1)S(1)}, bf16[256,128]{1,0:T(8,128)(2,1)S(1)}, u32[]{:S(2)}, u32[]{:S(2)}) collective-permute-start(bf16[256,128]{1,0:T(8,128)(2,1)S(1)} %get-tuple-element.36), channel_id=1, source_target_pairs={{0,16},{16,0},{32,48},{48,32},{64,80},{80,64},{96,112},{112,96},{1... | collective-permute-start | bytes 196616 | tf_op jit(solution)/shard_map/ppermute | solution.py:42
  12.4 3.8 %all-to-all-start = ((bf16[16,512,128]{2,1,0:T(8,128)(2,1)}), bf16[16,512,128]{2,1,0:T(8,128)(2,1)S(1)}, u32[]{:S(2)}, u32[]{:S(2)}) async-start(bf16[16,512,128]{2,1,0:T(8,128)(2,1)} %broadcast_in_dim.15), calls=%async_computation | async-start | bytes 4194304 | tf_op jit(solution)/shard_map/all_to_all | solution.py:192
  16.4 1.9 %collective-permute-start.7 = (bf16[128,768]{1,0:T(8,128)(2,1)S(1)}, bf16[128,768]{1,0:T(8,128)(2,1)S(1)}, u32[]{:S(2)}, u32[]{:S(2)}) collective-permute-start(bf16[128,768]{1,0:T(8,128)(2,1)S(1)} %bitcast_dynamic-update-slice_fusion.refs_0_), channel_id=1, source_target_pairs={{0,32},{16,48},{32,64},{48,80},{64,96},{80,112},{96,128},{112,144}... | collective-permute-start | bytes 589832 | tf_op jit(solution)/shard_map/ppermute | solution.py:38
  18.3 8.8 %collective-permute-start.1 = (bf16[128,768]{1,0:T(8,128)(2,1)S(1)}, bf16[128,768]{1,0:T(8,128)(2,1)S(1)}, u32[]{:S(2)}, u32[]{:S(2)}) collective-permute-start(bf16[128,768]{1,0:T(8,128)(2,1)S(1)} %bitcast_dynamic-update-slice_fusion.refs_0_), channel_id=1, source_target_pairs={{0,480},{16,496},{32,0},{48,16},{64,32},{80,48},{96,64},{112,80},{... | collective-permute-start | bytes 589832 | tf_op jit(solution)/shard_map/ppermute | solution.py:38
  27.1 2.9 %collective-permute-done.7.refs_1_ = bf16[128,768]{1,0:T(8,128)(2,1)S(1)} collective-permute-done((bf16[128,768]{1,0:T(8,128)(2,1)S(1)}, bf16[128,768]{1,0:T(8,128)(2,1)S(1)}, u32[]{:S(2)}, u32[]{:S(2)}) %collective-permute-start.7) | collective-permute-done | bytes 196640 | tf_op jit(solution)/shard_map/ppermute | solution.py:38
  29.9 1.9 %collective-permute-start.8 = (bf16[128,768]{1,0:T(8,128)(2,1)S(1)}, bf16[128,768]{1,0:T(8,128)(2,1)S(1)}, u32[]{:S(2)}, u32[]{:S(2)}) collective-permute-start(bf16[128,768]{1,0:T(8,128)(2,1)S(1)} %collective-permute-done.7.refs_1_), channel_id=1, source_target_pairs={{0,32},{16,48},{32,64},{48,80},{64,96},{80,112},{96,128},{112,144}... | collective-permute-start | bytes 589832 | tf_op jit(solution)/shard_map/ppermute | solution.py:38
  31.9 4.6 %collective-permute-start.2 = (bf16[128,768]{1,0:T(8,128)(2,1)S(1)}, bf16[128,768]{1,0:T(8,128)(2,1)S(1)}, u32[]{:S(2)}, u32[]{:S(2)}) collective-permute-start(bf16[128,768]{1,0:T(8,128)(2,1)S(1)} %collective-permute-done.1.refs_2_), channel_id=1, source_target_pairs={{0,480},{16,496},{32,0},{48,16},{64,32},{80,48},{96,64},{112,80},{... | collective-permute-start | bytes 589832 | tf_op jit(solution)/shard_map/ppermute | solution.py:38
  36.5 1.9 %collective-permute-done.8.refs_3_ = bf16[128,768]{1,0:T(8,128)(2,1)S(1)} collective-permute-done((bf16[128,768]{1,0:T(8,128)(2,1)S(1)}, bf16[128,768]{1,0:T(8,128)(2,1)S(1)}, u32[]{:S(2)}, u32[]{:S(2)}) %collective-permute-start.8) | collective-permute-done | bytes 196640 | tf_op jit(solution)/shard_map/ppermute | solution.py:38
  38.4 1.9 %collective-permute-start.9 = (bf16[128,768]{1,0:T(8,128)(2,1)S(1)}, bf16[128,768]{1,0:T(8,128)(2,1)S(1)}, u32[]{:S(2)}, u32[]{:S(2)}) collective-permute-start(bf16[128,768]{1,0:T(8,128)(2,1)S(1)} %collective-permute-done.8.refs_3_), channel_id=1, source_target_pairs={{0,32},{16,48},{32,64},{48,80},{64,96},{80,112},{96,128},{112,144}... | collective-permute-start | bytes 589832 | tf_op jit(solution)/shard_map/ppermute | solution.py:38
  40.3 4.6 %collective-permute-start.3 = (bf16[128,768]{1,0:T(8,128)(2,1)S(1)}, bf16[128,768]{1,0:T(8,128)(2,1)S(1)}, u32[]{:S(2)}, u32[]{:S(2)}) collective-permute-start(bf16[128,768]{1,0:T(8,128)(2,1)S(1)} %collective-permute-done.2.refs_4_), channel_id=1, source_target_pairs={{0,480},{16,496},{32,0},{48,16},{64,32},{80,48},{96,64},{112,80},{... | collective-permute-start | bytes 589832 | tf_op jit(solution)/shard_map/ppermute | solution.py:38
  46.0 1.9 %collective-permute-start.10 = (bf16[128,768]{1,0:T(8,128)(2,1)S(1)}, bf16[128,768]{1,0:T(8,128)(2,1)S(1)}, u32[]{:S(2)}, u32[]{:S(2)}) collective-permute-start(bf16[128,768]{1,0:T(8,128)(2,1)S(1)} %collective-permute-done.9.refs_5_), channel_id=1, source_target_pairs={{0,32},{16,48},{32,64},{48,80},{64,96},{80,112},{96,128},{112,144}... | collective-permute-start | bytes 589832 | tf_op jit(solution)/shard_map/ppermute | solution.py:38
  47.9 4.9 %collective-permute-start.4 = (bf16[128,768]{1,0:T(8,128)(2,1)S(1)}, bf16[128,768]{1,0:T(8,128)(2,1)S(1)}, u32[]{:S(2)}, u32[]{:S(2)}) collective-permute-start(bf16[128,768]{1,0:T(8,128)(2,1)S(1)} %collective-permute-done.3.refs_6_), channel_id=1, source_target_pairs={{0,480},{16,496},{32,0},{48,16},{64,32},{80,48},{96,64},{112,80},{... | collective-permute-start | bytes 589832 | tf_op jit(solution)/shard_map/ppermute | solution.py:38
  56.2 4.6 %collective-permute-start.5 = (bf16[128,768]{1,0:T(8,128)(2,1)S(1)}, bf16[128,768]{1,0:T(8,128)(2,1)S(1)}, u32[]{:S(2)}, u32[]{:S(2)}) collective-permute-start(bf16[128,768]{1,0:T(8,128)(2,1)S(1)} %collective-permute-done.4.refs_8_), channel_id=1, source_target_pairs={{0,480},{16,496},{32,0},{48,16},{64,32},{80,48},{96,64},{112,80},{... | collective-permute-start | bytes 589832 | tf_op jit(solution)/shard_map/ppermute | solution.py:38
  61.4 1.9 %collective-permute-start.12 = (bf16[128,768]{1,0:T(8,128)(2,1)S(1)}, bf16[128,768]{1,0:T(8,128)(2,1)S(1)}, u32[]{:S(2)}, u32[]{:S(2)}) collective-permute-start(bf16[128,768]{1,0:T(8,128)(2,1)S(1)} %collective-permute-done.11.refs_9_), channel_id=1, source_target_pairs={{0,32},{16,48},{32,64},{48,80},{64,96},{80,112},{96,128},{112,144}... | collective-permute-start | bytes 589832 | tf_op jit(solution)/shard_map/ppermute | solution.py:38
  64.1 4.6 %collective-permute-start.6 = (bf16[128,768]{1,0:T(8,128)(2,1)S(1)}, bf16[128,768]{1,0:T(8,128)(2,1)}, u32[]{:S(2)}, u32[]{:S(2)}) collective-permute-start(bf16[128,768]{1,0:T(8,128)(2,1)S(1)} %collective-permute-done.5.refs_10_), channel_id=1, source_target_pairs={{0,480},{16,496},{32,0},{48,16},{64,32},{80,48},{96,64},{112,80},{... | collective-permute-start | bytes 589832 | tf_op jit(solution)/shard_map/ppermute | solution.py:38
  69.3 1.9 %collective-permute-start.13 = (bf16[128,768]{1,0:T(8,128)(2,1)S(1)}, bf16[128,768]{1,0:T(8,128)(2,1)}, u32[]{:S(2)}, u32[]{:S(2)}) collective-permute-start(bf16[128,768]{1,0:T(8,128)(2,1)S(1)} %collective-permute-done.12.refs_11_), channel_id=1, source_target_pairs={{0,32},{16,48},{32,64},{48,80},{64,96},{80,112},{96,128},{112,144}... | collective-permute-start | bytes 589832 | tf_op jit(solution)/shard_map/ppermute | solution.py:38
  71.9 4.6 %collective-permute-start.14 = (bf16[128,768]{1,0:T(8,128)(2,1)}, bf16[128,768]{1,0:T(8,128)(2,1)}, u32[]{:S(2)}, u32[]{:S(2)}) collective-permute-start(bf16[128,768]{1,0:T(8,128)(2,1)} %collective-permute-done.6.refs_0_), channel_id=1, source_target_pairs={{0,480},{16,496},{32,0},{48,16},{64,32},{80,48},{96,64},{112,80},{... | collective-permute-start | bytes 589832 | tf_op jit(solution)/shard_map/ppermute | solution.py:38
  77.0 1.9 %collective-permute-start.15 = (bf16[128,768]{1,0:T(8,128)(2,1)}, bf16[128,768]{1,0:T(8,128)(2,1)}, u32[]{:S(2)}, u32[]{:S(2)}) collective-permute-start(bf16[128,768]{1,0:T(8,128)(2,1)} %collective-permute-done.13.refs_1_), channel_id=1, source_target_pairs={{0,32},{16,48},{32,64},{48,80},{64,96},{80,112},{96,128},{112,144}... | collective-permute-start | bytes 589832 | tf_op jit(solution)/shard_map/ppermute | solution.py:38
  87.5 10.3 %collective-permute-start.16 = (f32[256,512]{1,0:T(8,128)S(1)}, f32[256,512]{1,0:T(8,128)S(1)}, u32[]{:S(2)}, u32[]{:S(2)}) collective-permute-start(f32[256,512]{1,0:T(8,128)S(1)} %get-tuple-element.17), channel_id=1, source_target_pairs={{0,16},{16,0},{32,48},{48,32},{64,80},{80,64},{96,112},{112,96},{1... | collective-permute-start | bytes 1572872 | tf_op jit(solution)/shard_map/ppermute | solution.py:42
  99.7 2.3 %collective-permute-start.17 = (f32[136,128]{1,0:T(8,128)S(1)}, f32[136,128]{1,0:T(8,128)S(1)}, u32[]{:S(2)}, u32[]{:S(2)}) collective-permute-start(f32[136,128]{1,0:T(8,128)S(1)} %select_bitcast_fusion), channel_id=1, source_target_pairs={{0,16},{16,0},{32,48},{48,32},{64,80},{80,64},{96,112},{112,96},{1... | collective-permute-start | bytes 208904 | tf_op jit(solution)/shard_map/ppermute | solution.py:42
  102.0 2.0 %collective-permute-start.19 = (f32[256,256]{1,0:T(8,128)S(1)}, f32[256,256]{1,0:T(8,128)S(1)}, u32[]{:S(2)}, u32[]{:S(2)}) collective-permute-start(f32[256,256]{1,0:T(8,128)S(1)} %get-tuple-element.27), channel_id=1, source_target_pairs={{0,16},{16,0},{32,48},{48,32},{64,80},{80,64},{96,112},{112,96},{1... | collective-permute-start | bytes 786440 | tf_op jit(solution)/shard_map/ppermute | solution.py:42
  107.4 24.4 %all-gather = bf16[2304,128]{1,0:T(8,128)(2,1)S(1)} all-gather(bf16[144,128]{1,0:T(8,128)(2,1)S(1)} %pad_maximum_fusion.1), channel_id=2, replica_groups={{0,32,64,96,128,160,192,224,256,288,320,352,384,416,448,480},{16,48,80,..., dimensions={0}, use_global_device_ids=true | all-gather | bytes 626688 | tf_op jit(solution)/shard_map/all_gather | solution.py:257
  132.9 9.0 %collective-permute-start.18 = (f32[128,128]{1,0:T(8,128)S(1)}, f32[128,128]{1,0:T(8,128)S(1)}, u32[]{:S(2)}, u32[]{:S(2)}) collective-permute-start(f32[128,128]{1,0:T(8,128)S(1)} %get-tuple-element.31), channel_id=1, source_target_pairs={{0,16},{16,0},{32,48},{48,32},{64,80},{80,64},{96,112},{112,96},{1... | collective-permute-start | bytes 196616 | tf_op jit(solution)/shard_map/ppermute | solution.py:42
  143.5 13.0 %all_to_all.16 = f32[16,1,256]{2,1,0:T(1,128)S(1)} all-to-all(f32[16,1,256]{2,1,0:T(1,128)S(1)} %copy.12), channel_id=1, replica_groups=mesh['ctx'=32,'fsdp'=16] {'fsdp'}, dimensions={0} | all-to-all | bytes 32768 | tf_op jit(solution)/shard_map/all_to_all | solution.py:282
  (89 shorter events, 27.4 us)
Async XLA Ops:
  0.9 9.8 %collective-permute-start = (bf16[256,128]{1,0:T(8,128)(2,1)S(1)}, bf16[256,128]{1,0:T(8,128)(2,1)S(1)}, u32[]{:S(2)}, u32[]{:S(2)}) collective-permute-start(bf16[256,128]{1,0:T(8,128)(2,1)S(1)} %get-tuple-element.36), channel_id=1, source_target_pairs={{0,16},{16,0},{32,48},{48,32},{64,80},{80,64},{96,112},{112,96},{1... | collective-permute-start | bytes 196616 | tf_op jit(solution)/shard_map/ppermute | solution.py:42
  12.4 66.5 %all-to-all-start = ((bf16[16,512,128]{2,1,0:T(8,128)(2,1)}), bf16[16,512,128]{2,1,0:T(8,128)(2,1)S(1)}, u32[]{:S(2)}, u32[]{:S(2)}) async-start(bf16[16,512,128]{2,1,0:T(8,128)(2,1)} %broadcast_in_dim.15), calls=%async_computation | async-start | bytes 4194304 | tf_op jit(solution)/shard_map/all_to_all | solution.py:192
  16.4 13.6 %collective-permute-start.7 = (bf16[128,768]{1,0:T(8,128)(2,1)S(1)}, bf16[128,768]{1,0:T(8,128)(2,1)S(1)}, u32[]{:S(2)}, u32[]{:S(2)}) collective-permute-start(bf16[128,768]{1,0:T(8,128)(2,1)S(1)} %bitcast_dynamic-update-slice_fusion.refs_0_), channel_id=1, source_target_pairs={{0,32},{16,48},{32,64},{48,80},{64,96},{80,112},{96,128},{112,144}... | collective-permute-start | bytes 589832 | tf_op jit(solution)/shard_map/ppermute | solution.py:38
  18.3 13.6 %collective-permute-start.1 = (bf16[128,768]{1,0:T(8,128)(2,1)S(1)}, bf16[128,768]{1,0:T(8,128)(2,1)S(1)}, u32[]{:S(2)}, u32[]{:S(2)}) collective-permute-start(bf16[128,768]{1,0:T(8,128)(2,1)S(1)} %bitcast_dynamic-update-slice_fusion.refs_0_), channel_id=1, source_target_pairs={{0,480},{16,496},{32,0},{48,16},{64,32},{80,48},{96,64},{112,80},{... | collective-permute-start | bytes 589832 | tf_op jit(solution)/shard_map/ppermute | solution.py:38
  29.9 8.4 %collective-permute-start.8 = (bf16[128,768]{1,0:T(8,128)(2,1)S(1)}, bf16[128,768]{1,0:T(8,128)(2,1)S(1)}, u32[]{:S(2)}, u32[]{:S(2)}) collective-permute-start(bf16[128,768]{1,0:T(8,128)(2,1)S(1)} %collective-permute-done.7.refs_1_), channel_id=1, source_target_pairs={{0,32},{16,48},{32,64},{48,80},{64,96},{80,112},{96,128},{112,144}... | collective-permute-start | bytes 589832 | tf_op jit(solution)/shard_map/ppermute | solution.py:38
  31.9 8.4 %collective-permute-start.2 = (bf16[128,768]{1,0:T(8,128)(2,1)S(1)}, bf16[128,768]{1,0:T(8,128)(2,1)S(1)}, u32[]{:S(2)}, u32[]{:S(2)}) collective-permute-start(bf16[128,768]{1,0:T(8,128)(2,1)S(1)} %collective-permute-done.1.refs_2_), channel_id=1, source_target_pairs={{0,480},{16,496},{32,0},{48,16},{64,32},{80,48},{96,64},{112,80},{... | collective-permute-start | bytes 589832 | tf_op jit(solution)/shard_map/ppermute | solution.py:38
  38.4 7.6 %collective-permute-start.9 = (bf16[128,768]{1,0:T(8,128)(2,1)S(1)}, bf16[128,768]{1,0:T(8,128)(2,1)S(1)}, u32[]{:S(2)}, u32[]{:S(2)}) collective-permute-start(bf16[128,768]{1,0:T(8,128)(2,1)S(1)} %collective-permute-done.8.refs_3_), channel_id=1, source_target_pairs={{0,32},{16,48},{32,64},{48,80},{64,96},{80,112},{96,128},{112,144}... | collective-permute-start | bytes 589832 | tf_op jit(solution)/shard_map/ppermute | solution.py:38
  40.3 7.6 %collective-permute-start.3 = (bf16[128,768]{1,0:T(8,128)(2,1)S(1)}, bf16[128,768]{1,0:T(8,128)(2,1)S(1)}, u32[]{:S(2)}, u32[]{:S(2)}) collective-permute-start(bf16[128,768]{1,0:T(8,128)(2,1)S(1)} %collective-permute-done.2.refs_4_), channel_id=1, source_target_pairs={{0,480},{16,496},{32,0},{48,16},{64,32},{80,48},{96,64},{112,80},{... | collective-permute-start | bytes 589832 | tf_op jit(solution)/shard_map/ppermute | solution.py:38
  46.0 7.6 %collective-permute-start.10 = (bf16[128,768]{1,0:T(8,128)(2,1)S(1)}, bf16[128,768]{1,0:T(8,128)(2,1)S(1)}, u32[]{:S(2)}, u32[]{:S(2)}) collective-permute-start(bf16[128,768]{1,0:T(8,128)(2,1)S(1)} %collective-permute-done.9.refs_5_), channel_id=1, source_target_pairs={{0,32},{16,48},{32,64},{48,80},{64,96},{80,112},{96,128},{112,144}... | collective-permute-start | bytes 589832 | tf_op jit(solution)/shard_map/ppermute | solution.py:38
  47.9 8.3 %collective-permute-start.4 = (bf16[128,768]{1,0:T(8,128)(2,1)S(1)}, bf16[128,768]{1,0:T(8,128)(2,1)S(1)}, u32[]{:S(2)}, u32[]{:S(2)}) collective-permute-start(bf16[128,768]{1,0:T(8,128)(2,1)S(1)} %collective-permute-done.3.refs_6_), channel_id=1, source_target_pairs={{0,480},{16,496},{32,0},{48,16},{64,32},{80,48},{96,64},{112,80},{... | collective-permute-start | bytes 589832 | tf_op jit(solution)/shard_map/ppermute | solution.py:38
  53.6 7.8 %collective-permute-start.11 = (bf16[128,768]{1,0:T(8,128)(2,1)S(1)}, bf16[128,768]{1,0:T(8,128)(2,1)S(1)}, u32[]{:S(2)}, u32[]{:S(2)}) collective-permute-start(bf16[128,768]{1,0:T(8,128)(2,1)S(1)} %collective-permute-done.10.refs_7_), channel_id=1, source_target_pairs={{0,32},{16,48},{32,64},{48,80},{64,96},{80,112},{96,128},{112,144}... | collective-permute-start | bytes 589832 | tf_op jit(solution)/shard_map/ppermute | solution.py:38
  56.2 7.9 %collective-permute-start.5 = (bf16[128,768]{1,0:T(8,128)(2,1)S(1)}, bf16[128,768]{1,0:T(8,128)(2,1)S(1)}, u32[]{:S(2)}, u32[]{:S(2)}) collective-permute-start(bf16[128,768]{1,0:T(8,128)(2,1)S(1)} %collective-permute-done.4.refs_8_), channel_id=1, source_target_pairs={{0,480},{16,496},{32,0},{48,16},{64,32},{80,48},{96,64},{112,80},{... | collective-permute-start | bytes 589832 | tf_op jit(solution)/shard_map/ppermute | solution.py:38
  61.4 7.9 %collective-permute-start.12 = (bf16[128,768]{1,0:T(8,128)(2,1)S(1)}, bf16[128,768]{1,0:T(8,128)(2,1)S(1)}, u32[]{:S(2)}, u32[]{:S(2)}) collective-permute-start(bf16[128,768]{1,0:T(8,128)(2,1)S(1)} %collective-permute-done.11.refs_9_), channel_id=1, source_target_pairs={{0,32},{16,48},{32,64},{48,80},{64,96},{80,112},{96,128},{112,144}... | collective-permute-start | bytes 589832 | tf_op jit(solution)/shard_map/ppermute | solution.py:38
  64.1 7.8 %collective-permute-start.6 = (bf16[128,768]{1,0:T(8,128)(2,1)S(1)}, bf16[128,768]{1,0:T(8,128)(2,1)}, u32[]{:S(2)}, u32[]{:S(2)}) collective-permute-start(bf16[128,768]{1,0:T(8,128)(2,1)S(1)} %collective-permute-done.5.refs_10_), channel_id=1, source_target_pairs={{0,480},{16,496},{32,0},{48,16},{64,32},{80,48},{96,64},{112,80},{... | collective-permute-start | bytes 589832 | tf_op jit(solution)/shard_map/ppermute | solution.py:38
  69.3 7.7 %collective-permute-start.13 = (bf16[128,768]{1,0:T(8,128)(2,1)S(1)}, bf16[128,768]{1,0:T(8,128)(2,1)}, u32[]{:S(2)}, u32[]{:S(2)}) collective-permute-start(bf16[128,768]{1,0:T(8,128)(2,1)S(1)} %collective-permute-done.12.refs_11_), channel_id=1, source_target_pairs={{0,32},{16,48},{32,64},{48,80},{64,96},{80,112},{96,128},{112,144}... | collective-permute-start | bytes 589832 | tf_op jit(solution)/shard_map/ppermute | solution.py:38
  71.9 13.1 %collective-permute-start.14 = (bf16[128,768]{1,0:T(8,128)(2,1)}, bf16[128,768]{1,0:T(8,128)(2,1)}, u32[]{:S(2)}, u32[]{:S(2)}) collective-permute-start(bf16[128,768]{1,0:T(8,128)(2,1)} %collective-permute-done.6.refs_0_), channel_id=1, source_target_pairs={{0,480},{16,496},{32,0},{48,16},{64,32},{80,48},{96,64},{112,80},{... | collective-permute-start | bytes 589832 | tf_op jit(solution)/shard_map/ppermute | solution.py:38
  77.0 8.7 %collective-permute-start.15 = (bf16[128,768]{1,0:T(8,128)(2,1)}, bf16[128,768]{1,0:T(8,128)(2,1)}, u32[]{:S(2)}, u32[]{:S(2)}) collective-permute-start(bf16[128,768]{1,0:T(8,128)(2,1)} %collective-permute-done.13.refs_1_), channel_id=1, source_target_pairs={{0,32},{16,48},{32,64},{48,80},{64,96},{80,112},{96,128},{112,144}... | collective-permute-start | bytes 589832 | tf_op jit(solution)/shard_map/ppermute | solution.py:38
  85.0 12.8 %copy-start.10 = (f32[2,256]{1,0:T(2,128)S(1)}, f32[2,256]{1,0:T(2,128)}, u32[]{:S(2)}) copy-start(f32[2,256]{1,0:T(2,128)} %decays_ref.1) | copy-start | bytes 6148
  87.5 11.8 %collective-permute-start.16 = (f32[256,512]{1,0:T(8,128)S(1)}, f32[256,512]{1,0:T(8,128)S(1)}, u32[]{:S(2)}, u32[]{:S(2)}) collective-permute-start(f32[256,512]{1,0:T(8,128)S(1)} %get-tuple-element.17), channel_id=1, source_target_pairs={{0,16},{16,0},{32,48},{48,32},{64,80},{80,64},{96,112},{112,96},{1... | collective-permute-start | bytes 1572872 | tf_op jit(solution)/shard_map/ppermute | solution.py:42
  99.6 42.4 %copy-start.13 = (f32[2]{0:T(128)S(1)}, f32[2]{0:T(128)}, u32[]{:S(2)}) copy-start(f32[2]{0:T(128)} %skip_ref.1) | copy-start | bytes 28
  99.7 4.4 %collective-permute-start.17 = (f32[136,128]{1,0:T(8,128)S(1)}, f32[136,128]{1,0:T(8,128)S(1)}, u32[]{:S(2)}, u32[]{:S(2)}) collective-permute-start(f32[136,128]{1,0:T(8,128)S(1)} %select_bitcast_fusion), channel_id=1, source_target_pairs={{0,16},{16,0},{32,48},{48,32},{64,80},{80,64},{96,112},{112,96},{1... | collective-permute-start | bytes 208904 | tf_op jit(solution)/shard_map/ppermute | solution.py:42
  102.0 40.9 %collective-permute-start.19 = (f32[256,256]{1,0:T(8,128)S(1)}, f32[256,256]{1,0:T(8,128)S(1)}, u32[]{:S(2)}, u32[]{:S(2)}) collective-permute-start(f32[256,256]{1,0:T(8,128)S(1)} %get-tuple-element.27), channel_id=1, source_target_pairs={{0,16},{16,0},{32,48},{48,32},{64,80},{80,64},{96,112},{112,96},{1... | collective-permute-start | bytes 786440 | tf_op jit(solution)/shard_map/ppermute | solution.py:42
  104.1 52.4 %copy-start.11 = (f32[2,128]{1,0:T(2,128)S(1)}, f32[2,128]{1,0:T(2,128)}, u32[]{:S(2)}) copy-start(f32[2,128]{1,0:T(2,128)} %param.10) | copy-start | bytes 3076
  132.9 10.0 %collective-permute-start.18 = (f32[128,128]{1,0:T(8,128)S(1)}, f32[128,128]{1,0:T(8,128)S(1)}, u32[]{:S(2)}, u32[]{:S(2)}) collective-permute-start(f32[128,128]{1,0:T(8,128)S(1)} %get-tuple-element.31), channel_id=1, source_target_pairs={{0,16},{16,0},{32,48},{48,32},{64,80},{80,64},{96,112},{112,96},{1... | collective-permute-start | bytes 196616 | tf_op jit(solution)/shard_map/ppermute | solution.py:42
  (12 other events, 24.7 us)

commit v4 on v3

--- a/solution.py
+++ b/solution.py
@@ -71,57 +71,103 @@
 
 
 def partial_kernel(steps, with_acc, chip_ref, tok_ref, *refs):
-    n_out = 3
-    blocks, outs = refs[: len(steps)], refs[-n_out:]
+    count = len(steps)
+    blocks, outs, held, sem = refs[:count], refs[count + with_acc : -2], refs[-2], refs[-1]
+    copies = [
+        pltpu.make_async_copy(block, held.at[at], sem.at[at]) for at, block in enumerate(blocks)
+    ]
+    for copy in copies:
+        copy.start()
     n_chip, rows = tok_ref.shape[0], tok_ref.shape[1]
-    half = rows // 2
     chip = chip_ref[0]
-    edges = [0, outs[0].shape[1], outs[0].shape[1] + outs[2].shape[1]]
-    if with_acc:
-        acc = refs[len(steps)][...]
-    else:
-        acc = jnp.zeros((rows, edges[-1]), F32)
-    order = list(zip(steps, blocks))
-    for at in range(0, len(order), 2):
-        part = order[at : at + 2]
-        toks = [tok_ref[lax.rem(chip - s + 2 * n_chip, n_chip)] for s, _ in part]
-        ws = [w[...] for _, w in part]
+    acc = refs[count][...] if with_acc else jnp.zeros((rows, held.shape[2]), F32)
+    for at in range(0, count, 2):
+        part = range(at, min(at + 2, count))
+        for p in part:
+            copies[p].wait()
+        toks = [tok_ref[lax.rem(chip - steps[p] + 2 * n_chip, n_chip)] for p in part]
+        ws = [held[p] for p in part]
         tok = jnp.concatenate(toks, axis=1) if len(part) > 1 else toks[0]
         w = jnp.concatenate(ws, axis=0) if len(part) > 1 else ws[0]
         acc += jnp.dot(tok, w, preferred_element_type=F32)
-    outs[0][...] = acc[:half, : edges[1]]
-    outs[1][...] = acc[half:, : edges[1]]
-    outs[2][...] = acc[:, edges[1] :]
-
-
-def first_kernel(steps, chip_ref, tok_ref, *refs):
-    blocks, out_ref = refs[: len(steps)], refs[-1]
-    n_chip = tok_ref.shape[0]
-    chip = chip_ref[0]
-    acc = jnp.zeros(out_ref.shape, F32)
-    order = list(zip(steps, blocks))
-    for at in range(0, len(order), 2):
-        part = order[at : at + 2]
-        toks = [tok_ref[lax.rem(chip - s + 2 * n_chip, n_chip)] for s, _ in part]
-        ws = [w[...] for _, w in part]
-        tok = jnp.concatenate(toks, axis=1) if len(part) > 1 else toks[0]
-        w = jnp.concatenate(ws, axis=0) if len(part) > 1 else ws[0]
-        acc += jnp.dot(tok, w, preferred_element_type=F32)
-    out_ref[...] = acc
-
-
-def local_kernel(own_ref, got_ref, cols_ref, val_ref, maps_ref, local_ref):
-    heads, n_state, width = local_ref.shape
-    both = own_ref[...] + got_ref[...]
+    if len(outs) == 1:
+        outs[0][...] = acc
+    else:
+        outs[0][...] = acc[: rows // 2]
+        outs[1][...] = acc[rows // 2 :]
+
+
+def partial_product(n_out, steps, chip, tok, blocks, acc):
+    shape = (tok.shape[1] // n_out, blocks[0].shape[1])
+    count = len(steps)
+    return pl.pallas_call(
+        functools.partial(partial_kernel, steps, len(acc)),
+        out_shape=[jax.ShapeDtypeStruct(shape, F32)] * n_out,
+        in_specs=[SMEM, VMEM] + [pl.BlockSpec(memory_space=pltpu.HBM)] * count + [VMEM] * len(acc),
+        out_specs=[VMEM] * n_out,
+        scratch_shapes=[
+            pltpu.VMEM((count,) + blocks[0].shape, BF16),
+            pltpu.SemaphoreType.DMA((count,)),
+        ],
+        compiler_params=PARAMS,
+    )(chip, tok, *blocks, *acc)
+
+
+def local_kernel(core_ref, own_ref, got_ref, cols_ref, ends_ref, val_ref, maps_ref, keep_ref, send_ref):
+    heads, spare, width = ends_ref.shape
+    n_state = keep_ref.shape[0] - spare
+    n_val = heads * width
+    both = own_ref[:, : n_val + 2 * n_state] + got_ref[:, : n_val + 2 * n_state]
     act = silu(both).astype(BF16)
-    values = act[:, : heads * width]
-    maps = act[:, heads * width :]
+    values = act[:, :n_val]
+    maps = act[:, n_val:]
     val_ref[...] = values
     maps_ref[...] = maps
+    states = []
     for h in range(heads):
         v = values[:, h * width : (h + 1) * width].astype(F32)
         scaled = (cols_ref[:, h : h + 1] * v).astype(BF16)
-        local_ref[h] = lax.dot_general(maps[:, :n_state], scaled, TN, preferred_element_type=F32)
+        states.append(
+            lax.dot_general(maps[:, :n_state], scaled, TN, preferred_element_type=F32)
+        )
+    even = core_ref[0] == 0
+    keep_ref[:n_state] = jnp.where(even, states[0], states[1])
+    send_ref[:n_state] = jnp.where(even, states[1], states[0])
+    keep_ref[n_state:] = jnp.where(even, ends_ref[0], ends_ref[1])
+    send_ref[n_state:] = jnp.where(even, ends_ref[1], ends_ref[0])
+
+
+def chip_kernel(core_ref, keep_ref, got_ref, first_ref, packed_ref):
+    spare = packed_ref.shape[0] - 16
+    even = core_ref[0] == 0
+    keep, got = keep_ref[...], got_ref[...]
+    first, second = jnp.where(even, keep, got), jnp.where(even, got, keep)
+    first_ref[...] = first
+    s0, g0 = first[:spare], first[spare : spare + 1]
+    s1, g1 = second[:spare], second[spare : spare + 1]
+    packed_ref[:spare] = (g1 * s0 + s1).astype(BF16)
+    gate = jnp.broadcast_to(g0 * g1, (16, s0.shape[1]))
+    hi = gate.astype(BF16).astype(F32)
+    mid = (gate - hi).astype(BF16).astype(F32)
+    low = gate - hi - mid
+    row = lax.broadcasted_iota(jnp.int32, gate.shape, 0)
+    parts = jnp.where(row == 0, hi, jnp.where(row == 1, mid, jnp.where(row == 2, low, 0.0)))
+    packed_ref[spare:] = parts.astype(BF16)
+
+
+def incoming_kernel(core_ref, chip_ref, all_ref, first_ref, keep_ref, give_ref):
+    n_chip, n_state = all_ref.shape[0], keep_ref.shape[0]
+    chip = chip_ref[0]
+    state = jnp.zeros(keep_ref.shape, F32)
+    for z in range(n_chip - 1):
+        parts = all_ref[z, n_state:].astype(F32)
+        gate = parts[0:1] + parts[1:2] + parts[2:3]
+        later = gate * state + all_ref[z, :n_state].astype(F32)
+        state = jnp.where(z < chip, later, state)
+    second = first_ref[n_state : n_state + 1] * state + first_ref[:n_state]
+    even = core_ref[0] == 0
+    keep_ref[...] = jnp.where(even, state, second)
+    give_ref[...] = jnp.where(even, second, state)
 
 
 def diag_kernel(skip_ref, maps_ref, val_ref, decay_ref, out_ref):
@@ -146,7 +192,8 @@
     core = core_ref[0]
     c_map = maps_ref[:, n_state:]
     kept, came = kept_ref[...], came_ref[...]
-    gate = (gate_ref[...] + got_ref[...]).astype(BF16).astype(F32)
+    n_gate = gate_ref.shape[1] - heads * width
+    gate = (gate_ref[:, n_gate:] + got_ref[:, n_gate:]).astype(BF16).astype(F32)
     gate = silu(gate)
     total = jnp.zeros((rows, width), F32)
     for h in range(heads):
@@ -194,76 +241,59 @@
     block = jnp.concatenate(
         [w_xz[:, :, :width].reshape(depth, -1), w_bc, w_xz[:, :, width:].reshape(depth, -1)], axis=1
     )
-    up = down = block
-    steps, blocks = [0], [block]
-    for s in range(1, n_chip // 2 + 1):
-        up = shift(up, 2)
-        steps.append(s)
-        blocks.append(up)
-        if s < n_chip // 2:
-            down = shift(down, -2)
-            steps.append(-s)
-            blocks.append(down)
-    early = n_chip - 4
-
+    n_val = heads * width
     cols, decay, ends = call(
         decay_kernel,
         [((rows, 2 * heads), F32), ((heads, rows, rows), F32), ((heads, 8, width), F32)],
         decays,
         boundaries.reshape(1, rows),
     )
-
-    n_first = heads * width + 2 * n_state
-    acc = call(
-        functools.partial(first_kernel, steps[:early]),
-        [((2 * rows, block.shape[1]), F32)],
-        chip_1,
-        tok,
-        *blocks[:early],
-        smem=1,
-    )
-    own, other, gates = call(
-        functools.partial(partial_kernel, steps[early:], True),
-        [((rows, n_first), F32), ((rows, n_first), F32), ((2 * rows, heads * width), F32)],
-        chip_1,
-        tok,
-        *blocks[early:],
-        acc,
-        smem=1,
-    )
+    up = down = block
+    steps, blocks, acc = [0], [block], ()
+    half = n_chip // 2
+    for s in range(1, half + 1):
+        if s in (half - 2, half):
+            product = partial_product(1, steps, chip_1, tok, blocks, acc)[0]
+            up, down, product, cols, decay, ends = lax.optimization_barrier(
+                (up, down, product, cols, decay, ends)
+            )
+            steps, blocks, acc = [], [], (product,)
+        up = shift(up, 2)
+        steps.append(s)
+        blocks.append(up)
+        if s < half:
+            down = shift(down, -2)
+            steps.append(-s)
+            blocks.append(down)
+    own, other = partial_product(2, steps, chip_1, tok, blocks, acc)
     got = swap_cores(other)
-    gate_got = swap_cores(gates[rows:])
-    values, maps, local = call(
+
+    state = ((n_state + 8, width), F32)
+    values, maps, keep, send = call(
         local_kernel,
-        [((rows, heads * width), BF16), ((rows, 2 * n_state), BF16), ((heads, n_state, width), F32)],
+        [((rows, n_val), BF16), ((rows, 2 * n_state), BF16), state, state],
+        core_1,
         own,
         got,
         cols,
-    )
-
-    mine = jnp.concatenate([local, ends], axis=1)
-    keep, send = mine_other(mine[0], mine[1])
-    first, second = mine_other(keep, swap_cores(send))
-    diag = call(diag_kernel, [((rows, heads * width), F32)], skip, maps, values, decay, smem=1)
-    s0, g0, s1, g1 = first[:n_state], first[n_state, 0], second[:n_state], second[n_state, 0]
-    s_chip, g_chip = g1 * s0 + s1, g0 * g1
-    g_hi = g_chip.astype(BF16)
-    g_mid = (g_chip - g_hi.astype(F32)).astype(BF16)
-    g_lo = (g_chip - g_hi.astype(F32) - g_mid.astype(F32)).astype(BF16)
-    g_row = jnp.stack([g_hi, g_mid, g_lo] + [jnp.zeros_like(g_hi)] * 13)
-    packed = jnp.concatenate(
-        [s_chip.astype(BF16), jnp.broadcast_to(g_row[:, None], (16, width))], axis=0
+        ends,
+        smem=1,
+    )
+    came = swap_cores(send)
+    diag = call(diag_kernel, [((rows, n_val), F32)], skip, maps, values, decay, smem=1)
+    first, packed = call(
+        chip_kernel, [state, ((n_state + 16, width), BF16)], core_1, keep, came, smem=1
     )
     everyone = lax.all_gather(packed, "ctx", axis=0, axis_index_groups=same_core)
-    g_all = everyone[:, n_state : n_state + 3, 0].astype(F32)
-    g_all = g_all[:, 0] + g_all[:, 1] + g_all[:, 2]
-    at = jnp.arange(n_chip)
-    between = (at[None, :] > at[:, None]) & (at[None, :] < chip)
-    coef = jnp.prod(jnp.where(between, g_all[None, :], 1.0), axis=1)
-    coef = jnp.where(at < chip, coef, 0.0)
-    e0 = jnp.sum(coef[:, None, None] * everyone[:, :n_state].astype(F32), axis=0)
-    e1 = g0 * e0 + s0
-    kept, give = mine_other(e0, e1)
+    kept, give = call(
+        incoming_kernel,
+        [((n_state, width), F32)] * 2,
+        core_1,
+        chip_1,
+        everyone,
+        first,
+        smem=2,
+    )
     came = swap_cores(give)
 
     gated, sums = call(
@@ -275,8 +305,8 @@
         came,
         maps,
         cols,
-        gates[:rows],
-        gate_got,
+        own,
+        got,
         smem=1,
     )
     sums = lax.all_to_all(sums, "fsdp", 0, 0, tiled=True)

time: 159 us -> 169 us (1.063)
  waiting for transfers between devices: 8.33 us -> 22.6 us
  local copies, waits for them, and re-layouts: 12.9 us -> 7.49 us
  Pallas kernels: 6.38 us -> 9.91 us
  other arithmetic: 2.6 us -> 0.89 us
    ppermute x15, waiting for transfers between devices: 7.93 us -> 18.9 us  [shift(): return lax.ppermute(x, 'ctx', [(i, (i + by) % n) for i in range(n)])]
    pallas_call x0 -> x3, Pallas kernels: none -> 6.49 us  [partial_product(): pl.pallas_call(functools.partial(partial_kernel, steps, len(acc)), out_sh...]
    unnamed x35 -> x27, local copies, waits for them, and re-layouts: 8.15 us -> 4.85 us
    ppermute x5 -> x4, waiting for transfers between devices: 0.4 us -> 3.66 us  [swap_cores(): lax.ppermute(x, 'ctx', [(i, i ^ 1) for i in range(lax.axis_size('ctx'))])]
    pallas_call x7, Pallas kernels: 6.38 us -> 3.42 us  [call(): pl.pallas_call(kernel, out_shape=shapes, in_specs=[SMEM] * smem + [VMEM]...]
    ppermute x15, starting transfers between devices: 51.8 us -> 53.8 us  [shift(): return lax.ppermute(x, 'ctx', [(i, (i + by) % n) for i in range(n)])]
    ppermute x5 -> x4, starting transfers between devices: 32.4 us -> 31.5 us  [swap_cores(): lax.ppermute(x, 'ctx', [(i, i ^ 1) for i in range(lax.axis_size('ctx'))])]
  transfers between devices with their start and end apart: 21 -> 20, of which waited for: 7 -> 11; matrix products, arithmetic and copies ran while one was open for 3% -> 0% of each run, Pallas kernels for 2% -> 1%
where the time goes in v4:
time: 169 us; the launch traced here: 168 us
  starting transfers between devices  89.1 us (53%)
  blocking collectives  37.5 us (22%)
  waiting for transfers between devices  22.6 us (13%)
  Pallas kernels  9.91 us (6%)
  local copies, waits for them, and re-layouts  7.49 us (4%)
    ppermute x15, starting transfers between devices, shift(): return lax.ppermute(x, 'ctx', [(i, (i + by) % n) for i in range(n)])  53.8 us
    ppermute x4, starting transfers between devices, swap_cores(): lax.ppermute(x, 'ctx', [(i, i ^ 1) for i in range(lax.axis_size('ctx'))])  31.5 us
    all_gather x1, blocking collectives, per_device(): lax.all_gather(packed, 'ctx', axis=0, axis_index_groups=same_core)  24.3 us
    ppermute x15, waiting for transfers between devices, shift(): return lax.ppermute(x, 'ctx', [(i, (i + by) % n) for i in range(n)])  18.9 us
    all_to_all x1, blocking collectives, per_device(): sums = lax.all_to_all(sums, 'fsdp', 0, 0, tiled=True)  13.2 us
    pallas_call x3, Pallas kernels, partial_product(): pl.pallas_call(functools.partial(partial_kernel, steps, len(acc)), out_sh...  6.49 us
    unnamed x27, local copies, waits for them, and re-layouts  4.85 us
    all_to_all x1, starting transfers between devices, per_device(): tok = lax.all_to_all(copies, 'fsdp', 0, 0)  3.86 us
  transfers between devices with their start and end apart: 20, of which 11 were waited for; matrix products, arithmetic and copies ran while one was open for 0% of the time, Pallas kernels for 1%

profile of v4, /device:TPU:1, one launch (start us, length us, event | category | flops | bytes accessed | tf_op | source)
XLA Modules:
  0.0 167.9 jit_solution(3480457987392232131)
XLA Ops:
  0.9 8.8 %collective-permute-start = (bf16[256,128]{1,0:T(8,128)(2,1)S(1)}, bf16[256,128]{1,0:T(8,128)(2,1)S(1)}, u32[]{:S(2)}, u32[]{:S(2)}) collective-permute-start(bf16[256,128]{1,0:T(8,128)(2,1)S(1)} %get-tuple-element.60), channel_id=1, source_target_pairs={{0,16},{16,0},{32,48},{48,32},{64,80},{80,64},{96,112},{112,96},{1... | collective-permute-start | bytes 196616 | tf_op jit(solution)/shard_map/ppermute | solution.py:42
  12.3 3.9 %all-to-all-start = ((bf16[16,512,128]{2,1,0:T(8,128)(2,1)}), bf16[16,512,128]{2,1,0:T(8,128)(2,1)S(1)}, u32[]{:S(2)}, u32[]{:S(2)}) async-start(bf16[16,512,128]{2,1,0:T(8,128)(2,1)} %broadcast_in_dim.2), calls=%async_computation | async-start | bytes 4194304 | tf_op jit(solution)/shard_map/all_to_all | solution.py:239
  16.4 8.8 %collective-permute-start.6 = (bf16[128,768]{1,0:T(8,128)(2,1)S(1)}, bf16[128,768]{1,0:T(8,128)(2,1)S(1)}, u32[]{:S(2)}, u32[]{:S(2)}) collective-permute-start(bf16[128,768]{1,0:T(8,128)(2,1)S(1)} %bitcast_dynamic-update-slice_fusion.refs_0_), channel_id=1, source_target_pairs={{0,480},{16,496},{32,0},{48,16},{64,32},{80,48},{96,64},{112,80},{... | collective-permute-start | bytes 589832 | tf_op jit(solution)/shard_map/ppermute | solution.py:38
  25.2 1.9 %collective-permute-start.1 = (bf16[128,768]{1,0:T(8,128)(2,1)S(1)}, bf16[128,768]{1,0:T(8,128)(2,1)S(1)}, u32[]{:S(2)}, u32[]{:S(2)}) collective-permute-start(bf16[128,768]{1,0:T(8,128)(2,1)S(1)} %bitcast_dynamic-update-slice_fusion.refs_0_), channel_id=1, source_target_pairs={{0,32},{16,48},{32,64},{48,80},{64,96},{80,112},{96,128},{112,144}... | collective-permute-start | bytes 589832 | tf_op jit(solution)/shard_map/ppermute | solution.py:38
  28.8 5.3 %collective-permute-start.7 = (bf16[128,768]{1,0:T(8,128)(2,1)S(1)}, bf16[128,768]{1,0:T(8,128)(2,1)S(1)}, u32[]{:S(2)}, u32[]{:S(2)}) collective-permute-start(bf16[128,768]{1,0:T(8,128)(2,1)S(1)} %collective-permute-done.6.refs_2_), channel_id=1, source_target_pairs={{0,480},{16,496},{32,0},{48,16},{64,32},{80,48},{96,64},{112,80},{... | collective-permute-start | bytes 589832 | tf_op jit(solution)/shard_map/ppermute | solution.py:38
  34.1 1.9 %collective-permute-start.2 = (bf16[128,768]{1,0:T(8,128)(2,1)S(1)}, bf16[128,768]{1,0:T(8,128)(2,1)S(1)}, u32[]{:S(2)}, u32[]{:S(2)}) collective-permute-start(bf16[128,768]{1,0:T(8,128)(2,1)S(1)} %collective-permute-done.1.refs_1_), channel_id=1, source_target_pairs={{0,32},{16,48},{32,64},{48,80},{64,96},{80,112},{96,128},{112,144}... | collective-permute-start | bytes 589832 | tf_op jit(solution)/shard_map/ppermute | solution.py:38
  36.7 5.4 %collective-permute-start.8 = (bf16[128,768]{1,0:T(8,128)(2,1)S(1)}, bf16[128,768]{1,0:T(8,128)(2,1)S(1)}, u32[]{:S(2)}, u32[]{:S(2)}) collective-permute-start(bf16[128,768]{1,0:T(8,128)(2,1)S(1)} %collective-permute-done.7.refs_4_), channel_id=1, source_target_pairs={{0,480},{16,496},{32,0},{48,16},{64,32},{80,48},{96,64},{112,80},{... | collective-permute-start | bytes 589832 | tf_op jit(solution)/shard_map/ppermute | solution.py:38
  42.1 1.9 %collective-permute-start.3 = (bf16[128,768]{1,0:T(8,128)(2,1)S(1)}, bf16[128,768]{1,0:T(8,128)(2,1)S(1)}, u32[]{:S(2)}, u32[]{:S(2)}) collective-permute-start(bf16[128,768]{1,0:T(8,128)(2,1)S(1)} %collective-permute-done.2.refs_3_), channel_id=1, source_target_pairs={{0,32},{16,48},{32,64},{48,80},{64,96},{80,112},{96,128},{112,144}... | collective-permute-start | bytes 589832 | tf_op jit(solution)/shard_map/ppermute | solution.py:38
  44.7 5.3 %collective-permute-start.9 = (bf16[128,768]{1,0:T(8,128)(2,1)S(1)}, bf16[128,768]{1,0:T(8,128)(2,1)}, u32[]{:S(2)}, u32[]{:S(2)}) collective-permute-start(bf16[128,768]{1,0:T(8,128)(2,1)S(1)} %collective-permute-done.8.refs_6_), channel_id=1, source_target_pairs={{0,480},{16,496},{32,0},{48,16},{64,32},{80,48},{96,64},{112,80},{... | collective-permute-start | bytes 589832 | tf_op jit(solution)/shard_map/ppermute | solution.py:38
  50.7 1.9 %collective-permute-start.4 = (bf16[128,768]{1,0:T(8,128)(2,1)S(1)}, bf16[128,768]{1,0:T(8,128)(2,1)}, u32[]{:S(2)}, u32[]{:S(2)}) collective-permute-start(bf16[128,768]{1,0:T(8,128)(2,1)S(1)} %collective-permute-done.3.refs_5_), channel_id=1, source_target_pairs={{0,32},{16,48},{32,64},{48,80},{64,96},{80,112},{96,128},{112,144}... | collective-permute-start | bytes 589832 | tf_op jit(solution)/shard_map/ppermute | solution.py:38
  53.3 4.6 %collective-permute-start.10 = (bf16[128,768]{1,0:T(8,128)(2,1)}, bf16[128,768]{1,0:T(8,128)(2,1)}, u32[]{:S(2)}, u32[]{:S(2)}) collective-permute-start(bf16[128,768]{1,0:T(8,128)(2,1)} %collective-permute-done.9.refs_8_), channel_id=1, source_target_pairs={{0,480},{16,496},{32,0},{48,16},{64,32},{80,48},{96,64},{112,80},{... | collective-permute-start | bytes 589832 | tf_op jit(solution)/shard_map/ppermute | solution.py:38
  61.4 4.9 %collective-permute-done.5.refs_9_ = bf16[128,768]{1,0:T(8,128)(2,1)} collective-permute-done((bf16[128,768]{1,0:T(8,128)(2,1)}, bf16[128,768]{1,0:T(8,128)(2,1)}, u32[]{:S(2)}, u32[]{:S(2)}) %collective-permute-start.5) | collective-permute-done | bytes 196640 | tf_op jit(solution)/shard_map/ppermute | solution.py:38
  69.1 4.0 %shard_map.73.refs_4_ = f32[512,768]{1,0:T(8,128)S(1)} custom-call(s32[1]{0:T(128)} %bitcast.1.chip_ref, bf16[16,512,128]{2,1,0:T(8,128)(2,1)S(1)} %all-to-all-done.tok_ref, bf16[128,768]{1,0:T(8,128)(2,1)S(1)} %bitcast_dynamic-update-slice_fusion.refs_0_, bf16[128,768]{1,0:T(8,128)(2,1)S(1)} %collective-permute-done.1.refs_1_, ...), custom_call_target="tpu_custom_call" | custom-call | tf_op jit(solution)/shard_map/pallas_call | solution.py:103
  73.1 1.9 %collective-permute-start.11 = (bf16[128,768]{1,0:T(8,128)(2,1)}, bf16[128,768]{1,0:T(8,128)(2,1)S(1)}, u32[]{:S(2)}, u32[]{:S(2)}) collective-permute-start(bf16[128,768]{1,0:T(8,128)(2,1)} %collective-permute-done.5.refs_9_), channel_id=1, source_target_pairs={{0,32},{16,48},{32,64},{48,80},{64,96},{80,112},{96,128},{112,144}... | collective-permute-start | bytes 589832 | tf_op jit(solution)/shard_map/ppermute | solution.py:38
  75.0 4.6 %collective-permute-start.13 = (bf16[128,768]{1,0:T(8,128)(2,1)}, bf16[128,768]{1,0:T(8,128)(2,1)S(1)}, u32[]{:S(2)}, u32[]{:S(2)}) collective-permute-start(bf16[128,768]{1,0:T(8,128)(2,1)} %collective-permute-done.10.refs_10_), channel_id=1, source_target_pairs={{0,480},{16,496},{32,0},{48,16},{64,32},{80,48},{96,64},{112,80},{... | collective-permute-start | bytes 589832 | tf_op jit(solution)/shard_map/ppermute | solution.py:38
  82.8 4.6 %collective-permute-start.14 = (bf16[128,768]{1,0:T(8,128)(2,1)S(1)}, bf16[128,768]{1,0:T(8,128)(2,1)S(1)}, u32[]{:S(2)}, u32[]{:S(2)}) collective-permute-start(bf16[128,768]{1,0:T(8,128)(2,1)S(1)} %collective-permute-done.13.refs_1_), channel_id=1, source_target_pairs={{0,480},{16,496},{32,0},{48,16},{64,32},{80,48},{96,64},{112,80},{... | collective-permute-start | bytes 589832 | tf_op jit(solution)/shard_map/ppermute | solution.py:38
  87.4 1.9 %collective-permute-done.12.refs_2_ = bf16[128,768]{1,0:T(8,128)(2,1)S(1)} collective-permute-done((bf16[128,768]{1,0:T(8,128)(2,1)S(1)}, bf16[128,768]{1,0:T(8,128)(2,1)S(1)}, u32[]{:S(2)}, u32[]{:S(2)}) %collective-permute-start.12) | collective-permute-done | bytes 196640 | tf_op jit(solution)/shard_map/ppermute | solution.py:38
  92.9 1.9 %collective-permute-start.15 = (bf16[128,768]{1,0:T(8,128)(2,1)S(1)}, bf16[128,768]{1,0:T(8,128)(2,1)S(1)}, u32[]{:S(2)}, u32[]{:S(2)}) collective-permute-start(bf16[128,768]{1,0:T(8,128)(2,1)S(1)} %collective-permute-done.12.refs_2_), channel_id=1, source_target_pairs={{0,32},{16,48},{32,64},{48,80},{64,96},{80,112},{96,128},{112,144}... | collective-permute-start | bytes 589832 | tf_op jit(solution)/shard_map/ppermute | solution.py:38
  94.9 6.2 %collective-permute-done.15.refs_0_ = bf16[128,768]{1,0:T(8,128)(2,1)S(1)} collective-permute-done((bf16[128,768]{1,0:T(8,128)(2,1)S(1)}, bf16[128,768]{1,0:T(8,128)(2,1)S(1)}, u32[]{:S(2)}, u32[]{:S(2)}) %collective-permute-start.15) | collective-permute-done | bytes 196640 | tf_op jit(solution)/shard_map/ppermute | solution.py:38
  101.7 11.2 %collective-permute-start.16 = (f32[256,768]{1,0:T(8,128)S(1)}, f32[256,768]{1,0:T(8,128)S(1)}, u32[]{:S(2)}, u32[]{:S(2)}) collective-permute-start(f32[256,768]{1,0:T(8,128)S(1)} %get-tuple-element.43), channel_id=1, source_target_pairs={{0,16},{16,0},{32,48},{48,32},{64,80},{80,64},{96,112},{112,96},{1... | collective-permute-start | bytes 2359304 | tf_op jit(solution)/shard_map/ppermute | solution.py:42
  115.2 2.3 %collective-permute-start.17 = (f32[136,128]{1,0:T(8,128)S(1)}, f32[136,128]{1,0:T(8,128)S(1)}, u32[]{:S(2)}, u32[]{:S(2)}) collective-permute-start(f32[136,128]{1,0:T(8,128)S(1)} %get-tuple-element.50), channel_id=1, source_target_pairs={{0,16},{16,0},{32,48},{48,32},{64,80},{80,64},{96,112},{112,96},{1... | collective-permute-start | bytes 208904 | tf_op jit(solution)/shard_map/ppermute | solution.py:42
  118.4 24.3 %all-gather = bf16[2304,128]{1,0:T(8,128)(2,1)S(1)} all-gather(bf16[144,128]{1,0:T(8,128)(2,1)S(1)} %get-tuple-element.51), channel_id=2, replica_groups={{0,32,64,96,128,160,192,224,256,288,320,352,384,416,448,480},{16,48,80,..., dimensions={0}, use_global_device_ids=true | all-gather | bytes 626688 | tf_op jit(solution)/shard_map/all_gather | solution.py:287
  142.8 9.2 %collective-permute-start.18 = (f32[128,128]{1,0:T(8,128)S(1)}, f32[128,128]{1,0:T(8,128)S(1)}, u32[]{:S(2)}, u32[]{:S(2)}) collective-permute-start(f32[128,128]{1,0:T(8,128)S(1)} %get-tuple-element.54), channel_id=1, source_target_pairs={{0,16},{16,0},{32,48},{48,32},{64,80},{80,64},{96,112},{112,96},{1... | collective-permute-start | bytes 196616 | tf_op jit(solution)/shard_map/ppermute | solution.py:42
  153.6 13.2 %all_to_all.16 = f32[16,1,256]{2,1,0:T(1,128)S(1)} all-to-all(f32[16,1,256]{2,1,0:T(1,128)S(1)} %copy.8), channel_id=1, replica_groups=mesh['ctx'=32,'fsdp'=16] {'fsdp'}, dimensions={0} | all-to-all | bytes 32768 | tf_op jit(solution)/shard_map/all_to_all | solution.py:312
  (62 shorter events, 27.8 us)
Async XLA Ops:
  0.9 9.7 %collective-permute-start = (bf16[256,128]{1,0:T(8,128)(2,1)S(1)}, bf16[256,128]{1,0:T(8,128)(2,1)S(1)}, u32[]{:S(2)}, u32[]{:S(2)}) collective-permute-start(bf16[256,128]{1,0:T(8,128)(2,1)S(1)} %get-tuple-element.60), channel_id=1, source_target_pairs={{0,16},{16,0},{32,48},{48,32},{64,80},{80,64},{96,112},{112,96},{1... | collective-permute-start | bytes 196616 | tf_op jit(solution)/shard_map/ppermute | solution.py:42
  12.3 48.0 %copy-start.6 = (f32[2,256]{1,0:T(2,128)S(1)}, f32[2,256]{1,0:T(2,128)}, u32[]{:S(2)}) copy-start(f32[2,256]{1,0:T(2,128)} %decays_ref.1) | copy-start | bytes 6148
  12.3 48.0 %copy-start.8 = (s32[256]{0:T(256)S(1)}, s32[256]{0:T(256)}, u32[]{:S(2)}) copy-start(s32[256]{0:T(256)} %param.13) | copy-start | bytes 3076
  12.3 54.0 %all-to-all-start = ((bf16[16,512,128]{2,1,0:T(8,128)(2,1)}), bf16[16,512,128]{2,1,0:T(8,128)(2,1)S(1)}, u32[]{:S(2)}, u32[]{:S(2)}) async-start(bf16[16,512,128]{2,1,0:T(8,128)(2,1)} %broadcast_in_dim.2), calls=%async_computation | async-start | bytes 4194304 | tf_op jit(solution)/shard_map/all_to_all | solution.py:239
  16.4 12.4 %collective-permute-start.6 = (bf16[128,768]{1,0:T(8,128)(2,1)S(1)}, bf16[128,768]{1,0:T(8,128)(2,1)S(1)}, u32[]{:S(2)}, u32[]{:S(2)}) collective-permute-start(bf16[128,768]{1,0:T(8,128)(2,1)S(1)} %bitcast_dynamic-update-slice_fusion.refs_0_), channel_id=1, source_target_pairs={{0,480},{16,496},{32,0},{48,16},{64,32},{80,48},{96,64},{112,80},{... | collective-permute-start | bytes 589832 | tf_op jit(solution)/shard_map/ppermute | solution.py:38
  25.2 8.9 %collective-permute-start.1 = (bf16[128,768]{1,0:T(8,128)(2,1)S(1)}, bf16[128,768]{1,0:T(8,128)(2,1)S(1)}, u32[]{:S(2)}, u32[]{:S(2)}) collective-permute-start(bf16[128,768]{1,0:T(8,128)(2,1)S(1)} %bitcast_dynamic-update-slice_fusion.refs_0_), channel_id=1, source_target_pairs={{0,32},{16,48},{32,64},{48,80},{64,96},{80,112},{96,128},{112,144}... | collective-permute-start | bytes 589832 | tf_op jit(solution)/shard_map/ppermute | solution.py:38
  28.8 7.9 %collective-permute-start.7 = (bf16[128,768]{1,0:T(8,128)(2,1)S(1)}, bf16[128,768]{1,0:T(8,128)(2,1)S(1)}, u32[]{:S(2)}, u32[]{:S(2)}) collective-permute-start(bf16[128,768]{1,0:T(8,128)(2,1)S(1)} %collective-permute-done.6.refs_2_), channel_id=1, source_target_pairs={{0,480},{16,496},{32,0},{48,16},{64,32},{80,48},{96,64},{112,80},{... | collective-permute-start | bytes 589832 | tf_op jit(solution)/shard_map/ppermute | solution.py:38
  34.1 8.0 %collective-permute-start.2 = (bf16[128,768]{1,0:T(8,128)(2,1)S(1)}, bf16[128,768]{1,0:T(8,128)(2,1)S(1)}, u32[]{:S(2)}, u32[]{:S(2)}) collective-permute-start(bf16[128,768]{1,0:T(8,128)(2,1)S(1)} %collective-permute-done.1.refs_1_), channel_id=1, source_target_pairs={{0,32},{16,48},{32,64},{48,80},{64,96},{80,112},{96,128},{112,144}... | collective-permute-start | bytes 589832 | tf_op jit(solution)/shard_map/ppermute | solution.py:38
  36.7 8.0 %collective-permute-start.8 = (bf16[128,768]{1,0:T(8,128)(2,1)S(1)}, bf16[128,768]{1,0:T(8,128)(2,1)S(1)}, u32[]{:S(2)}, u32[]{:S(2)}) collective-permute-start(bf16[128,768]{1,0:T(8,128)(2,1)S(1)} %collective-permute-done.7.refs_4_), channel_id=1, source_target_pairs={{0,480},{16,496},{32,0},{48,16},{64,32},{80,48},{96,64},{112,80},{... | collective-permute-start | bytes 589832 | tf_op jit(solution)/shard_map/ppermute | solution.py:38
  42.1 8.6 %collective-permute-start.3 = (bf16[128,768]{1,0:T(8,128)(2,1)S(1)}, bf16[128,768]{1,0:T(8,128)(2,1)S(1)}, u32[]{:S(2)}, u32[]{:S(2)}) collective-permute-start(bf16[128,768]{1,0:T(8,128)(2,1)S(1)} %collective-permute-done.2.refs_3_), channel_id=1, source_target_pairs={{0,32},{16,48},{32,64},{48,80},{64,96},{80,112},{96,128},{112,144}... | collective-permute-start | bytes 589832 | tf_op jit(solution)/shard_map/ppermute | solution.py:38
  44.7 8.6 %collective-permute-start.9 = (bf16[128,768]{1,0:T(8,128)(2,1)S(1)}, bf16[128,768]{1,0:T(8,128)(2,1)}, u32[]{:S(2)}, u32[]{:S(2)}) collective-permute-start(bf16[128,768]{1,0:T(8,128)(2,1)S(1)} %collective-permute-done.8.refs_6_), channel_id=1, source_target_pairs={{0,480},{16,496},{32,0},{48,16},{64,32},{80,48},{96,64},{112,80},{... | collective-permute-start | bytes 589832 | tf_op jit(solution)/shard_map/ppermute | solution.py:38
  50.7 7.7 %collective-permute-start.4 = (bf16[128,768]{1,0:T(8,128)(2,1)S(1)}, bf16[128,768]{1,0:T(8,128)(2,1)}, u32[]{:S(2)}, u32[]{:S(2)}) collective-permute-start(bf16[128,768]{1,0:T(8,128)(2,1)S(1)} %collective-permute-done.3.refs_5_), channel_id=1, source_target_pairs={{0,32},{16,48},{32,64},{48,80},{64,96},{80,112},{96,128},{112,144}... | collective-permute-start | bytes 589832 | tf_op jit(solution)/shard_map/ppermute | solution.py:38
  53.3 8.2 %collective-permute-start.10 = (bf16[128,768]{1,0:T(8,128)(2,1)}, bf16[128,768]{1,0:T(8,128)(2,1)}, u32[]{:S(2)}, u32[]{:S(2)}) collective-permute-start(bf16[128,768]{1,0:T(8,128)(2,1)} %collective-permute-done.9.refs_8_), channel_id=1, source_target_pairs={{0,480},{16,496},{32,0},{48,16},{64,32},{80,48},{96,64},{112,80},{... | collective-permute-start | bytes 589832 | tf_op jit(solution)/shard_map/ppermute | solution.py:38
  58.4 7.9 %collective-permute-start.5 = (bf16[128,768]{1,0:T(8,128)(2,1)}, bf16[128,768]{1,0:T(8,128)(2,1)}, u32[]{:S(2)}, u32[]{:S(2)}) collective-permute-start(bf16[128,768]{1,0:T(8,128)(2,1)} %collective-permute-done.4.refs_7_), channel_id=1, source_target_pairs={{0,32},{16,48},{32,64},{48,80},{64,96},{80,112},{96,128},{112,144}... | collective-permute-start | bytes 589832 | tf_op jit(solution)/shard_map/ppermute | solution.py:38
  73.1 7.8 %collective-permute-start.11 = (bf16[128,768]{1,0:T(8,128)(2,1)}, bf16[128,768]{1,0:T(8,128)(2,1)S(1)}, u32[]{:S(2)}, u32[]{:S(2)}) collective-permute-start(bf16[128,768]{1,0:T(8,128)(2,1)} %collective-permute-done.5.refs_9_), channel_id=1, source_target_pairs={{0,32},{16,48},{32,64},{48,80},{64,96},{80,112},{96,128},{112,144}... | collective-permute-start | bytes 589832 | tf_op jit(solution)/shard_map/ppermute | solution.py:38
  75.0 7.8 %collective-permute-start.13 = (bf16[128,768]{1,0:T(8,128)(2,1)}, bf16[128,768]{1,0:T(8,128)(2,1)S(1)}, u32[]{:S(2)}, u32[]{:S(2)}) collective-permute-start(bf16[128,768]{1,0:T(8,128)(2,1)} %collective-permute-done.10.refs_10_), channel_id=1, source_target_pairs={{0,480},{16,496},{32,0},{48,16},{64,32},{80,48},{96,64},{112,80},{... | collective-permute-start | bytes 589832 | tf_op jit(solution)/shard_map/ppermute | solution.py:38
  80.9 8.4 %collective-permute-start.12 = (bf16[128,768]{1,0:T(8,128)(2,1)S(1)}, bf16[128,768]{1,0:T(8,128)(2,1)S(1)}, u32[]{:S(2)}, u32[]{:S(2)}) collective-permute-start(bf16[128,768]{1,0:T(8,128)(2,1)S(1)} %collective-permute-done.11.refs_0_), channel_id=1, source_target_pairs={{0,32},{16,48},{32,64},{48,80},{64,96},{80,112},{96,128},{112,144}... | collective-permute-start | bytes 589832 | tf_op jit(solution)/shard_map/ppermute | solution.py:38
  82.8 8.3 %collective-permute-start.14 = (bf16[128,768]{1,0:T(8,128)(2,1)S(1)}, bf16[128,768]{1,0:T(8,128)(2,1)S(1)}, u32[]{:S(2)}, u32[]{:S(2)}) collective-permute-start(bf16[128,768]{1,0:T(8,128)(2,1)S(1)} %collective-permute-done.13.refs_1_), channel_id=1, source_target_pairs={{0,480},{16,496},{32,0},{48,16},{64,32},{80,48},{96,64},{112,80},{... | collective-permute-start | bytes 589832 | tf_op jit(solution)/shard_map/ppermute | solution.py:38
  92.9 8.1 %collective-permute-start.15 = (bf16[128,768]{1,0:T(8,128)(2,1)S(1)}, bf16[128,768]{1,0:T(8,128)(2,1)S(1)}, u32[]{:S(2)}, u32[]{:S(2)}) collective-permute-start(bf16[128,768]{1,0:T(8,128)(2,1)S(1)} %collective-permute-done.12.refs_2_), channel_id=1, source_target_pairs={{0,32},{16,48},{32,64},{48,80},{64,96},{80,112},{96,128},{112,144}... | collective-permute-start | bytes 589832 | tf_op jit(solution)/shard_map/ppermute | solution.py:38
  101.7 50.3 %copy-start.9 = (f32[2]{0:T(128)S(1)}, f32[2]{0:T(128)}, u32[]{:S(2)}) copy-start(f32[2]{0:T(128)} %skip_ref.1) | copy-start | bytes 28
  101.7 13.1 %collective-permute-start.16 = (f32[256,768]{1,0:T(8,128)S(1)}, f32[256,768]{1,0:T(8,128)S(1)}, u32[]{:S(2)}, u32[]{:S(2)}) collective-permute-start(f32[256,768]{1,0:T(8,128)S(1)} %get-tuple-element.43), channel_id=1, source_target_pairs={{0,16},{16,0},{32,48},{48,32},{64,80},{80,64},{96,112},{112,96},{1... | collective-permute-start | bytes 2359304 | tf_op jit(solution)/shard_map/ppermute | solution.py:42
  115.2 3.2 %collective-permute-start.17 = (f32[136,128]{1,0:T(8,128)S(1)}, f32[136,128]{1,0:T(8,128)S(1)}, u32[]{:S(2)}, u32[]{:S(2)}) collective-permute-start(f32[136,128]{1,0:T(8,128)S(1)} %get-tuple-element.50), channel_id=1, source_target_pairs={{0,16},{16,0},{32,48},{48,32},{64,80},{80,64},{96,112},{112,96},{1... | collective-permute-start | bytes 208904 | tf_op jit(solution)/shard_map/ppermute | solution.py:42
  142.7 24.1 %copy-start.7 = (f32[2,128]{1,0:T(2,128)S(1)}, f32[2,128]{1,0:T(2,128)}, u32[]{:S(2)}) copy-start(f32[2,128]{1,0:T(2,128)} %param.10) | copy-start | bytes 3076
  142.8 10.2 %collective-permute-start.18 = (f32[128,128]{1,0:T(8,128)S(1)}, f32[128,128]{1,0:T(8,128)S(1)}, u32[]{:S(2)}, u32[]{:S(2)}) collective-permute-start(f32[128,128]{1,0:T(8,128)S(1)} %get-tuple-element.54), channel_id=1, source_target_pairs={{0,16},{16,0},{32,48},{48,32},{64,80},{80,64},{96,112},{112,96},{1... | collective-permute-start | bytes 196616 | tf_op jit(solution)/shard_map/ppermute | solution.py:42
  (8 other events, 12.7 us)

commit v5 on v4

--- a/solution.py
+++ b/solution.py
@@ -71,22 +71,15 @@
 
 
 def partial_kernel(steps, with_acc, chip_ref, tok_ref, *refs):
-    count = len(steps)
-    blocks, outs, held, sem = refs[:count], refs[count + with_acc : -2], refs[-2], refs[-1]
-    copies = [
-        pltpu.make_async_copy(block, held.at[at], sem.at[at]) for at, block in enumerate(blocks)
-    ]
-    for copy in copies:
-        copy.start()
+    blocks, outs = refs[: len(steps)], refs[len(steps) + with_acc :]
     n_chip, rows = tok_ref.shape[0], tok_ref.shape[1]
     chip = chip_ref[0]
-    acc = refs[count][...] if with_acc else jnp.zeros((rows, held.shape[2]), F32)
-    for at in range(0, count, 2):
-        part = range(at, min(at + 2, count))
-        for p in part:
-            copies[p].wait()
-        toks = [tok_ref[lax.rem(chip - steps[p] + 2 * n_chip, n_chip)] for p in part]
-        ws = [held[p] for p in part]
+    acc = refs[len(steps)][...] if with_acc else jnp.zeros((rows, blocks[0].shape[1]), F32)
+    order = list(zip(steps, blocks))
+    for at in range(0, len(order), 2):
+        part = order[at : at + 2]
+        toks = [tok_ref[lax.rem(chip - s + 2 * n_chip, n_chip)] for s, _ in part]
+        ws = [w[...] for _, w in part]
         tok = jnp.concatenate(toks, axis=1) if len(part) > 1 else toks[0]
         w = jnp.concatenate(ws, axis=0) if len(part) > 1 else ws[0]
         acc += jnp.dot(tok, w, preferred_element_type=F32)
@@ -99,18 +92,16 @@
 
 def partial_product(n_out, steps, chip, tok, blocks, acc):
     shape = (tok.shape[1] // n_out, blocks[0].shape[1])
-    count = len(steps)
-    return pl.pallas_call(
+    got = call(
         functools.partial(partial_kernel, steps, len(acc)),
-        out_shape=[jax.ShapeDtypeStruct(shape, F32)] * n_out,
-        in_specs=[SMEM, VMEM] + [pl.BlockSpec(memory_space=pltpu.HBM)] * count + [VMEM] * len(acc),
-        out_specs=[VMEM] * n_out,
-        scratch_shapes=[
-            pltpu.VMEM((count,) + blocks[0].shape, BF16),
-            pltpu.SemaphoreType.DMA((count,)),
-        ],
-        compiler_params=PARAMS,
-    )(chip, tok, *blocks, *acc)
+        [(shape, F32)] * n_out,
+        chip,
+        tok,
+        *blocks,
+        *acc,
+        smem=1,
+    )
+    return [got] if n_out == 1 else got
 
 
 def local_kernel(core_ref, own_ref, got_ref, cols_ref, ends_ref, val_ref, maps_ref, keep_ref, send_ref):
@@ -233,11 +224,6 @@
     def mine_other(a, b):
         return jnp.where(core == 0, a, b), jnp.where(core == 0, b, a)
 
-    tok_mine, tok_other = mine_other(tokens[:, :depth], tokens[:, depth:])
-    tok = jnp.concatenate([tok_mine, swap_cores(tok_other)], axis=0)
-    copies = jnp.broadcast_to(tok[None], (n_fsdp,) + tok.shape)
-    tok = lax.all_to_all(copies, "fsdp", 0, 0)
-
     block = jnp.concatenate(
         [w_xz[:, :, :width].reshape(depth, -1), w_bc, w_xz[:, :, width:].reshape(depth, -1)], axis=1
     )
@@ -248,16 +234,16 @@
         decays,
         boundaries.reshape(1, rows),
     )
+    half = n_chip // 2
+    early = half - 3
     up = down = block
     steps, blocks, acc = [0], [block], ()
-    half = n_chip // 2
     for s in range(1, half + 1):
-        if s in (half - 2, half):
-            product = partial_product(1, steps, chip_1, tok, blocks, acc)[0]
-            up, down, product, cols, decay, ends = lax.optimization_barrier(
-                (up, down, product, cols, decay, ends)
+        if s == half:
+            up, product, cols, decay, ends = lax.optimization_barrier(
+                (up, product, cols, decay, ends)
             )
-            steps, blocks, acc = [], [], (product,)
+            acc = (product,)
         up = shift(up, 2)
         steps.append(s)
         blocks.append(up)
@@ -265,6 +251,15 @@
             down = shift(down, -2)
             steps.append(-s)
             blocks.append(down)
+        if s == 1:
+            up, tokens = lax.optimization_barrier((up, tokens))
+            tok_mine, tok_other = mine_other(tokens[:, :depth], tokens[:, depth:])
+            tok = jnp.concatenate([tok_mine, swap_cores(tok_other)], axis=0)
+            copies = jnp.broadcast_to(tok[None], (n_fsdp,) + tok.shape)
+            tok = lax.all_to_all(copies, "fsdp", 0, 0)
+        if s == early:
+            product = partial_product(1, steps, chip_1, tok, blocks, acc)[0]
+            steps, blocks = [], []
     own, other = partial_product(2, steps, chip_1, tok, blocks, acc)
     got = swap_cores(other)
 

time: 169 us -> 165 us (0.976)
  starting transfers between devices: 89.1 us -> 80.4 us
  local copies, waits for them, and re-layouts: 7.49 us -> 14 us
  waiting for transfers between devices: 22.6 us -> 25.4 us
  blocking collectives: 37.5 us -> 35.2 us
  Pallas kernels: 9.91 us -> 7.72 us
    ppermute x4, starting transfers between devices: 31.5 us -> 24.1 us  [swap_cores(): lax.ppermute(x, 'ctx', [(i, i ^ 1) for i in range(lax.axis_size('ctx'))])]
    pallas_call x3 -> x0, Pallas kernels: 6.49 us -> none  [partial_product(): pl.pallas_call(functools.partial(partial_kernel, steps, len(acc)), out_sh...]
    unnamed x27 -> x35, local copies, waits for them, and re-layouts: 4.85 us -> 10.5 us
    ppermute x15, starting transfers between devices: 53.8 us -> 49.4 us  [shift(): return lax.ppermute(x, 'ctx', [(i, (i + by) % n) for i in range(n)])]
    pallas_call x7 -> x9, Pallas kernels: 3.42 us -> 7.72 us  [call(): pl.pallas_call(kernel, out_shape=shapes, in_specs=[SMEM] * smem + [VMEM]...]
    all_to_all x1, starting transfers between devices: 3.86 us -> 6.89 us  [per_device(): tok = lax.all_to_all(copies, 'fsdp', 0, 0)]
    ppermute x15, waiting for transfers between devices: 18.9 us -> 21.7 us  [shift(): return lax.ppermute(x, 'ctx', [(i, (i + by) % n) for i in range(n)])]
    all_gather x1, blocking collectives: 24.3 us -> 22.5 us  [per_device(): lax.all_gather(packed, 'ctx', axis=0, axis_index_groups=same_core)]
  transfers between devices with their start and end apart: 20 -> 20, of which waited for: 11 -> 8; matrix products, arithmetic and copies ran while one was open for 0% -> 0% of each run, Pallas kernels for 1% -> 3%
where the time goes in v5:
time: 165 us; the launch traced here: 164 us
  starting transfers between devices  80.4 us (49%)
  blocking collectives  35.2 us (21%)
  waiting for transfers between devices  25.4 us (15%)
  local copies, waits for them, and re-layouts  14 us (8%)
  Pallas kernels  7.72 us (5%)
    ppermute x15, starting transfers between devices, shift(): return lax.ppermute(x, 'ctx', [(i, (i + by) % n) for i in range(n)])  49.4 us
    ppermute x4, starting transfers between devices, swap_cores(): lax.ppermute(x, 'ctx', [(i, i ^ 1) for i in range(lax.axis_size('ctx'))])  24.1 us
    all_gather x1, blocking collectives, per_device(): lax.all_gather(packed, 'ctx', axis=0, axis_index_groups=same_core)  22.5 us
    ppermute x15, waiting for transfers between devices, shift(): return lax.ppermute(x, 'ctx', [(i, (i + by) % n) for i in range(n)])  21.7 us
    all_to_all x1, blocking collectives, per_device(): sums = lax.all_to_all(sums, 'fsdp', 0, 0, tiled=True)  12.7 us
    unnamed x35, local copies, waits for them, and re-layouts  10.5 us
    pallas_call x9, Pallas kernels, call(): pl.pallas_call(kernel, out_shape=shapes, in_specs=[SMEM] * smem + [VMEM]...  7.72 us
    all_to_all x1, starting transfers between devices, per_device(): tok = lax.all_to_all(copies, 'fsdp', 0, 0)  6.89 us
  transfers between devices with their start and end apart: 20, of which 8 were waited for; matrix products, arithmetic and copies ran while one was open for 0% of the time, Pallas kernels for 3%

profile of v5, /device:TPU:1, one launch (start us, length us, event | category | flops | bytes accessed | tf_op | source)
XLA Modules:
  0.0 164.0 jit_solution(16213557384042035648)
XLA Ops:
  1.8 4.4 %collective-permute-start = (bf16[128,768]{1,0:T(8,128)(2,1)S(1)}, bf16[128,768]{1,0:T(8,128)(2,1)S(1)}, u32[]{:S(2)}, u32[]{:S(2)}) collective-permute-start(bf16[128,768]{1,0:T(8,128)(2,1)S(1)} %bitcast_dynamic-update-slice_fusion.refs_0_), channel_id=1, source_target_pairs={{0,32},{16,48},{32,64},{48,80},{64,96},{80,112},{96,128},{112,144}... | collective-permute-start | bytes 589832 | tf_op jit(solution)/shard_map/ppermute | solution.py:38
  6.2 12.2 %collective-permute-done.refs_1_ = bf16[128,768]{1,0:T(8,128)(2,1)S(1)} collective-permute-done((bf16[128,768]{1,0:T(8,128)(2,1)S(1)}, bf16[128,768]{1,0:T(8,128)(2,1)S(1)}, u32[]{:S(2)}, u32[]{:S(2)}) %collective-permute-start) | collective-permute-done | bytes 196640 | tf_op jit(solution)/shard_map/ppermute | solution.py:38
  19.3 3.1 %collective-permute-start.1 = (bf16[256,128]{1,0:T(8,128)(2,1)S(1)}, bf16[256,128]{1,0:T(8,128)(2,1)S(1)}, u32[]{:S(2)}, u32[]{:S(2)}) collective-permute-start(bf16[256,128]{1,0:T(8,128)(2,1)S(1)} %get-tuple-element.50), channel_id=1, source_target_pairs={{0,16},{16,0},{32,48},{48,32},{64,80},{80,64},{96,112},{112,96},{1... | collective-permute-start | bytes 196616 | tf_op jit(solution)/shard_map/ppermute | solution.py:42
  25.1 6.9 %all-to-all-start = ((bf16[16,512,128]{2,1,0:T(8,128)(2,1)}), bf16[16,512,128]{2,1,0:T(8,128)(2,1)S(1)}, u32[]{:S(2)}, u32[]{:S(2)}) async-start(bf16[16,512,128]{2,1,0:T(8,128)(2,1)} %broadcast_in_dim.2), calls=%async_computation | async-start | bytes 4194304 | tf_op jit(solution)/shard_map/all_to_all | solution.py:259
  32.0 3.4 %collective-permute-start.7 = (bf16[128,768]{1,0:T(8,128)(2,1)S(1)}, bf16[128,768]{1,0:T(8,128)(2,1)S(1)}, u32[]{:S(2)}, u32[]{:S(2)}) collective-permute-start(bf16[128,768]{1,0:T(8,128)(2,1)S(1)} %bitcast_dynamic-update-slice_fusion.refs_0_), channel_id=1, source_target_pairs={{0,480},{16,496},{32,0},{48,16},{64,32},{80,48},{96,64},{112,80},{... | collective-permute-start | bytes 589832 | tf_op jit(solution)/shard_map/ppermute | solution.py:38
  35.4 1.9 %collective-permute-start.2 = (bf16[128,768]{1,0:T(8,128)(2,1)S(1)}, bf16[128,768]{1,0:T(8,128)(2,1)S(1)}, u32[]{:S(2)}, u32[]{:S(2)}) collective-permute-start(bf16[128,768]{1,0:T(8,128)(2,1)S(1)} %collective-permute-done.refs_1_), channel_id=1, source_target_pairs={{0,32},{16,48},{32,64},{48,80},{64,96},{80,112},{96,128},{112,144}... | collective-permute-start | bytes 589832 | tf_op jit(solution)/shard_map/ppermute | solution.py:38
  37.3 2.4 %collective-permute-done.7.refs_2_ = bf16[128,768]{1,0:T(8,128)(2,1)S(1)} collective-permute-done((bf16[128,768]{1,0:T(8,128)(2,1)S(1)}, bf16[128,768]{1,0:T(8,128)(2,1)S(1)}, u32[]{:S(2)}, u32[]{:S(2)}) %collective-permute-start.7) | collective-permute-done | bytes 196640 | tf_op jit(solution)/shard_map/ppermute | solution.py:38
  39.7 4.6 %collective-permute-start.8 = (bf16[128,768]{1,0:T(8,128)(2,1)S(1)}, bf16[128,768]{1,0:T(8,128)(2,1)S(1)}, u32[]{:S(2)}, u32[]{:S(2)}) collective-permute-start(bf16[128,768]{1,0:T(8,128)(2,1)S(1)} %collective-permute-done.7.refs_2_), channel_id=1, source_target_pairs={{0,480},{16,496},{32,0},{48,16},{64,32},{80,48},{96,64},{112,80},{... | collective-permute-start | bytes 589832 | tf_op jit(solution)/shard_map/ppermute | solution.py:38
  44.3 1.9 %collective-permute-start.3 = (bf16[128,768]{1,0:T(8,128)(2,1)S(1)}, bf16[128,768]{1,0:T(8,128)(2,1)S(1)}, u32[]{:S(2)}, u32[]{:S(2)}) collective-permute-start(bf16[128,768]{1,0:T(8,128)(2,1)S(1)} %collective-permute-done.2.refs_3_), channel_id=1, source_target_pairs={{0,32},{16,48},{32,64},{48,80},{64,96},{80,112},{96,128},{112,144}... | collective-permute-start | bytes 589832 | tf_op jit(solution)/shard_map/ppermute | solution.py:38
  46.9 5.4 %collective-permute-start.9 = (bf16[128,768]{1,0:T(8,128)(2,1)S(1)}, bf16[128,768]{1,0:T(8,128)(2,1)S(1)}, u32[]{:S(2)}, u32[]{:S(2)}) collective-permute-start(bf16[128,768]{1,0:T(8,128)(2,1)S(1)} %collective-permute-done.8.refs_4_), channel_id=1, source_target_pairs={{0,480},{16,496},{32,0},{48,16},{64,32},{80,48},{96,64},{112,80},{... | collective-permute-start | bytes 589832 | tf_op jit(solution)/shard_map/ppermute | solution.py:38
  55.5 4.6 %collective-permute-start.10 = (bf16[128,768]{1,0:T(8,128)(2,1)S(1)}, bf16[128,768]{1,0:T(8,128)(2,1)S(1)}, u32[]{:S(2)}, u32[]{:S(2)}) collective-permute-start(bf16[128,768]{1,0:T(8,128)(2,1)S(1)} %collective-permute-done.9.refs_6_), channel_id=1, source_target_pairs={{0,480},{16,496},{32,0},{48,16},{64,32},{80,48},{96,64},{112,80},{... | collective-permute-start | bytes 589832 | tf_op jit(solution)/shard_map/ppermute | solution.py:38
  63.5 4.6 %collective-permute-start.11 = (bf16[128,768]{1,0:T(8,128)(2,1)S(1)}, bf16[128,768]{1,0:T(8,128)(2,1)}, u32[]{:S(2)}, u32[]{:S(2)}) collective-permute-start(bf16[128,768]{1,0:T(8,128)(2,1)S(1)} %collective-permute-done.10.refs_8_), channel_id=1, source_target_pairs={{0,480},{16,496},{32,0},{48,16},{64,32},{80,48},{96,64},{112,80},{... | collective-permute-start | bytes 589832 | tf_op jit(solution)/shard_map/ppermute | solution.py:38
  68.7 1.9 %collective-permute-start.6 = (bf16[128,768]{1,0:T(8,128)(2,1)S(1)}, bf16[128,768]{1,0:T(8,128)(2,1)}, u32[]{:S(2)}, u32[]{:S(2)}) collective-permute-start(bf16[128,768]{1,0:T(8,128)(2,1)S(1)} %collective-permute-done.5.refs_9_), channel_id=1, source_target_pairs={{0,32},{16,48},{32,64},{48,80},{64,96},{80,112},{96,128},{112,144}... | collective-permute-start | bytes 589832 | tf_op jit(solution)/shard_map/ppermute | solution.py:38
  71.3 4.6 %collective-permute-start.12 = (bf16[128,768]{1,0:T(8,128)(2,1)}, bf16[128,768]{1,0:T(8,128)(2,1)}, u32[]{:S(2)}, u32[]{:S(2)}) collective-permute-start(bf16[128,768]{1,0:T(8,128)(2,1)} %collective-permute-done.11.refs_10_), channel_id=1, source_target_pairs={{0,480},{16,496},{32,0},{48,16},{64,32},{80,48},{96,64},{112,80},{... | collective-permute-start | bytes 589832 | tf_op jit(solution)/shard_map/ppermute | solution.py:38
  79.5 4.6 %collective-permute-start.14 = (bf16[128,768]{1,0:T(8,128)(2,1)}, bf16[128,768]{1,0:T(8,128)(2,1)}, u32[]{:S(2)}, u32[]{:S(2)}) collective-permute-start(bf16[128,768]{1,0:T(8,128)(2,1)} %collective-permute-done.12.refs_1_), channel_id=1, source_target_pairs={{0,480},{16,496},{32,0},{48,16},{64,32},{80,48},{96,64},{112,80},{... | collective-permute-start | bytes 589832 | tf_op jit(solution)/shard_map/ppermute | solution.py:38
  89.7 2.3 %shard_map.73.refs_5_ = f32[512,768]{1,0:T(8,128)S(1)} custom-call(s32[1]{0:T(128)} %bitcast.1.chip_ref, bf16[16,512,128]{2,1,0:T(8,128)(2,1)S(1)} %all-to-all-done.tok_ref, bf16[128,768]{1,0:T(8,128)(2,1)S(1)} %bitcast_dynamic-update-slice_fusion.refs_0_, bf16[128,768]{1,0:T(8,128)(2,1)S(1)} %collective-permute-done.refs_1_, ...), custom_call_target="tpu_custom_call" | custom-call | tf_op jit(solution)/shard_map/pallas_call | solution.py:22
  92.0 1.9 %collective-permute-start.15 = (bf16[128,768]{1,0:T(8,128)(2,1)}, bf16[128,768]{1,0:T(8,128)(2,1)S(1)}, u32[]{:S(2)}, u32[]{:S(2)}) collective-permute-start(bf16[128,768]{1,0:T(8,128)(2,1)} %collective-permute-done.13.refs_2_), channel_id=1, source_target_pairs={{0,32},{16,48},{32,64},{48,80},{64,96},{80,112},{96,128},{112,144}... | collective-permute-start | bytes 589832 | tf_op jit(solution)/shard_map/ppermute | solution.py:38
  93.9 5.9 %collective-permute-done.15.refs_4_ = bf16[128,768]{1,0:T(8,128)(2,1)S(1)} collective-permute-done((bf16[128,768]{1,0:T(8,128)(2,1)}, bf16[128,768]{1,0:T(8,128)(2,1)S(1)}, u32[]{:S(2)}, u32[]{:S(2)}) %collective-permute-start.15) | collective-permute-done | bytes 196640 | tf_op jit(solution)/shard_map/ppermute | solution.py:38
  99.8 2.0 %shard_map.75 = (f32[256,768]{1,0:T(8,128)S(1)}, f32[256,768]{1,0:T(8,128)S(1)}) custom-call(s32[1]{0:T(128)} %bitcast.1.chip_ref, bf16[16,512,128]{2,1,0:T(8,128)(2,1)S(1)} %all-to-all-done.tok_ref, bf16[128,768]{1,0:T(8,128)(2,1)} %collective-permute-done.6.refs_0_, bf16[128,768]{1,0:T(8,128)(2,1)} %collective-permute-done.12.refs_1_, ...), custom_call_target="tpu_custom_call" | custom-call | tf_op jit(solution)/shard_map/pallas_call | solution.py:22
  101.8 9.4 %collective-permute-start.16 = (f32[256,768]{1,0:T(8,128)S(1)}, f32[256,768]{1,0:T(8,128)S(1)}, u32[]{:S(2)}, u32[]{:S(2)}) collective-permute-start(f32[256,768]{1,0:T(8,128)S(1)} %get-tuple-element.35), channel_id=1, source_target_pairs={{0,16},{16,0},{32,48},{48,32},{64,80},{80,64},{96,112},{112,96},{1... | collective-permute-start | bytes 2359304 | tf_op jit(solution)/shard_map/ppermute | solution.py:42
  113.5 2.3 %collective-permute-start.17 = (f32[136,128]{1,0:T(8,128)S(1)}, f32[136,128]{1,0:T(8,128)S(1)}, u32[]{:S(2)}, u32[]{:S(2)}) collective-permute-start(f32[136,128]{1,0:T(8,128)S(1)} %get-tuple-element.42), channel_id=1, source_target_pairs={{0,16},{16,0},{32,48},{48,32},{64,80},{80,64},{96,112},{112,96},{1... | collective-permute-start | bytes 208904 | tf_op jit(solution)/shard_map/ppermute | solution.py:42
  116.7 22.5 %all-gather = bf16[2304,128]{1,0:T(8,128)(2,1)S(1)} all-gather(bf16[144,128]{1,0:T(8,128)(2,1)S(1)} %get-tuple-element.43), channel_id=2, replica_groups={{0,32,64,96,128,160,192,224,256,288,320,352,384,416,448,480},{16,48,80,..., dimensions={0}, use_global_device_ids=true | all-gather | bytes 626688 | tf_op jit(solution)/shard_map/all_gather | solution.py:282
  139.4 9.2 %collective-permute-start.18 = (f32[128,128]{1,0:T(8,128)S(1)}, f32[128,128]{1,0:T(8,128)S(1)}, u32[]{:S(2)}, u32[]{:S(2)}) collective-permute-start(f32[128,128]{1,0:T(8,128)S(1)} %get-tuple-element.46), channel_id=1, source_target_pairs={{0,16},{16,0},{32,48},{48,32},{64,80},{80,64},{96,112},{112,96},{1... | collective-permute-start | bytes 196616 | tf_op jit(solution)/shard_map/ppermute | solution.py:42
  150.1 12.7 %all_to_all.16 = f32[16,1,256]{2,1,0:T(1,128)S(1)} all-to-all(f32[16,1,256]{2,1,0:T(1,128)S(1)} %copy.8), channel_id=1, replica_groups=mesh['ctx'=32,'fsdp'=16] {'fsdp'}, dimensions={0} | all-to-all | bytes 32768 | tf_op jit(solution)/shard_map/all_to_all | solution.py:307
  (69 shorter events, 28.9 us)
Async XLA Ops:
  1.8 16.6 %collective-permute-start = (bf16[128,768]{1,0:T(8,128)(2,1)S(1)}, bf16[128,768]{1,0:T(8,128)(2,1)S(1)}, u32[]{:S(2)}, u32[]{:S(2)}) collective-permute-start(bf16[128,768]{1,0:T(8,128)(2,1)S(1)} %bitcast_dynamic-update-slice_fusion.refs_0_), channel_id=1, source_target_pairs={{0,32},{16,48},{32,64},{48,80},{64,96},{80,112},{96,128},{112,144}... | collective-permute-start | bytes 589832 | tf_op jit(solution)/shard_map/ppermute | solution.py:38
  19.3 4.0 %collective-permute-start.1 = (bf16[256,128]{1,0:T(8,128)(2,1)S(1)}, bf16[256,128]{1,0:T(8,128)(2,1)S(1)}, u32[]{:S(2)}, u32[]{:S(2)}) collective-permute-start(bf16[256,128]{1,0:T(8,128)(2,1)S(1)} %get-tuple-element.50), channel_id=1, source_target_pairs={{0,16},{16,0},{32,48},{48,32},{64,80},{80,64},{96,112},{112,96},{1... | collective-permute-start | bytes 196616 | tf_op jit(solution)/shard_map/ppermute | solution.py:42
  25.1 53.3 %copy-start.12 = (f32[2,256]{1,0:T(2,128)S(1)}, f32[2,256]{1,0:T(2,128)}, u32[]{:S(2)}) copy-start(f32[2,256]{1,0:T(2,128)} %decays_ref.1) | copy-start | bytes 6148
  25.1 53.3 %copy-start.14 = (s32[256]{0:T(256)S(1)}, s32[256]{0:T(256)}, u32[]{:S(2)}) copy-start(s32[256]{0:T(256)} %param.13) | copy-start | bytes 3076
  25.1 59.0 %all-to-all-start = ((bf16[16,512,128]{2,1,0:T(8,128)(2,1)}), bf16[16,512,128]{2,1,0:T(8,128)(2,1)S(1)}, u32[]{:S(2)}, u32[]{:S(2)}) async-start(bf16[16,512,128]{2,1,0:T(8,128)(2,1)} %broadcast_in_dim.2), calls=%async_computation | async-start | bytes 4194304 | tf_op jit(solution)/shard_map/all_to_all | solution.py:259
  32.0 7.7 %collective-permute-start.7 = (bf16[128,768]{1,0:T(8,128)(2,1)S(1)}, bf16[128,768]{1,0:T(8,128)(2,1)S(1)}, u32[]{:S(2)}, u32[]{:S(2)}) collective-permute-start(bf16[128,768]{1,0:T(8,128)(2,1)S(1)} %bitcast_dynamic-update-slice_fusion.refs_0_), channel_id=1, source_target_pairs={{0,480},{16,496},{32,0},{48,16},{64,32},{80,48},{96,64},{112,80},{... | collective-permute-start | bytes 589832 | tf_op jit(solution)/shard_map/ppermute | solution.py:38
  35.4 8.9 %collective-permute-start.2 = (bf16[128,768]{1,0:T(8,128)(2,1)S(1)}, bf16[128,768]{1,0:T(8,128)(2,1)S(1)}, u32[]{:S(2)}, u32[]{:S(2)}) collective-permute-start(bf16[128,768]{1,0:T(8,128)(2,1)S(1)} %collective-permute-done.refs_1_), channel_id=1, source_target_pairs={{0,32},{16,48},{32,64},{48,80},{64,96},{80,112},{96,128},{112,144}... | collective-permute-start | bytes 589832 | tf_op jit(solution)/shard_map/ppermute | solution.py:38
  39.7 7.2 %collective-permute-start.8 = (bf16[128,768]{1,0:T(8,128)(2,1)S(1)}, bf16[128,768]{1,0:T(8,128)(2,1)S(1)}, u32[]{:S(2)}, u32[]{:S(2)}) collective-permute-start(bf16[128,768]{1,0:T(8,128)(2,1)S(1)} %collective-permute-done.7.refs_2_), channel_id=1, source_target_pairs={{0,480},{16,496},{32,0},{48,16},{64,32},{80,48},{96,64},{112,80},{... | collective-permute-start | bytes 589832 | tf_op jit(solution)/shard_map/ppermute | solution.py:38
  44.3 8.6 %collective-permute-start.3 = (bf16[128,768]{1,0:T(8,128)(2,1)S(1)}, bf16[128,768]{1,0:T(8,128)(2,1)S(1)}, u32[]{:S(2)}, u32[]{:S(2)}) collective-permute-start(bf16[128,768]{1,0:T(8,128)(2,1)S(1)} %collective-permute-done.2.refs_3_), channel_id=1, source_target_pairs={{0,32},{16,48},{32,64},{48,80},{64,96},{80,112},{96,128},{112,144}... | collective-permute-start | bytes 589832 | tf_op jit(solution)/shard_map/ppermute | solution.py:38
  46.9 8.7 %collective-permute-start.9 = (bf16[128,768]{1,0:T(8,128)(2,1)S(1)}, bf16[128,768]{1,0:T(8,128)(2,1)S(1)}, u32[]{:S(2)}, u32[]{:S(2)}) collective-permute-start(bf16[128,768]{1,0:T(8,128)(2,1)S(1)} %collective-permute-done.8.refs_4_), channel_id=1, source_target_pairs={{0,480},{16,496},{32,0},{48,16},{64,32},{80,48},{96,64},{112,80},{... | collective-permute-start | bytes 589832 | tf_op jit(solution)/shard_map/ppermute | solution.py:38
  52.9 7.9 %collective-permute-start.4 = (bf16[128,768]{1,0:T(8,128)(2,1)S(1)}, bf16[128,768]{1,0:T(8,128)(2,1)S(1)}, u32[]{:S(2)}, u32[]{:S(2)}) collective-permute-start(bf16[128,768]{1,0:T(8,128)(2,1)S(1)} %collective-permute-done.3.refs_5_), channel_id=1, source_target_pairs={{0,32},{16,48},{32,64},{48,80},{64,96},{80,112},{96,128},{112,144}... | collective-permute-start | bytes 589832 | tf_op jit(solution)/shard_map/ppermute | solution.py:38
  55.5 7.9 %collective-permute-start.10 = (bf16[128,768]{1,0:T(8,128)(2,1)S(1)}, bf16[128,768]{1,0:T(8,128)(2,1)S(1)}, u32[]{:S(2)}, u32[]{:S(2)}) collective-permute-start(bf16[128,768]{1,0:T(8,128)(2,1)S(1)} %collective-permute-done.9.refs_6_), channel_id=1, source_target_pairs={{0,480},{16,496},{32,0},{48,16},{64,32},{80,48},{96,64},{112,80},{... | collective-permute-start | bytes 589832 | tf_op jit(solution)/shard_map/ppermute | solution.py:38
  60.9 7.9 %collective-permute-start.5 = (bf16[128,768]{1,0:T(8,128)(2,1)S(1)}, bf16[128,768]{1,0:T(8,128)(2,1)S(1)}, u32[]{:S(2)}, u32[]{:S(2)}) collective-permute-start(bf16[128,768]{1,0:T(8,128)(2,1)S(1)} %collective-permute-done.4.refs_7_), channel_id=1, source_target_pairs={{0,32},{16,48},{32,64},{48,80},{64,96},{80,112},{96,128},{112,144}... | collective-permute-start | bytes 589832 | tf_op jit(solution)/shard_map/ppermute | solution.py:38
  63.5 7.9 %collective-permute-start.11 = (bf16[128,768]{1,0:T(8,128)(2,1)S(1)}, bf16[128,768]{1,0:T(8,128)(2,1)}, u32[]{:S(2)}, u32[]{:S(2)}) collective-permute-start(bf16[128,768]{1,0:T(8,128)(2,1)S(1)} %collective-permute-done.10.refs_8_), channel_id=1, source_target_pairs={{0,480},{16,496},{32,0},{48,16},{64,32},{80,48},{96,64},{112,80},{... | collective-permute-start | bytes 589832 | tf_op jit(solution)/shard_map/ppermute | solution.py:38
  68.7 7.7 %collective-permute-start.6 = (bf16[128,768]{1,0:T(8,128)(2,1)S(1)}, bf16[128,768]{1,0:T(8,128)(2,1)}, u32[]{:S(2)}, u32[]{:S(2)}) collective-permute-start(bf16[128,768]{1,0:T(8,128)(2,1)S(1)} %collective-permute-done.5.refs_9_), channel_id=1, source_target_pairs={{0,32},{16,48},{32,64},{48,80},{64,96},{80,112},{96,128},{112,144}... | collective-permute-start | bytes 589832 | tf_op jit(solution)/shard_map/ppermute | solution.py:38
  71.3 8.2 %collective-permute-start.12 = (bf16[128,768]{1,0:T(8,128)(2,1)}, bf16[128,768]{1,0:T(8,128)(2,1)}, u32[]{:S(2)}, u32[]{:S(2)}) collective-permute-start(bf16[128,768]{1,0:T(8,128)(2,1)} %collective-permute-done.11.refs_10_), channel_id=1, source_target_pairs={{0,480},{16,496},{32,0},{48,16},{64,32},{80,48},{96,64},{112,80},{... | collective-permute-start | bytes 589832 | tf_op jit(solution)/shard_map/ppermute | solution.py:38
  76.4 15.5 %collective-permute-start.13 = (bf16[128,768]{1,0:T(8,128)(2,1)}, bf16[128,768]{1,0:T(8,128)(2,1)}, u32[]{:S(2)}, u32[]{:S(2)}) collective-permute-start(bf16[128,768]{1,0:T(8,128)(2,1)} %collective-permute-done.6.refs_0_), channel_id=1, source_target_pairs={{0,32},{16,48},{32,64},{48,80},{64,96},{80,112},{96,128},{112,144}... | collective-permute-start | bytes 589832 | tf_op jit(solution)/shard_map/ppermute | solution.py:38
  79.5 14.4 %collective-permute-start.14 = (bf16[128,768]{1,0:T(8,128)(2,1)}, bf16[128,768]{1,0:T(8,128)(2,1)}, u32[]{:S(2)}, u32[]{:S(2)}) collective-permute-start(bf16[128,768]{1,0:T(8,128)(2,1)} %collective-permute-done.12.refs_1_), channel_id=1, source_target_pairs={{0,480},{16,496},{32,0},{48,16},{64,32},{80,48},{96,64},{112,80},{... | collective-permute-start | bytes 589832 | tf_op jit(solution)/shard_map/ppermute | solution.py:38
  92.0 7.8 %collective-permute-start.15 = (bf16[128,768]{1,0:T(8,128)(2,1)}, bf16[128,768]{1,0:T(8,128)(2,1)S(1)}, u32[]{:S(2)}, u32[]{:S(2)}) collective-permute-start(bf16[128,768]{1,0:T(8,128)(2,1)} %collective-permute-done.13.refs_2_), channel_id=1, source_target_pairs={{0,32},{16,48},{32,64},{48,80},{64,96},{80,112},{96,128},{112,144}... | collective-permute-start | bytes 589832 | tf_op jit(solution)/shard_map/ppermute | solution.py:38
  101.8 46.8 %copy-start.15 = (f32[2]{0:T(128)S(1)}, f32[2]{0:T(128)}, u32[]{:S(2)}) copy-start(f32[2]{0:T(128)} %skip_ref.1) | copy-start | bytes 28
  101.8 11.3 %collective-permute-start.16 = (f32[256,768]{1,0:T(8,128)S(1)}, f32[256,768]{1,0:T(8,128)S(1)}, u32[]{:S(2)}, u32[]{:S(2)}) collective-permute-start(f32[256,768]{1,0:T(8,128)S(1)} %get-tuple-element.35), channel_id=1, source_target_pairs={{0,16},{16,0},{32,48},{48,32},{64,80},{80,64},{96,112},{112,96},{1... | collective-permute-start | bytes 2359304 | tf_op jit(solution)/shard_map/ppermute | solution.py:42
  113.5 3.2 %collective-permute-start.17 = (f32[136,128]{1,0:T(8,128)S(1)}, f32[136,128]{1,0:T(8,128)S(1)}, u32[]{:S(2)}, u32[]{:S(2)}) collective-permute-start(f32[136,128]{1,0:T(8,128)S(1)} %get-tuple-element.42), channel_id=1, source_target_pairs={{0,16},{16,0},{32,48},{48,32},{64,80},{80,64},{96,112},{112,96},{1... | collective-permute-start | bytes 208904 | tf_op jit(solution)/shard_map/ppermute | solution.py:42
  139.2 23.7 %copy-start.13 = (f32[2,128]{1,0:T(2,128)S(1)}, f32[2,128]{1,0:T(2,128)}, u32[]{:S(2)}) copy-start(f32[2,128]{1,0:T(2,128)} %param.10) | copy-start | bytes 3076
  139.4 10.2 %collective-permute-start.18 = (f32[128,128]{1,0:T(8,128)S(1)}, f32[128,128]{1,0:T(8,128)S(1)}, u32[]{:S(2)}, u32[]{:S(2)}) collective-permute-start(f32[128,128]{1,0:T(8,128)S(1)} %get-tuple-element.46), channel_id=1, source_target_pairs={{0,16},{16,0},{32,48},{48,32},{64,80},{80,64},{96,112},{112,96},{1... | collective-permute-start | bytes 196616 | tf_op jit(solution)/shard_map/ppermute | solution.py:42
  (12 other events, 9.6 us)

commit v6 on v5

--- a/solution.py
+++ b/solution.py
@@ -224,6 +224,11 @@
     def mine_other(a, b):
         return jnp.where(core == 0, a, b), jnp.where(core == 0, b, a)
 
+    tok_mine, tok_other = mine_other(tokens[:, :depth], tokens[:, depth:])
+    tok = jnp.concatenate([tok_mine, swap_cores(tok_other)], axis=0)
+    copies = jnp.broadcast_to(tok[None], (n_fsdp,) + tok.shape)
+    tok = lax.all_to_all(copies, "fsdp", 0, 0)
+
     block = jnp.concatenate(
         [w_xz[:, :, :width].reshape(depth, -1), w_bc, w_xz[:, :, width:].reshape(depth, -1)], axis=1
     )
@@ -235,31 +240,19 @@
         boundaries.reshape(1, rows),
     )
     half = n_chip // 2
-    early = half - 3
     up = down = block
     steps, blocks, acc = [0], [block], ()
     for s in range(1, half + 1):
-        if s == half:
-            up, product, cols, decay, ends = lax.optimization_barrier(
-                (up, product, cols, decay, ends)
-            )
-            acc = (product,)
         up = shift(up, 2)
         steps.append(s)
         blocks.append(up)
+        if s == half - 2:
+            acc = partial_product(1, steps, chip_1, tok, blocks, acc)
+            steps, blocks = [], []
         if s < half:
             down = shift(down, -2)
             steps.append(-s)
             blocks.append(down)
-        if s == 1:
-            up, tokens = lax.optimization_barrier((up, tokens))
-            tok_mine, tok_other = mine_other(tokens[:, :depth], tokens[:, depth:])
-            tok = jnp.concatenate([tok_mine, swap_cores(tok_other)], axis=0)
-            copies = jnp.broadcast_to(tok[None], (n_fsdp,) + tok.shape)
-            tok = lax.all_to_all(copies, "fsdp", 0, 0)
-        if s == early:
-            product = partial_product(1, steps, chip_1, tok, blocks, acc)[0]
-            steps, blocks = [], []
     own, other = partial_product(2, steps, chip_1, tok, blocks, acc)
     got = swap_cores(other)
 

time: 165 us -> 154 us (0.933)
  waiting for transfers between devices: 25.4 us -> 9.62 us
  starting transfers between devices: 80.4 us -> 86 us
  local copies, waits for them, and re-layouts: 14 us -> 11.5 us
  blocking collectives: 35.2 us -> 37.5 us
    ppermute x15, waiting for transfers between devices: 21.7 us -> 7.95 us  [shift(): return lax.ppermute(x, 'ctx', [(i, (i + by) % n) for i in range(n)])]
    ppermute x4, starting transfers between devices: 24.1 us -> 30.3 us  [swap_cores(): lax.ppermute(x, 'ctx', [(i, i ^ 1) for i in range(lax.axis_size('ctx'))])]
    all_to_all x1, starting transfers between devices: 6.89 us -> 3.85 us  [per_device(): tok = lax.all_to_all(copies, 'fsdp', 0, 0)]
    unnamed x35 -> x33, local copies, waits for them, and re-layouts: 10.5 us -> 8 us
    ppermute x15, starting transfers between devices: 49.4 us -> 51.8 us  [shift(): return lax.ppermute(x, 'ctx', [(i, (i + by) % n) for i in range(n)])]
    ppermute x4, waiting for transfers between devices: 3.66 us -> 1.67 us  [swap_cores(): lax.ppermute(x, 'ctx', [(i, i ^ 1) for i in range(lax.axis_size('ctx'))])]
    all_gather x1, blocking collectives: 22.5 us -> 24.5 us  [per_device(): lax.all_gather(packed, 'ctx', axis=0, axis_index_groups=same_core)]
  transfers between devices with their start and end apart: 20 -> 20, of which waited for: 8 -> 8; matrix products, arithmetic and copies ran while one was open for 0% -> 1% of each run, Pallas kernels for 3% -> 2%
where the time goes in v6:
time: 154 us; the launch traced here: 153 us
  starting transfers between devices  86 us (56%)
  blocking collectives  37.5 us (24%)
  local copies, waits for them, and re-layouts  11.5 us (7%)
  waiting for transfers between devices  9.62 us (6%)
  Pallas kernels  6.6 us (4%)
    ppermute x15, starting transfers between devices, shift(): return lax.ppermute(x, 'ctx', [(i, (i + by) % n) for i in range(n)])  51.8 us
    ppermute x4, starting transfers between devices, swap_cores(): lax.ppermute(x, 'ctx', [(i, i ^ 1) for i in range(lax.axis_size('ctx'))])  30.3 us
    all_gather x1, blocking collectives, per_device(): lax.all_gather(packed, 'ctx', axis=0, axis_index_groups=same_core)  24.5 us
    all_to_all x1, blocking collectives, per_device(): sums = lax.all_to_all(sums, 'fsdp', 0, 0, tiled=True)  13 us
    unnamed x33, local copies, waits for them, and re-layouts  8 us
    ppermute x15, waiting for transfers between devices, shift(): return lax.ppermute(x, 'ctx', [(i, (i + by) % n) for i in range(n)])  7.95 us
    pallas_call x9, Pallas kernels, call(): pl.pallas_call(kernel, out_shape=shapes, in_specs=[SMEM] * smem + [VMEM]...  6.6 us
    all_to_all x1, starting transfers between devices, per_device(): tok = lax.all_to_all(copies, 'fsdp', 0, 0)  3.85 us
  transfers between devices with their start and end apart: 20, of which 8 were waited for; matrix products, arithmetic and copies ran while one was open for 1% of the time, Pallas kernels for 2%

profile of v6, /device:TPU:1, one launch (start us, length us, event | category | flops | bytes accessed | tf_op | source)
XLA Modules:
  0.0 152.5 jit_solution(14478122210466113977)
XLA Ops:
  0.9 8.8 %collective-permute-start = (bf16[256,128]{1,0:T(8,128)(2,1)S(1)}, bf16[256,128]{1,0:T(8,128)(2,1)S(1)}, u32[]{:S(2)}, u32[]{:S(2)}) collective-permute-start(bf16[256,128]{1,0:T(8,128)(2,1)S(1)} %get-tuple-element.38), channel_id=1, source_target_pairs={{0,16},{16,0},{32,48},{48,32},{64,80},{80,64},{96,112},{112,96},{1... | collective-permute-start | bytes 196616 | tf_op jit(solution)/shard_map/ppermute | solution.py:42
  12.5 3.8 %all-to-all-start = ((bf16[16,512,128]{2,1,0:T(8,128)(2,1)}), bf16[16,512,128]{2,1,0:T(8,128)(2,1)S(1)}, u32[]{:S(2)}, u32[]{:S(2)}) async-start(bf16[16,512,128]{2,1,0:T(8,128)(2,1)} %broadcast_in_dim.2), calls=%async_computation | async-start | bytes 4194304 | tf_op jit(solution)/shard_map/all_to_all | solution.py:230
  16.4 1.9 %collective-permute-start.7 = (bf16[128,768]{1,0:T(8,128)(2,1)S(1)}, bf16[128,768]{1,0:T(8,128)(2,1)S(1)}, u32[]{:S(2)}, u32[]{:S(2)}) collective-permute-start(bf16[128,768]{1,0:T(8,128)(2,1)S(1)} %bitcast_dynamic-update-slice_fusion.refs_0_), channel_id=1, source_target_pairs={{0,32},{16,48},{32,64},{48,80},{64,96},{80,112},{96,128},{112,144}... | collective-permute-start | bytes 589832 | tf_op jit(solution)/shard_map/ppermute | solution.py:38
  18.3 8.8 %collective-permute-start.1 = (bf16[128,768]{1,0:T(8,128)(2,1)S(1)}, bf16[128,768]{1,0:T(8,128)(2,1)S(1)}, u32[]{:S(2)}, u32[]{:S(2)}) collective-permute-start(bf16[128,768]{1,0:T(8,128)(2,1)S(1)} %bitcast_dynamic-update-slice_fusion.refs_0_), channel_id=1, source_target_pairs={{0,480},{16,496},{32,0},{48,16},{64,32},{80,48},{96,64},{112,80},{... | collective-permute-start | bytes 589832 | tf_op jit(solution)/shard_map/ppermute | solution.py:38
  27.1 2.9 %collective-permute-done.7.refs_1_ = bf16[128,768]{1,0:T(8,128)(2,1)S(1)} collective-permute-done((bf16[128,768]{1,0:T(8,128)(2,1)S(1)}, bf16[128,768]{1,0:T(8,128)(2,1)S(1)}, u32[]{:S(2)}, u32[]{:S(2)}) %collective-permute-start.7) | collective-permute-done | bytes 196640 | tf_op jit(solution)/shard_map/ppermute | solution.py:38
  29.9 1.9 %collective-permute-start.8 = (bf16[128,768]{1,0:T(8,128)(2,1)S(1)}, bf16[128,768]{1,0:T(8,128)(2,1)S(1)}, u32[]{:S(2)}, u32[]{:S(2)}) collective-permute-start(bf16[128,768]{1,0:T(8,128)(2,1)S(1)} %collective-permute-done.7.refs_1_), channel_id=1, source_target_pairs={{0,32},{16,48},{32,64},{48,80},{64,96},{80,112},{96,128},{112,144}... | collective-permute-start | bytes 589832 | tf_op jit(solution)/shard_map/ppermute | solution.py:38
  31.9 4.6 %collective-permute-start.2 = (bf16[128,768]{1,0:T(8,128)(2,1)S(1)}, bf16[128,768]{1,0:T(8,128)(2,1)S(1)}, u32[]{:S(2)}, u32[]{:S(2)}) collective-permute-start(bf16[128,768]{1,0:T(8,128)(2,1)S(1)} %collective-permute-done.1.refs_2_), channel_id=1, source_target_pairs={{0,480},{16,496},{32,0},{48,16},{64,32},{80,48},{96,64},{112,80},{... | collective-permute-start | bytes 589832 | tf_op jit(solution)/shard_map/ppermute | solution.py:38
  36.5 1.9 %collective-permute-done.8.refs_3_ = bf16[128,768]{1,0:T(8,128)(2,1)S(1)} collective-permute-done((bf16[128,768]{1,0:T(8,128)(2,1)S(1)}, bf16[128,768]{1,0:T(8,128)(2,1)S(1)}, u32[]{:S(2)}, u32[]{:S(2)}) %collective-permute-start.8) | collective-permute-done | bytes 196640 | tf_op jit(solution)/shard_map/ppermute | solution.py:38
  38.4 1.9 %collective-permute-start.9 = (bf16[128,768]{1,0:T(8,128)(2,1)S(1)}, bf16[128,768]{1,0:T(8,128)(2,1)S(1)}, u32[]{:S(2)}, u32[]{:S(2)}) collective-permute-start(bf16[128,768]{1,0:T(8,128)(2,1)S(1)} %collective-permute-done.8.refs_3_), channel_id=1, source_target_pairs={{0,32},{16,48},{32,64},{48,80},{64,96},{80,112},{96,128},{112,144}... | collective-permute-start | bytes 589832 | tf_op jit(solution)/shard_map/ppermute | solution.py:38
  40.3 4.6 %collective-permute-start.3 = (bf16[128,768]{1,0:T(8,128)(2,1)S(1)}, bf16[128,768]{1,0:T(8,128)(2,1)S(1)}, u32[]{:S(2)}, u32[]{:S(2)}) collective-permute-start(bf16[128,768]{1,0:T(8,128)(2,1)S(1)} %collective-permute-done.2.refs_4_), channel_id=1, source_target_pairs={{0,480},{16,496},{32,0},{48,16},{64,32},{80,48},{96,64},{112,80},{... | collective-permute-start | bytes 589832 | tf_op jit(solution)/shard_map/ppermute | solution.py:38
  46.0 1.9 %collective-permute-start.10 = (bf16[128,768]{1,0:T(8,128)(2,1)S(1)}, bf16[128,768]{1,0:T(8,128)(2,1)S(1)}, u32[]{:S(2)}, u32[]{:S(2)}) collective-permute-start(bf16[128,768]{1,0:T(8,128)(2,1)S(1)} %collective-permute-done.9.refs_5_), channel_id=1, source_target_pairs={{0,32},{16,48},{32,64},{48,80},{64,96},{80,112},{96,128},{112,144}... | collective-permute-start | bytes 589832 | tf_op jit(solution)/shard_map/ppermute | solution.py:38
  47.9 4.9 %collective-permute-start.4 = (bf16[128,768]{1,0:T(8,128)(2,1)S(1)}, bf16[128,768]{1,0:T(8,128)(2,1)S(1)}, u32[]{:S(2)}, u32[]{:S(2)}) collective-permute-start(bf16[128,768]{1,0:T(8,128)(2,1)S(1)} %collective-permute-done.3.refs_6_), channel_id=1, source_target_pairs={{0,480},{16,496},{32,0},{48,16},{64,32},{80,48},{96,64},{112,80},{... | collective-permute-start | bytes 589832 | tf_op jit(solution)/shard_map/ppermute | solution.py:38
  53.6 1.9 %collective-permute-start.11 = (bf16[128,768]{1,0:T(8,128)(2,1)S(1)}, bf16[128,768]{1,0:T(8,128)(2,1)S(1)}, u32[]{:S(2)}, u32[]{:S(2)}) collective-permute-start(bf16[128,768]{1,0:T(8,128)(2,1)S(1)} %collective-permute-done.10.refs_7_), channel_id=1, source_target_pairs={{0,32},{16,48},{32,64},{48,80},{64,96},{80,112},{96,128},{112,144}... | collective-permute-start | bytes 589832 | tf_op jit(solution)/shard_map/ppermute | solution.py:38
  56.2 4.6 %collective-permute-start.5 = (bf16[128,768]{1,0:T(8,128)(2,1)S(1)}, bf16[128,768]{1,0:T(8,128)(2,1)S(1)}, u32[]{:S(2)}, u32[]{:S(2)}) collective-permute-start(bf16[128,768]{1,0:T(8,128)(2,1)S(1)} %collective-permute-done.4.refs_8_), channel_id=1, source_target_pairs={{0,480},{16,496},{32,0},{48,16},{64,32},{80,48},{96,64},{112,80},{... | collective-permute-start | bytes 589832 | tf_op jit(solution)/shard_map/ppermute | solution.py:38
  61.4 1.9 %collective-permute-start.12 = (bf16[128,768]{1,0:T(8,128)(2,1)S(1)}, bf16[128,768]{1,0:T(8,128)(2,1)S(1)}, u32[]{:S(2)}, u32[]{:S(2)}) collective-permute-start(bf16[128,768]{1,0:T(8,128)(2,1)S(1)} %collective-permute-done.11.refs_9_), channel_id=1, source_target_pairs={{0,32},{16,48},{32,64},{48,80},{64,96},{80,112},{96,128},{112,144}... | collective-permute-start | bytes 589832 | tf_op jit(solution)/shard_map/ppermute | solution.py:38
  64.0 4.6 %collective-permute-start.6 = (bf16[128,768]{1,0:T(8,128)(2,1)S(1)}, bf16[128,768]{1,0:T(8,128)(2,1)}, u32[]{:S(2)}, u32[]{:S(2)}) collective-permute-start(bf16[128,768]{1,0:T(8,128)(2,1)S(1)} %collective-permute-done.5.refs_10_), channel_id=1, source_target_pairs={{0,480},{16,496},{32,0},{48,16},{64,32},{80,48},{96,64},{112,80},{... | collective-permute-start | bytes 589832 | tf_op jit(solution)/shard_map/ppermute | solution.py:38
  69.3 1.9 %collective-permute-start.13 = (bf16[128,768]{1,0:T(8,128)(2,1)S(1)}, bf16[128,768]{1,0:T(8,128)(2,1)}, u32[]{:S(2)}, u32[]{:S(2)}) collective-permute-start(bf16[128,768]{1,0:T(8,128)(2,1)S(1)} %collective-permute-done.12.refs_11_), channel_id=1, source_target_pairs={{0,32},{16,48},{32,64},{48,80},{64,96},{80,112},{96,128},{112,144}... | collective-permute-start | bytes 589832 | tf_op jit(solution)/shard_map/ppermute | solution.py:38
  71.9 4.6 %collective-permute-start.14 = (bf16[128,768]{1,0:T(8,128)(2,1)}, bf16[128,768]{1,0:T(8,128)(2,1)}, u32[]{:S(2)}, u32[]{:S(2)}) collective-permute-start(bf16[128,768]{1,0:T(8,128)(2,1)} %collective-permute-done.6.refs_0_), channel_id=1, source_target_pairs={{0,480},{16,496},{32,0},{48,16},{64,32},{80,48},{96,64},{112,80},{... | collective-permute-start | bytes 589832 | tf_op jit(solution)/shard_map/ppermute | solution.py:38
  77.0 1.9 %collective-permute-start.15 = (bf16[128,768]{1,0:T(8,128)(2,1)}, bf16[128,768]{1,0:T(8,128)(2,1)}, u32[]{:S(2)}, u32[]{:S(2)}) collective-permute-start(bf16[128,768]{1,0:T(8,128)(2,1)} %collective-permute-done.13.refs_1_), channel_id=1, source_target_pairs={{0,32},{16,48},{32,64},{48,80},{64,96},{80,112},{96,128},{112,144}... | collective-permute-start | bytes 589832 | tf_op jit(solution)/shard_map/ppermute | solution.py:38
  87.5 10.3 %collective-permute-start.16 = (f32[256,768]{1,0:T(8,128)S(1)}, f32[256,768]{1,0:T(8,128)S(1)}, u32[]{:S(2)}, u32[]{:S(2)}) collective-permute-start(f32[256,768]{1,0:T(8,128)S(1)} %get-tuple-element.21), channel_id=1, source_target_pairs={{0,16},{16,0},{32,48},{48,32},{64,80},{80,64},{96,112},{112,96},{1... | collective-permute-start | bytes 2359304 | tf_op jit(solution)/shard_map/ppermute | solution.py:42
  100.0 2.3 %collective-permute-start.17 = (f32[136,128]{1,0:T(8,128)S(1)}, f32[136,128]{1,0:T(8,128)S(1)}, u32[]{:S(2)}, u32[]{:S(2)}) collective-permute-start(f32[136,128]{1,0:T(8,128)S(1)} %get-tuple-element.28), channel_id=1, source_target_pairs={{0,16},{16,0},{32,48},{48,32},{64,80},{80,64},{96,112},{112,96},{1... | collective-permute-start | bytes 208904 | tf_op jit(solution)/shard_map/ppermute | solution.py:42
  103.2 24.5 %all-gather = bf16[2304,128]{1,0:T(8,128)(2,1)S(1)} all-gather(bf16[144,128]{1,0:T(8,128)(2,1)S(1)} %get-tuple-element.29), channel_id=2, replica_groups={{0,32,64,96,128,160,192,224,256,288,320,352,384,416,448,480},{16,48,80,..., dimensions={0}, use_global_device_ids=true | all-gather | bytes 626688 | tf_op jit(solution)/shard_map/all_gather | solution.py:275
  127.9 9.0 %collective-permute-start.18 = (f32[128,128]{1,0:T(8,128)S(1)}, f32[128,128]{1,0:T(8,128)S(1)}, u32[]{:S(2)}, u32[]{:S(2)}) collective-permute-start(f32[128,128]{1,0:T(8,128)S(1)} %get-tuple-element.32), channel_id=1, source_target_pairs={{0,16},{16,0},{32,48},{48,32},{64,80},{80,64},{96,112},{112,96},{1... | collective-permute-start | bytes 196616 | tf_op jit(solution)/shard_map/ppermute | solution.py:42
  138.4 13.0 %all_to_all.16 = f32[16,1,256]{2,1,0:T(1,128)S(1)} all-to-all(f32[16,1,256]{2,1,0:T(1,128)S(1)} %copy.8), channel_id=1, replica_groups=mesh['ctx'=32,'fsdp'=16] {'fsdp'}, dimensions={0} | all-to-all | bytes 32768 | tf_op jit(solution)/shard_map/all_to_all | solution.py:300
  (67 shorter events, 23.9 us)
Async XLA Ops:
  0.9 9.8 %collective-permute-start = (bf16[256,128]{1,0:T(8,128)(2,1)S(1)}, bf16[256,128]{1,0:T(8,128)(2,1)S(1)}, u32[]{:S(2)}, u32[]{:S(2)}) collective-permute-start(bf16[256,128]{1,0:T(8,128)(2,1)S(1)} %get-tuple-element.38), channel_id=1, source_target_pairs={{0,16},{16,0},{32,48},{48,32},{64,80},{80,64},{96,112},{112,96},{1... | collective-permute-start | bytes 196616 | tf_op jit(solution)/shard_map/ppermute | solution.py:42
  12.5 66.5 %all-to-all-start = ((bf16[16,512,128]{2,1,0:T(8,128)(2,1)}), bf16[16,512,128]{2,1,0:T(8,128)(2,1)S(1)}, u32[]{:S(2)}, u32[]{:S(2)}) async-start(bf16[16,512,128]{2,1,0:T(8,128)(2,1)} %broadcast_in_dim.2), calls=%async_computation | async-start | bytes 4194304 | tf_op jit(solution)/shard_map/all_to_all | solution.py:230
  16.4 13.6 %collective-permute-start.7 = (bf16[128,768]{1,0:T(8,128)(2,1)S(1)}, bf16[128,768]{1,0:T(8,128)(2,1)S(1)}, u32[]{:S(2)}, u32[]{:S(2)}) collective-permute-start(bf16[128,768]{1,0:T(8,128)(2,1)S(1)} %bitcast_dynamic-update-slice_fusion.refs_0_), channel_id=1, source_target_pairs={{0,32},{16,48},{32,64},{48,80},{64,96},{80,112},{96,128},{112,144}... | collective-permute-start | bytes 589832 | tf_op jit(solution)/shard_map/ppermute | solution.py:38
  18.3 13.6 %collective-permute-start.1 = (bf16[128,768]{1,0:T(8,128)(2,1)S(1)}, bf16[128,768]{1,0:T(8,128)(2,1)S(1)}, u32[]{:S(2)}, u32[]{:S(2)}) collective-permute-start(bf16[128,768]{1,0:T(8,128)(2,1)S(1)} %bitcast_dynamic-update-slice_fusion.refs_0_), channel_id=1, source_target_pairs={{0,480},{16,496},{32,0},{48,16},{64,32},{80,48},{96,64},{112,80},{... | collective-permute-start | bytes 589832 | tf_op jit(solution)/shard_map/ppermute | solution.py:38
  29.9 8.4 %collective-permute-start.8 = (bf16[128,768]{1,0:T(8,128)(2,1)S(1)}, bf16[128,768]{1,0:T(8,128)(2,1)S(1)}, u32[]{:S(2)}, u32[]{:S(2)}) collective-permute-start(bf16[128,768]{1,0:T(8,128)(2,1)S(1)} %collective-permute-done.7.refs_1_), channel_id=1, source_target_pairs={{0,32},{16,48},{32,64},{48,80},{64,96},{80,112},{96,128},{112,144}... | collective-permute-start | bytes 589832 | tf_op jit(solution)/shard_map/ppermute | solution.py:38
  31.9 8.4 %collective-permute-start.2 = (bf16[128,768]{1,0:T(8,128)(2,1)S(1)}, bf16[128,768]{1,0:T(8,128)(2,1)S(1)}, u32[]{:S(2)}, u32[]{:S(2)}) collective-permute-start(bf16[128,768]{1,0:T(8,128)(2,1)S(1)} %collective-permute-done.1.refs_2_), channel_id=1, source_target_pairs={{0,480},{16,496},{32,0},{48,16},{64,32},{80,48},{96,64},{112,80},{... | collective-permute-start | bytes 589832 | tf_op jit(solution)/shard_map/ppermute | solution.py:38
  38.4 7.6 %collective-permute-start.9 = (bf16[128,768]{1,0:T(8,128)(2,1)S(1)}, bf16[128,768]{1,0:T(8,128)(2,1)S(1)}, u32[]{:S(2)}, u32[]{:S(2)}) collective-permute-start(bf16[128,768]{1,0:T(8,128)(2,1)S(1)} %collective-permute-done.8.refs_3_), channel_id=1, source_target_pairs={{0,32},{16,48},{32,64},{48,80},{64,96},{80,112},{96,128},{112,144}... | collective-permute-start | bytes 589832 | tf_op jit(solution)/shard_map/ppermute | solution.py:38
  40.3 7.6 %collective-permute-start.3 = (bf16[128,768]{1,0:T(8,128)(2,1)S(1)}, bf16[128,768]{1,0:T(8,128)(2,1)S(1)}, u32[]{:S(2)}, u32[]{:S(2)}) collective-permute-start(bf16[128,768]{1,0:T(8,128)(2,1)S(1)} %collective-permute-done.2.refs_4_), channel_id=1, source_target_pairs={{0,480},{16,496},{32,0},{48,16},{64,32},{80,48},{96,64},{112,80},{... | collective-permute-start | bytes 589832 | tf_op jit(solution)/shard_map/ppermute | solution.py:38
  46.0 7.6 %collective-permute-start.10 = (bf16[128,768]{1,0:T(8,128)(2,1)S(1)}, bf16[128,768]{1,0:T(8,128)(2,1)S(1)}, u32[]{:S(2)}, u32[]{:S(2)}) collective-permute-start(bf16[128,768]{1,0:T(8,128)(2,1)S(1)} %collective-permute-done.9.refs_5_), channel_id=1, source_target_pairs={{0,32},{16,48},{32,64},{48,80},{64,96},{80,112},{96,128},{112,144}... | collective-permute-start | bytes 589832 | tf_op jit(solution)/shard_map/ppermute | solution.py:38
  47.9 8.3 %collective-permute-start.4 = (bf16[128,768]{1,0:T(8,128)(2,1)S(1)}, bf16[128,768]{1,0:T(8,128)(2,1)S(1)}, u32[]{:S(2)}, u32[]{:S(2)}) collective-permute-start(bf16[128,768]{1,0:T(8,128)(2,1)S(1)} %collective-permute-done.3.refs_6_), channel_id=1, source_target_pairs={{0,480},{16,496},{32,0},{48,16},{64,32},{80,48},{96,64},{112,80},{... | collective-permute-start | bytes 589832 | tf_op jit(solution)/shard_map/ppermute | solution.py:38
  53.6 7.8 %collective-permute-start.11 = (bf16[128,768]{1,0:T(8,128)(2,1)S(1)}, bf16[128,768]{1,0:T(8,128)(2,1)S(1)}, u32[]{:S(2)}, u32[]{:S(2)}) collective-permute-start(bf16[128,768]{1,0:T(8,128)(2,1)S(1)} %collective-permute-done.10.refs_7_), channel_id=1, source_target_pairs={{0,32},{16,48},{32,64},{48,80},{64,96},{80,112},{96,128},{112,144}... | collective-permute-start | bytes 589832 | tf_op jit(solution)/shard_map/ppermute | solution.py:38
  56.2 7.9 %collective-permute-start.5 = (bf16[128,768]{1,0:T(8,128)(2,1)S(1)}, bf16[128,768]{1,0:T(8,128)(2,1)S(1)}, u32[]{:S(2)}, u32[]{:S(2)}) collective-permute-start(bf16[128,768]{1,0:T(8,128)(2,1)S(1)} %collective-permute-done.4.refs_8_), channel_id=1, source_target_pairs={{0,480},{16,496},{32,0},{48,16},{64,32},{80,48},{96,64},{112,80},{... | collective-permute-start | bytes 589832 | tf_op jit(solution)/shard_map/ppermute | solution.py:38
  61.4 7.9 %collective-permute-start.12 = (bf16[128,768]{1,0:T(8,128)(2,1)S(1)}, bf16[128,768]{1,0:T(8,128)(2,1)S(1)}, u32[]{:S(2)}, u32[]{:S(2)}) collective-permute-start(bf16[128,768]{1,0:T(8,128)(2,1)S(1)} %collective-permute-done.11.refs_9_), channel_id=1, source_target_pairs={{0,32},{16,48},{32,64},{48,80},{64,96},{80,112},{96,128},{112,144}... | collective-permute-start | bytes 589832 | tf_op jit(solution)/shard_map/ppermute | solution.py:38
  64.0 7.8 %collective-permute-start.6 = (bf16[128,768]{1,0:T(8,128)(2,1)S(1)}, bf16[128,768]{1,0:T(8,128)(2,1)}, u32[]{:S(2)}, u32[]{:S(2)}) collective-permute-start(bf16[128,768]{1,0:T(8,128)(2,1)S(1)} %collective-permute-done.5.refs_10_), channel_id=1, source_target_pairs={{0,480},{16,496},{32,0},{48,16},{64,32},{80,48},{96,64},{112,80},{... | collective-permute-start | bytes 589832 | tf_op jit(solution)/shard_map/ppermute | solution.py:38
  69.3 7.7 %collective-permute-start.13 = (bf16[128,768]{1,0:T(8,128)(2,1)S(1)}, bf16[128,768]{1,0:T(8,128)(2,1)}, u32[]{:S(2)}, u32[]{:S(2)}) collective-permute-start(bf16[128,768]{1,0:T(8,128)(2,1)S(1)} %collective-permute-done.12.refs_11_), channel_id=1, source_target_pairs={{0,32},{16,48},{32,64},{48,80},{64,96},{80,112},{96,128},{112,144}... | collective-permute-start | bytes 589832 | tf_op jit(solution)/shard_map/ppermute | solution.py:38
  71.9 13.1 %collective-permute-start.14 = (bf16[128,768]{1,0:T(8,128)(2,1)}, bf16[128,768]{1,0:T(8,128)(2,1)}, u32[]{:S(2)}, u32[]{:S(2)}) collective-permute-start(bf16[128,768]{1,0:T(8,128)(2,1)} %collective-permute-done.6.refs_0_), channel_id=1, source_target_pairs={{0,480},{16,496},{32,0},{48,16},{64,32},{80,48},{96,64},{112,80},{... | collective-permute-start | bytes 589832 | tf_op jit(solution)/shard_map/ppermute | solution.py:38
  77.0 8.7 %collective-permute-start.15 = (bf16[128,768]{1,0:T(8,128)(2,1)}, bf16[128,768]{1,0:T(8,128)(2,1)}, u32[]{:S(2)}, u32[]{:S(2)}) collective-permute-start(bf16[128,768]{1,0:T(8,128)(2,1)} %collective-permute-done.13.refs_1_), channel_id=1, source_target_pairs={{0,32},{16,48},{32,64},{48,80},{64,96},{80,112},{96,128},{112,144}... | collective-permute-start | bytes 589832 | tf_op jit(solution)/shard_map/ppermute | solution.py:38
  85.0 12.8 %copy-start.10 = (f32[2,256]{1,0:T(2,128)S(1)}, f32[2,256]{1,0:T(2,128)}, u32[]{:S(2)}) copy-start(f32[2,256]{1,0:T(2,128)} %decays_ref.1) | copy-start | bytes 6148
  85.0 12.8 %copy-start.12 = (s32[256]{0:T(256)S(1)}, s32[256]{0:T(256)}, u32[]{:S(2)}) copy-start(s32[256]{0:T(256)} %param.13) | copy-start | bytes 3076
  87.5 49.4 %copy-start.13 = (f32[2]{0:T(128)S(1)}, f32[2]{0:T(128)}, u32[]{:S(2)}) copy-start(f32[2]{0:T(128)} %skip_ref.1) | copy-start | bytes 28
  87.5 12.2 %collective-permute-start.16 = (f32[256,768]{1,0:T(8,128)S(1)}, f32[256,768]{1,0:T(8,128)S(1)}, u32[]{:S(2)}, u32[]{:S(2)}) collective-permute-start(f32[256,768]{1,0:T(8,128)S(1)} %get-tuple-element.21), channel_id=1, source_target_pairs={{0,16},{16,0},{32,48},{48,32},{64,80},{80,64},{96,112},{112,96},{1... | collective-permute-start | bytes 2359304 | tf_op jit(solution)/shard_map/ppermute | solution.py:42
  100.0 3.2 %collective-permute-start.17 = (f32[136,128]{1,0:T(8,128)S(1)}, f32[136,128]{1,0:T(8,128)S(1)}, u32[]{:S(2)}, u32[]{:S(2)}) collective-permute-start(f32[136,128]{1,0:T(8,128)S(1)} %get-tuple-element.28), channel_id=1, source_target_pairs={{0,16},{16,0},{32,48},{48,32},{64,80},{80,64},{96,112},{112,96},{1... | collective-permute-start | bytes 208904 | tf_op jit(solution)/shard_map/ppermute | solution.py:42
  127.7 23.8 %copy-start.11 = (f32[2,128]{1,0:T(2,128)S(1)}, f32[2,128]{1,0:T(2,128)}, u32[]{:S(2)}) copy-start(f32[2,128]{1,0:T(2,128)} %param.10) | copy-start | bytes 3076
  127.9 10.0 %collective-permute-start.18 = (f32[128,128]{1,0:T(8,128)S(1)}, f32[128,128]{1,0:T(8,128)S(1)}, u32[]{:S(2)}, u32[]{:S(2)}) collective-permute-start(f32[128,128]{1,0:T(8,128)S(1)} %get-tuple-element.32), channel_id=1, source_target_pairs={{0,16},{16,0},{32,48},{48,32},{64,80},{80,64},{96,112},{112,96},{1... | collective-permute-start | bytes 196616 | tf_op jit(solution)/shard_map/ppermute | solution.py:42
  (11 other events, 11.9 us)

commit v7 on v6

--- a/solution.py
+++ b/solution.py
@@ -243,16 +243,19 @@
     up = down = block
     steps, blocks, acc = [0], [block], ()
     for s in range(1, half + 1):
+        if s == half - 1:
+            up, done = lax.optimization_barrier((up, acc[0]))
+            acc = [done]
         up = shift(up, 2)
         steps.append(s)
         blocks.append(up)
-        if s == half - 2:
-            acc = partial_product(1, steps, chip_1, tok, blocks, acc)
-            steps, blocks = [], []
         if s < half:
             down = shift(down, -2)
             steps.append(-s)
             blocks.append(down)
+        if s == half - 4:
+            acc = partial_product(1, steps, chip_1, tok, blocks, acc)
+            steps, blocks = [], []
     own, other = partial_product(2, steps, chip_1, tok, blocks, acc)
     got = swap_cores(other)
 

time: 154 us -> 154 us (level)
  waiting for transfers between devices: 9.62 us -> 18 us
  local copies, waits for them, and re-layouts: 11.5 us -> 4.26 us
  blocking collectives: 37.5 us -> 35.5 us
    ppermute x15, waiting for transfers between devices: 7.95 us -> 15.5 us  [shift(): return lax.ppermute(x, 'ctx', [(i, (i + by) % n) for i in range(n)])]
    unnamed x33 -> x19, local copies, waits for them, and re-layouts: 8 us -> 1.64 us
    all_gather x1, blocking collectives: 24.5 us -> 22.5 us  [per_device(): lax.all_gather(packed, 'ctx', axis=0, axis_index_groups=same_core)]
  transfers between devices with their start and end apart: 20 -> 20, of which waited for: 8 -> 11; matrix products, arithmetic and copies ran while one was open for 1% -> 0% of each run, Pallas kernels for 2% -> 3%
where the time goes in v7:
time: 154 us
  starting transfers between devices  86.7 us (56%)
  blocking collectives  35.5 us (23%)
  waiting for transfers between devices  18 us (12%)
  Pallas kernels  7.76 us (5%)
  local copies, waits for them, and re-layouts  4.26 us (3%)
    ppermute x15, starting transfers between devices, shift(): return lax.ppermute(x, 'ctx', [(i, (i + by) % n) for i in range(n)])  52.2 us
    ppermute x4, starting transfers between devices, swap_cores(): lax.ppermute(x, 'ctx', [(i, i ^ 1) for i in range(lax.axis_size('ctx'))])  30.6 us
    all_gather x1, blocking collectives, per_device(): lax.all_gather(packed, 'ctx', axis=0, axis_index_groups=same_core)  22.5 us
    ppermute x15, waiting for transfers between devices, shift(): return lax.ppermute(x, 'ctx', [(i, (i + by) % n) for i in range(n)])  15.5 us
    all_to_all x1, blocking collectives, per_device(): sums = lax.all_to_all(sums, 'fsdp', 0, 0, tiled=True)  12.9 us
    pallas_call x9, Pallas kernels, call(): pl.pallas_call(kernel, out_shape=shapes, in_specs=[SMEM] * smem + [VMEM]...  7.76 us
    all_to_all x1, starting transfers between devices, per_device(): tok = lax.all_to_all(copies, 'fsdp', 0, 0)  3.85 us
  transfers between devices with their start and end apart: 20, of which 11 were waited for; matrix products, arithmetic and copies ran while one was open for 0% of the time, Pallas kernels for 3%

profile of v7, /device:TPU:1, one launch (start us, length us, event | category | flops | bytes accessed | tf_op | source)
XLA Modules:
  0.0 153.5 jit_solution(4921681516853440410)
XLA Ops:
  0.9 8.8 %collective-permute-start = (bf16[256,128]{1,0:T(8,128)(2,1)S(1)}, bf16[256,128]{1,0:T(8,128)(2,1)S(1)}, u32[]{:S(2)}, u32[]{:S(2)}) collective-permute-start(bf16[256,128]{1,0:T(8,128)(2,1)S(1)} %get-tuple-element.42), channel_id=1, source_target_pairs={{0,16},{16,0},{32,48},{48,32},{64,80},{80,64},{96,112},{112,96},{1... | collective-permute-start | bytes 196616 | tf_op jit(solution)/shard_map/ppermute | solution.py:42
  12.3 3.8 %all-to-all-start = ((bf16[16,512,128]{2,1,0:T(8,128)(2,1)}), bf16[16,512,128]{2,1,0:T(8,128)(2,1)S(1)}, u32[]{:S(2)}, u32[]{:S(2)}) async-start(bf16[16,512,128]{2,1,0:T(8,128)(2,1)} %broadcast_in_dim.2), calls=%async_computation | async-start | bytes 4194304 | tf_op jit(solution)/shard_map/all_to_all | solution.py:230
  16.4 1.9 %collective-permute-start.1 = (bf16[128,768]{1,0:T(8,128)(2,1)S(1)}, bf16[128,768]{1,0:T(8,128)(2,1)S(1)}, u32[]{:S(2)}, u32[]{:S(2)}) collective-permute-start(bf16[128,768]{1,0:T(8,128)(2,1)S(1)} %bitcast_dynamic-update-slice_fusion.refs_0_), channel_id=1, source_target_pairs={{0,32},{16,48},{32,64},{48,80},{64,96},{80,112},{96,128},{112,144}... | collective-permute-start | bytes 589832 | tf_op jit(solution)/shard_map/ppermute | solution.py:38
  18.3 8.8 %collective-permute-start.6 = (bf16[128,768]{1,0:T(8,128)(2,1)S(1)}, bf16[128,768]{1,0:T(8,128)(2,1)S(1)}, u32[]{:S(2)}, u32[]{:S(2)}) collective-permute-start(bf16[128,768]{1,0:T(8,128)(2,1)S(1)} %bitcast_dynamic-update-slice_fusion.refs_0_), channel_id=1, source_target_pairs={{0,480},{16,496},{32,0},{48,16},{64,32},{80,48},{96,64},{112,80},{... | collective-permute-start | bytes 589832 | tf_op jit(solution)/shard_map/ppermute | solution.py:38
  27.1 2.7 %collective-permute-done.1.refs_1_ = bf16[128,768]{1,0:T(8,128)(2,1)S(1)} collective-permute-done((bf16[128,768]{1,0:T(8,128)(2,1)S(1)}, bf16[128,768]{1,0:T(8,128)(2,1)S(1)}, u32[]{:S(2)}, u32[]{:S(2)}) %collective-permute-start.1) | collective-permute-done | bytes 196640 | tf_op jit(solution)/shard_map/ppermute | solution.py:38
  29.8 1.9 %collective-permute-start.2 = (bf16[128,768]{1,0:T(8,128)(2,1)S(1)}, bf16[128,768]{1,0:T(8,128)(2,1)S(1)}, u32[]{:S(2)}, u32[]{:S(2)}) collective-permute-start(bf16[128,768]{1,0:T(8,128)(2,1)S(1)} %collective-permute-done.1.refs_1_), channel_id=1, source_target_pairs={{0,32},{16,48},{32,64},{48,80},{64,96},{80,112},{96,128},{112,144}... | collective-permute-start | bytes 589832 | tf_op jit(solution)/shard_map/ppermute | solution.py:38
  31.7 4.6 %collective-permute-start.7 = (bf16[128,768]{1,0:T(8,128)(2,1)S(1)}, bf16[128,768]{1,0:T(8,128)(2,1)S(1)}, u32[]{:S(2)}, u32[]{:S(2)}) collective-permute-start(bf16[128,768]{1,0:T(8,128)(2,1)S(1)} %collective-permute-done.6.refs_2_), channel_id=1, source_target_pairs={{0,480},{16,496},{32,0},{48,16},{64,32},{80,48},{96,64},{112,80},{... | collective-permute-start | bytes 589832 | tf_op jit(solution)/shard_map/ppermute | solution.py:38
  40.0 4.6 %collective-permute-start.8 = (bf16[128,768]{1,0:T(8,128)(2,1)S(1)}, bf16[128,768]{1,0:T(8,128)(2,1)S(1)}, u32[]{:S(2)}, u32[]{:S(2)}) collective-permute-start(bf16[128,768]{1,0:T(8,128)(2,1)S(1)} %collective-permute-done.7.refs_4_), channel_id=1, source_target_pairs={{0,480},{16,496},{32,0},{48,16},{64,32},{80,48},{96,64},{112,80},{... | collective-permute-start | bytes 589832 | tf_op jit(solution)/shard_map/ppermute | solution.py:38
  45.7 1.9 %collective-permute-start.4 = (bf16[128,768]{1,0:T(8,128)(2,1)S(1)}, bf16[128,768]{1,0:T(8,128)(2,1)S(1)}, u32[]{:S(2)}, u32[]{:S(2)}) collective-permute-start(bf16[128,768]{1,0:T(8,128)(2,1)S(1)} %collective-permute-done.3.refs_5_), channel_id=1, source_target_pairs={{0,32},{16,48},{32,64},{48,80},{64,96},{80,112},{96,128},{112,144}... | collective-permute-start | bytes 589832 | tf_op jit(solution)/shard_map/ppermute | solution.py:38
  47.7 4.9 %collective-permute-start.9 = (bf16[128,768]{1,0:T(8,128)(2,1)S(1)}, bf16[128,768]{1,0:T(8,128)(2,1)}, u32[]{:S(2)}, u32[]{:S(2)}) collective-permute-start(bf16[128,768]{1,0:T(8,128)(2,1)S(1)} %collective-permute-done.8.refs_6_), channel_id=1, source_target_pairs={{0,480},{16,496},{32,0},{48,16},{64,32},{80,48},{96,64},{112,80},{... | collective-permute-start | bytes 589832 | tf_op jit(solution)/shard_map/ppermute | solution.py:38
  53.3 1.9 %collective-permute-start.5 = (bf16[128,768]{1,0:T(8,128)(2,1)S(1)}, bf16[128,768]{1,0:T(8,128)(2,1)}, u32[]{:S(2)}, u32[]{:S(2)}) collective-permute-start(bf16[128,768]{1,0:T(8,128)(2,1)S(1)} %collective-permute-done.4.refs_7_), channel_id=1, source_target_pairs={{0,32},{16,48},{32,64},{48,80},{64,96},{80,112},{96,128},{112,144}... | collective-permute-start | bytes 589832 | tf_op jit(solution)/shard_map/ppermute | solution.py:38
  55.9 4.6 %collective-permute-start.10 = (bf16[128,768]{1,0:T(8,128)(2,1)}, bf16[128,768]{1,0:T(8,128)(2,1)}, u32[]{:S(2)}, u32[]{:S(2)}) collective-permute-start(bf16[128,768]{1,0:T(8,128)(2,1)} %collective-permute-done.9.refs_8_), channel_id=1, source_target_pairs={{0,480},{16,496},{32,0},{48,16},{64,32},{80,48},{96,64},{112,80},{... | collective-permute-start | bytes 589832 | tf_op jit(solution)/shard_map/ppermute | solution.py:38
  61.1 1.9 %collective-permute-start.11 = (bf16[128,768]{1,0:T(8,128)(2,1)}, bf16[128,768]{1,0:T(8,128)(2,1)}, u32[]{:S(2)}, u32[]{:S(2)}) collective-permute-start(bf16[128,768]{1,0:T(8,128)(2,1)} %collective-permute-done.5.refs_0_), channel_id=1, source_target_pairs={{0,32},{16,48},{32,64},{48,80},{64,96},{80,112},{96,128},{112,144}... | collective-permute-start | bytes 589832 | tf_op jit(solution)/shard_map/ppermute | solution.py:38
  63.4 5.0 %collective-permute-start.12 = (bf16[128,768]{1,0:T(8,128)(2,1)}, bf16[128,768]{1,0:T(8,128)(2,1)}, u32[]{:S(2)}, u32[]{:S(2)}) collective-permute-start(bf16[128,768]{1,0:T(8,128)(2,1)} %collective-permute-done.10.refs_1_), channel_id=1, source_target_pairs={{0,480},{16,496},{32,0},{48,16},{64,32},{80,48},{96,64},{112,80},{... | collective-permute-start | bytes 589832 | tf_op jit(solution)/shard_map/ppermute | solution.py:38
  69.4 2.1 %shard_map.73.refs_7_ = f32[512,768]{1,0:T(8,128)S(1)} custom-call(s32[1]{0:T(128)} %bitcast.1.chip_ref, bf16[16,512,128]{2,1,0:T(8,128)(2,1)S(1)} %all-to-all-done.tok_ref, bf16[128,768]{1,0:T(8,128)(2,1)S(1)} %bitcast_dynamic-update-slice_fusion.refs_0_, bf16[128,768]{1,0:T(8,128)(2,1)S(1)} %collective-permute-done.1.refs_1_, ...), custom_call_target="tpu_custom_call" | custom-call | tf_op jit(solution)/shard_map/pallas_call | solution.py:22
  71.5 1.9 %collective-permute-start.13 = (bf16[128,768]{1,0:T(8,128)(2,1)}, bf16[128,768]{1,0:T(8,128)(2,1)S(1)}, u32[]{:S(2)}, u32[]{:S(2)}) collective-permute-start(bf16[128,768]{1,0:T(8,128)(2,1)} %collective-permute-done.11.refs_2_), channel_id=1, source_target_pairs={{0,32},{16,48},{32,64},{48,80},{64,96},{80,112},{96,128},{112,144}... | collective-permute-start | bytes 589832 | tf_op jit(solution)/shard_map/ppermute | solution.py:38
  73.5 4.6 %collective-permute-start.14 = (bf16[128,768]{1,0:T(8,128)(2,1)}, bf16[128,768]{1,0:T(8,128)(2,1)S(1)}, u32[]{:S(2)}, u32[]{:S(2)}) collective-permute-start(bf16[128,768]{1,0:T(8,128)(2,1)} %collective-permute-done.12.refs_3_), channel_id=1, source_target_pairs={{0,480},{16,496},{32,0},{48,16},{64,32},{80,48},{96,64},{112,80},{... | collective-permute-start | bytes 589832 | tf_op jit(solution)/shard_map/ppermute | solution.py:38
  81.3 6.8 %collective-permute-done.15.refs_6_ = bf16[128,768]{1,0:T(8,128)(2,1)S(1)} collective-permute-done((bf16[128,768]{1,0:T(8,128)(2,1)S(1)}, bf16[128,768]{1,0:T(8,128)(2,1)S(1)}, u32[]{:S(2)}, u32[]{:S(2)}) %collective-permute-start.15) | collective-permute-done | bytes 196640 | tf_op jit(solution)/shard_map/ppermute | solution.py:38
  88.0 2.2 %shard_map.74 = (f32[256,768]{1,0:T(8,128)S(1)}, f32[256,768]{1,0:T(8,128)S(1)}) custom-call(s32[1]{0:T(128)} %bitcast.1.chip_ref, bf16[16,512,128]{2,1,0:T(8,128)(2,1)S(1)} %all-to-all-done.tok_ref, bf16[128,768]{1,0:T(8,128)(2,1)} %collective-permute-done.5.refs_0_, bf16[128,768]{1,0:T(8,128)(2,1)} %collective-permute-done.10.refs_1_, ...), custom_call_target="tpu_custom_call" | custom-call | tf_op jit(solution)/shard_map/pallas_call | solution.py:22
  90.3 10.3 %collective-permute-start.16 = (f32[256,768]{1,0:T(8,128)S(1)}, f32[256,768]{1,0:T(8,128)S(1)}, u32[]{:S(2)}, u32[]{:S(2)}) collective-permute-start(f32[256,768]{1,0:T(8,128)S(1)} %get-tuple-element.25), channel_id=1, source_target_pairs={{0,16},{16,0},{32,48},{48,32},{64,80},{80,64},{96,112},{112,96},{1... | collective-permute-start | bytes 2359304 | tf_op jit(solution)/shard_map/ppermute | solution.py:42
  102.9 2.3 %collective-permute-start.17 = (f32[136,128]{1,0:T(8,128)S(1)}, f32[136,128]{1,0:T(8,128)S(1)}, u32[]{:S(2)}, u32[]{:S(2)}) collective-permute-start(f32[136,128]{1,0:T(8,128)S(1)} %get-tuple-element.32), channel_id=1, source_target_pairs={{0,16},{16,0},{32,48},{48,32},{64,80},{80,64},{96,112},{112,96},{1... | collective-permute-start | bytes 208904 | tf_op jit(solution)/shard_map/ppermute | solution.py:42
  106.1 22.5 %all-gather = bf16[2304,128]{1,0:T(8,128)(2,1)S(1)} all-gather(bf16[144,128]{1,0:T(8,128)(2,1)S(1)} %get-tuple-element.33), channel_id=2, replica_groups={{0,32,64,96,128,160,192,224,256,288,320,352,384,416,448,480},{16,48,80,..., dimensions={0}, use_global_device_ids=true | all-gather | bytes 626688 | tf_op jit(solution)/shard_map/all_gather | solution.py:278
  128.7 9.2 %collective-permute-start.18 = (f32[128,128]{1,0:T(8,128)S(1)}, f32[128,128]{1,0:T(8,128)S(1)}, u32[]{:S(2)}, u32[]{:S(2)}) collective-permute-start(f32[128,128]{1,0:T(8,128)S(1)} %get-tuple-element.36), channel_id=1, source_target_pairs={{0,16},{16,0},{32,48},{48,32},{64,80},{80,64},{96,112},{112,96},{1... | collective-permute-start | bytes 196616 | tf_op jit(solution)/shard_map/ppermute | solution.py:42
  139.5 12.9 %all_to_all.16 = f32[16,1,256]{2,1,0:T(1,128)S(1)} all-to-all(f32[16,1,256]{2,1,0:T(1,128)S(1)} %copy.8), channel_id=1, replica_groups=mesh['ctx'=32,'fsdp'=16] {'fsdp'}, dimensions={0} | all-to-all | bytes 32768 | tf_op jit(solution)/shard_map/all_to_all | solution.py:303
  (53 shorter events, 21.0 us)
Async XLA Ops:
  0.9 9.7 %collective-permute-start = (bf16[256,128]{1,0:T(8,128)(2,1)S(1)}, bf16[256,128]{1,0:T(8,128)(2,1)S(1)}, u32[]{:S(2)}, u32[]{:S(2)}) collective-permute-start(bf16[256,128]{1,0:T(8,128)(2,1)S(1)} %get-tuple-element.42), channel_id=1, source_target_pairs={{0,16},{16,0},{32,48},{48,32},{64,80},{80,64},{96,112},{112,96},{1... | collective-permute-start | bytes 196616 | tf_op jit(solution)/shard_map/ppermute | solution.py:42
  12.3 56.1 %all-to-all-start = ((bf16[16,512,128]{2,1,0:T(8,128)(2,1)}), bf16[16,512,128]{2,1,0:T(8,128)(2,1)S(1)}, u32[]{:S(2)}, u32[]{:S(2)}) async-start(bf16[16,512,128]{2,1,0:T(8,128)(2,1)} %broadcast_in_dim.2), calls=%async_computation | async-start | bytes 4194304 | tf_op jit(solution)/shard_map/all_to_all | solution.py:230
  16.4 13.4 %collective-permute-start.1 = (bf16[128,768]{1,0:T(8,128)(2,1)S(1)}, bf16[128,768]{1,0:T(8,128)(2,1)S(1)}, u32[]{:S(2)}, u32[]{:S(2)}) collective-permute-start(bf16[128,768]{1,0:T(8,128)(2,1)S(1)} %bitcast_dynamic-update-slice_fusion.refs_0_), channel_id=1, source_target_pairs={{0,32},{16,48},{32,64},{48,80},{64,96},{80,112},{96,128},{112,144}... | collective-permute-start | bytes 589832 | tf_op jit(solution)/shard_map/ppermute | solution.py:38
  18.3 13.4 %collective-permute-start.6 = (bf16[128,768]{1,0:T(8,128)(2,1)S(1)}, bf16[128,768]{1,0:T(8,128)(2,1)S(1)}, u32[]{:S(2)}, u32[]{:S(2)}) collective-permute-start(bf16[128,768]{1,0:T(8,128)(2,1)S(1)} %bitcast_dynamic-update-slice_fusion.refs_0_), channel_id=1, source_target_pairs={{0,480},{16,496},{32,0},{48,16},{64,32},{80,48},{96,64},{112,80},{... | collective-permute-start | bytes 589832 | tf_op jit(solution)/shard_map/ppermute | solution.py:38
  29.8 8.3 %collective-permute-start.2 = (bf16[128,768]{1,0:T(8,128)(2,1)S(1)}, bf16[128,768]{1,0:T(8,128)(2,1)S(1)}, u32[]{:S(2)}, u32[]{:S(2)}) collective-permute-start(bf16[128,768]{1,0:T(8,128)(2,1)S(1)} %collective-permute-done.1.refs_1_), channel_id=1, source_target_pairs={{0,32},{16,48},{32,64},{48,80},{64,96},{80,112},{96,128},{112,144}... | collective-permute-start | bytes 589832 | tf_op jit(solution)/shard_map/ppermute | solution.py:38
  31.7 8.3 %collective-permute-start.7 = (bf16[128,768]{1,0:T(8,128)(2,1)S(1)}, bf16[128,768]{1,0:T(8,128)(2,1)S(1)}, u32[]{:S(2)}, u32[]{:S(2)}) collective-permute-start(bf16[128,768]{1,0:T(8,128)(2,1)S(1)} %collective-permute-done.6.refs_2_), channel_id=1, source_target_pairs={{0,480},{16,496},{32,0},{48,16},{64,32},{80,48},{96,64},{112,80},{... | collective-permute-start | bytes 589832 | tf_op jit(solution)/shard_map/ppermute | solution.py:38
  38.1 7.6 %collective-permute-start.3 = (bf16[128,768]{1,0:T(8,128)(2,1)S(1)}, bf16[128,768]{1,0:T(8,128)(2,1)S(1)}, u32[]{:S(2)}, u32[]{:S(2)}) collective-permute-start(bf16[128,768]{1,0:T(8,128)(2,1)S(1)} %collective-permute-done.2.refs_3_), channel_id=1, source_target_pairs={{0,32},{16,48},{32,64},{48,80},{64,96},{80,112},{96,128},{112,144}... | collective-permute-start | bytes 589832 | tf_op jit(solution)/shard_map/ppermute | solution.py:38
  40.0 7.6 %collective-permute-start.8 = (bf16[128,768]{1,0:T(8,128)(2,1)S(1)}, bf16[128,768]{1,0:T(8,128)(2,1)S(1)}, u32[]{:S(2)}, u32[]{:S(2)}) collective-permute-start(bf16[128,768]{1,0:T(8,128)(2,1)S(1)} %collective-permute-done.7.refs_4_), channel_id=1, source_target_pairs={{0,480},{16,496},{32,0},{48,16},{64,32},{80,48},{96,64},{112,80},{... | collective-permute-start | bytes 589832 | tf_op jit(solution)/shard_map/ppermute | solution.py:38
  45.7 7.6 %collective-permute-start.4 = (bf16[128,768]{1,0:T(8,128)(2,1)S(1)}, bf16[128,768]{1,0:T(8,128)(2,1)S(1)}, u32[]{:S(2)}, u32[]{:S(2)}) collective-permute-start(bf16[128,768]{1,0:T(8,128)(2,1)S(1)} %collective-permute-done.3.refs_5_), channel_id=1, source_target_pairs={{0,32},{16,48},{32,64},{48,80},{64,96},{80,112},{96,128},{112,144}... | collective-permute-start | bytes 589832 | tf_op jit(solution)/shard_map/ppermute | solution.py:38
  47.7 8.3 %collective-permute-start.9 = (bf16[128,768]{1,0:T(8,128)(2,1)S(1)}, bf16[128,768]{1,0:T(8,128)(2,1)}, u32[]{:S(2)}, u32[]{:S(2)}) collective-permute-start(bf16[128,768]{1,0:T(8,128)(2,1)S(1)} %collective-permute-done.8.refs_6_), channel_id=1, source_target_pairs={{0,480},{16,496},{32,0},{48,16},{64,32},{80,48},{96,64},{112,80},{... | collective-permute-start | bytes 589832 | tf_op jit(solution)/shard_map/ppermute | solution.py:38
  53.3 7.7 %collective-permute-start.5 = (bf16[128,768]{1,0:T(8,128)(2,1)S(1)}, bf16[128,768]{1,0:T(8,128)(2,1)}, u32[]{:S(2)}, u32[]{:S(2)}) collective-permute-start(bf16[128,768]{1,0:T(8,128)(2,1)S(1)} %collective-permute-done.4.refs_7_), channel_id=1, source_target_pairs={{0,32},{16,48},{32,64},{48,80},{64,96},{80,112},{96,128},{112,144}... | collective-permute-start | bytes 589832 | tf_op jit(solution)/shard_map/ppermute | solution.py:38
  55.9 7.5 %collective-permute-start.10 = (bf16[128,768]{1,0:T(8,128)(2,1)}, bf16[128,768]{1,0:T(8,128)(2,1)}, u32[]{:S(2)}, u32[]{:S(2)}) collective-permute-start(bf16[128,768]{1,0:T(8,128)(2,1)} %collective-permute-done.9.refs_8_), channel_id=1, source_target_pairs={{0,480},{16,496},{32,0},{48,16},{64,32},{80,48},{96,64},{112,80},{... | collective-permute-start | bytes 589832 | tf_op jit(solution)/shard_map/ppermute | solution.py:38
  61.1 10.5 %collective-permute-start.11 = (bf16[128,768]{1,0:T(8,128)(2,1)}, bf16[128,768]{1,0:T(8,128)(2,1)}, u32[]{:S(2)}, u32[]{:S(2)}) collective-permute-start(bf16[128,768]{1,0:T(8,128)(2,1)} %collective-permute-done.5.refs_0_), channel_id=1, source_target_pairs={{0,32},{16,48},{32,64},{48,80},{64,96},{80,112},{96,128},{112,144}... | collective-permute-start | bytes 589832 | tf_op jit(solution)/shard_map/ppermute | solution.py:38
  63.4 10.0 %collective-permute-start.12 = (bf16[128,768]{1,0:T(8,128)(2,1)}, bf16[128,768]{1,0:T(8,128)(2,1)}, u32[]{:S(2)}, u32[]{:S(2)}) collective-permute-start(bf16[128,768]{1,0:T(8,128)(2,1)} %collective-permute-done.10.refs_1_), channel_id=1, source_target_pairs={{0,480},{16,496},{32,0},{48,16},{64,32},{80,48},{96,64},{112,80},{... | collective-permute-start | bytes 589832 | tf_op jit(solution)/shard_map/ppermute | solution.py:38
  71.5 29.1 %copy-start.2 = (f32[2,256]{1,0:T(2,128)S(1)}, f32[2,256]{1,0:T(2,128)}, u32[]{:S(2)}) copy-start(f32[2,256]{1,0:T(2,128)} %decays_ref.1) | copy-start | bytes 6148
  71.5 29.1 %copy-start.4 = (s32[256]{0:T(256)S(1)}, s32[256]{0:T(256)}, u32[]{:S(2)}) copy-start(s32[256]{0:T(256)} %param.13) | copy-start | bytes 3076
  71.5 7.8 %collective-permute-start.13 = (bf16[128,768]{1,0:T(8,128)(2,1)}, bf16[128,768]{1,0:T(8,128)(2,1)S(1)}, u32[]{:S(2)}, u32[]{:S(2)}) collective-permute-start(bf16[128,768]{1,0:T(8,128)(2,1)} %collective-permute-done.11.refs_2_), channel_id=1, source_target_pairs={{0,32},{16,48},{32,64},{48,80},{64,96},{80,112},{96,128},{112,144}... | collective-permute-start | bytes 589832 | tf_op jit(solution)/shard_map/ppermute | solution.py:38
  73.5 7.8 %collective-permute-start.14 = (bf16[128,768]{1,0:T(8,128)(2,1)}, bf16[128,768]{1,0:T(8,128)(2,1)S(1)}, u32[]{:S(2)}, u32[]{:S(2)}) collective-permute-start(bf16[128,768]{1,0:T(8,128)(2,1)} %collective-permute-done.12.refs_3_), channel_id=1, source_target_pairs={{0,480},{16,496},{32,0},{48,16},{64,32},{80,48},{96,64},{112,80},{... | collective-permute-start | bytes 589832 | tf_op jit(solution)/shard_map/ppermute | solution.py:38
  79.4 8.7 %collective-permute-start.15 = (bf16[128,768]{1,0:T(8,128)(2,1)S(1)}, bf16[128,768]{1,0:T(8,128)(2,1)S(1)}, u32[]{:S(2)}, u32[]{:S(2)}) collective-permute-start(bf16[128,768]{1,0:T(8,128)(2,1)S(1)} %collective-permute-done.13.refs_4_), channel_id=1, source_target_pairs={{0,32},{16,48},{32,64},{48,80},{64,96},{80,112},{96,128},{112,144}... | collective-permute-start | bytes 589832 | tf_op jit(solution)/shard_map/ppermute | solution.py:38
  90.3 47.7 %copy-start.5 = (f32[2]{0:T(128)S(1)}, f32[2]{0:T(128)}, u32[]{:S(2)}) copy-start(f32[2]{0:T(128)} %skip_ref.1) | copy-start | bytes 28
  90.3 12.2 %collective-permute-start.16 = (f32[256,768]{1,0:T(8,128)S(1)}, f32[256,768]{1,0:T(8,128)S(1)}, u32[]{:S(2)}, u32[]{:S(2)}) collective-permute-start(f32[256,768]{1,0:T(8,128)S(1)} %get-tuple-element.25), channel_id=1, source_target_pairs={{0,16},{16,0},{32,48},{48,32},{64,80},{80,64},{96,112},{112,96},{1... | collective-permute-start | bytes 2359304 | tf_op jit(solution)/shard_map/ppermute | solution.py:42
  102.9 3.2 %collective-permute-start.17 = (f32[136,128]{1,0:T(8,128)S(1)}, f32[136,128]{1,0:T(8,128)S(1)}, u32[]{:S(2)}, u32[]{:S(2)}) collective-permute-start(f32[136,128]{1,0:T(8,128)S(1)} %get-tuple-element.32), channel_id=1, source_target_pairs={{0,16},{16,0},{32,48},{48,32},{64,80},{80,64},{96,112},{112,96},{1... | collective-permute-start | bytes 208904 | tf_op jit(solution)/shard_map/ppermute | solution.py:42
  128.6 23.9 %copy-start.3 = (f32[2,128]{1,0:T(2,128)S(1)}, f32[2,128]{1,0:T(2,128)}, u32[]{:S(2)}) copy-start(f32[2,128]{1,0:T(2,128)} %param.10) | copy-start | bytes 3076
  128.7 10.2 %collective-permute-start.18 = (f32[128,128]{1,0:T(8,128)S(1)}, f32[128,128]{1,0:T(8,128)S(1)}, u32[]{:S(2)}, u32[]{:S(2)}) collective-permute-start(f32[128,128]{1,0:T(8,128)S(1)} %get-tuple-element.36), channel_id=1, source_target_pairs={{0,16},{16,0},{32,48},{48,32},{64,80},{80,64},{96,112},{112,96},{1... | collective-permute-start | bytes 196616 | tf_op jit(solution)/shard_map/ppermute | solution.py:42
  (4 other events, 9.5 us)

commit v8 on v7

--- a/solution.py
+++ b/solution.py
@@ -104,9 +104,27 @@
     return [got] if n_out == 1 else got
 
 
-def local_kernel(core_ref, own_ref, got_ref, cols_ref, ends_ref, val_ref, maps_ref, keep_ref, send_ref):
-    heads, spare, width = ends_ref.shape
-    n_state = keep_ref.shape[0] - spare
+def three_parts(gates):
+    rows = []
+    for gate in gates:
+        hi = gate.astype(BF16).astype(F32)
+        mid = (gate - hi).astype(BF16).astype(F32)
+        rows += [hi, mid, gate - hi - mid]
+    index = lax.broadcasted_iota(jnp.int32, (16, gates[0].shape[1]), 0)
+    out = jnp.zeros(index.shape, F32)
+    for at, row in enumerate(rows):
+        out = jnp.where(index == at, row, out)
+    return out.astype(BF16)
+
+
+def gate_of(parts, at):
+    parts = parts.astype(F32)
+    return parts[3 * at : 3 * at + 1] + parts[3 * at + 1 : 3 * at + 2] + parts[3 * at + 2 : 3 * at + 3]
+
+
+def local_kernel(own_ref, got_ref, cols_ref, ends_ref, val_ref, maps_ref, state_ref):
+    heads, _, width = ends_ref.shape
+    n_state = maps_ref.shape[1] // 2
     n_val = heads * width
     both = own_ref[:, : n_val + 2 * n_state] + got_ref[:, : n_val + 2 * n_state]
     act = silu(both).astype(BF16)
@@ -114,51 +132,42 @@
     maps = act[:, n_val:]
     val_ref[...] = values
     maps_ref[...] = maps
-    states = []
     for h in range(heads):
         v = values[:, h * width : (h + 1) * width].astype(F32)
         scaled = (cols_ref[:, h : h + 1] * v).astype(BF16)
-        states.append(
-            lax.dot_general(maps[:, :n_state], scaled, TN, preferred_element_type=F32)
-        )
-    even = core_ref[0] == 0
-    keep_ref[:n_state] = jnp.where(even, states[0], states[1])
-    send_ref[:n_state] = jnp.where(even, states[1], states[0])
-    keep_ref[n_state:] = jnp.where(even, ends_ref[0], ends_ref[1])
-    send_ref[n_state:] = jnp.where(even, ends_ref[1], ends_ref[0])
-
-
-def chip_kernel(core_ref, keep_ref, got_ref, first_ref, packed_ref):
-    spare = packed_ref.shape[0] - 16
-    even = core_ref[0] == 0
-    keep, got = keep_ref[...], got_ref[...]
-    first, second = jnp.where(even, keep, got), jnp.where(even, got, keep)
-    first_ref[...] = first
-    s0, g0 = first[:spare], first[spare : spare + 1]
-    s1, g1 = second[:spare], second[spare : spare + 1]
-    packed_ref[:spare] = (g1 * s0 + s1).astype(BF16)
-    gate = jnp.broadcast_to(g0 * g1, (16, s0.shape[1]))
-    hi = gate.astype(BF16).astype(F32)
-    mid = (gate - hi).astype(BF16).astype(F32)
-    low = gate - hi - mid
-    row = lax.broadcasted_iota(jnp.int32, gate.shape, 0)
-    parts = jnp.where(row == 0, hi, jnp.where(row == 1, mid, jnp.where(row == 2, low, 0.0)))
-    packed_ref[spare:] = parts.astype(BF16)
-
-
-def incoming_kernel(core_ref, chip_ref, all_ref, first_ref, keep_ref, give_ref):
-    n_chip, n_state = all_ref.shape[0], keep_ref.shape[0]
-    chip = chip_ref[0]
-    state = jnp.zeros(keep_ref.shape, F32)
-    for z in range(n_chip - 1):
-        parts = all_ref[z, n_state:].astype(F32)
-        gate = parts[0:1] + parts[1:2] + parts[2:3]
-        later = gate * state + all_ref[z, :n_state].astype(F32)
-        state = jnp.where(z < chip, later, state)
-    second = first_ref[n_state : n_state + 1] * state + first_ref[:n_state]
-    even = core_ref[0] == 0
-    keep_ref[...] = jnp.where(even, state, second)
-    give_ref[...] = jnp.where(even, second, state)
+        state = lax.dot_general(maps[:, :n_state], scaled, TN, preferred_element_type=F32)
+        state_ref[h * n_state : (h + 1) * n_state] = state.astype(BF16)
+    state_ref[heads * n_state :] = three_parts([ends_ref[h, 0:1] for h in range(heads)])
+
+
+def quad_kernel(heads, place_ref, quad_ref, out_ref):
+    members, rows = quad_ref.shape[0], quad_ref.shape[1] - 16
+    share = rows // members
+    place = place_ref[0]
+    at = pl.ds(pl.multiple_of(place * share, share), share)
+    state = jnp.zeros((share, quad_ref.shape[2]), F32)
+    kept = jnp.ones((1, quad_ref.shape[2]), F32)
+    for i in range(members):
+        parts = quad_ref[i, rows:]
+        gate = gate_of(parts, 0)
+        for h in range(1, heads):
+            gate = jnp.where(place * heads >= h * members, gate_of(parts, h), gate)
+        state = gate * state + quad_ref[i, at].astype(F32)
+        kept = gate * kept
+    state, parts = state.astype(BF16), three_parts([kept])
+    for p in range(out_ref.shape[0]):
+        out_ref[p, :share] = state
+        out_ref[p, share:] = parts
+
+
+def before_kernel(quad_place_ref, all_ref, out_ref):
+    share = out_ref.shape[0]
+    mine = quad_place_ref[0]
+    state = jnp.zeros(out_ref.shape, F32)
+    for p in range(all_ref.shape[0] - 1):
+        later = gate_of(all_ref[p, share:], 0) * state + all_ref[p, :share].astype(F32)
+        state = jnp.where(p < mine, later, state)
+    out_ref[...] = state
 
 
 def diag_kernel(skip_ref, maps_ref, val_ref, decay_ref, out_ref):
@@ -176,20 +185,24 @@
         out_ref[:, at] = out + skip_ref[h] * v.astype(F32)
 
 
-def gated_kernel(heads, core_ref, diag_ref, kept_ref, came_ref, maps_ref, cols_ref, gate_ref, got_ref, out_ref, sum_ref):
+def gated_kernel(heads, place_ref, diag_ref, quad_ref, before_ref, maps_ref, cols_ref, gate_ref, got_ref, out_ref, sum_ref):
     rows = diag_ref.shape[0]
     width = diag_ref.shape[1] // heads
     n_state = maps_ref.shape[1] // 2
-    core = core_ref[0]
+    place = place_ref[0]
     c_map = maps_ref[:, n_state:]
-    kept, came = kept_ref[...], came_ref[...]
     n_gate = gate_ref.shape[1] - heads * width
     gate = (gate_ref[:, n_gate:] + got_ref[:, n_gate:]).astype(BF16).astype(F32)
     gate = silu(gate)
     total = jnp.zeros((rows, width), F32)
     for h in range(heads):
         at = slice(h * width, (h + 1) * width)
-        state = jnp.where(core == h, kept, came)
+        here = slice(h * n_state, (h + 1) * n_state)
+        state = before_ref[here]
+        for i in range(quad_ref.shape[0] - 1):
+            gate_i = gate_of(quad_ref[i, heads * n_state :], h)
+            later = gate_i * state + quad_ref[i, here].astype(F32)
+            state = jnp.where(i < place, later, state)
         hi = state.astype(BF16)
         lo = (state - hi.astype(F32)).astype(BF16)
         off = jnp.dot(c_map, hi, preferred_element_type=F32)
@@ -218,8 +231,7 @@
     n_chip = n_ctx // 2
     ctx = lax.axis_index("ctx")
     core, chip = ctx % 2, ctx // 2
-    same_core = [[2 * z + c for z in range(n_chip)] for c in range(2)]
-    core_1, chip_1 = core.reshape(1), chip.reshape(1)
+    chip_1 = chip.reshape(1)
 
     def mine_other(a, b):
         return jnp.where(core == 0, a, b), jnp.where(core == 0, b, a)
@@ -259,41 +271,43 @@
     own, other = partial_product(2, steps, chip_1, tok, blocks, acc)
     got = swap_cores(other)
 
-    state = ((n_state + 8, width), F32)
-    values, maps, keep, send = call(
+    place, quad_place = (ctx % 4).reshape(1), (ctx // 4).reshape(1)
+    n_quad = n_ctx // 4
+    quads = [[4 * p + q for q in range(4)] for p in range(n_quad)]
+    across = [[4 * p + q for p in range(n_quad)] for q in range(4)]
+    values, maps, state = call(
         local_kernel,
-        [((rows, n_val), BF16), ((rows, 2 * n_state), BF16), state, state],
-        core_1,
+        [
+            ((rows, n_val), BF16),
+            ((rows, 2 * n_state), BF16),
+            ((heads * n_state + 16, width), BF16),
+        ],
         own,
         got,
         cols,
         ends,
+    )
+    quad = lax.all_gather(state, "ctx", axis=0, axis_index_groups=quads)
+    share = heads * n_state // 4
+    totals = call(
+        functools.partial(quad_kernel, heads),
+        [((n_quad, share + 16, width), BF16)],
+        place,
+        quad,
         smem=1,
     )
-    came = swap_cores(send)
+    totals = lax.all_to_all(totals, "ctx", 0, 0, axis_index_groups=across)
     diag = call(diag_kernel, [((rows, n_val), F32)], skip, maps, values, decay, smem=1)
-    first, packed = call(
-        chip_kernel, [state, ((n_state + 16, width), BF16)], core_1, keep, came, smem=1
-    )
-    everyone = lax.all_gather(packed, "ctx", axis=0, axis_index_groups=same_core)
-    kept, give = call(
-        incoming_kernel,
-        [((n_state, width), F32)] * 2,
-        core_1,
-        chip_1,
-        everyone,
-        first,
-        smem=2,
-    )
-    came = swap_cores(give)
+    before = call(before_kernel, [((share, width), F32)], quad_place, totals, smem=1)
+    before = lax.all_gather(before, "ctx", axis=0, tiled=True, axis_index_groups=quads)
 
     gated, sums = call(
         functools.partial(gated_kernel, heads),
         [((rows, heads * width), F32), ((n_fsdp, rows), F32)],
-        core_1,
+        place,
         diag,
-        kept,
-        came,
+        quad,
+        before,
         maps,
         cols,
         own,

time: 154 us -> 158 us (1.026)
  waiting for transfers between devices: 18 us -> 31.2 us
  blocking collectives: 35.5 us -> 27.6 us
  starting transfers between devices: 86.7 us -> 83.3 us
    all_to_all x0 -> x1, waiting for transfers between devices: none -> 13.8 us  [per_device(): totals = lax.all_to_all(totals, 'ctx', 0, 0, axis_index_groups=across)]
    ppermute x4 -> x2, starting transfers between devices: 30.6 us -> 19.2 us  [swap_cores(): lax.ppermute(x, 'ctx', [(i, i ^ 1) for i in range(lax.axis_size('ctx'))])]
    all_gather x1 -> x2, blocking collectives: 22.5 us -> 14.4 us  [the longest x1 8.33 us: per_device(): lax.all_gather(before, 'ctx', axis=0, tiled=True, axis_index_groups=quads)]
    all_to_all x0 -> x1, starting transfers between devices: none -> 7.97 us  [per_device(): totals = lax.all_to_all(totals, 'ctx', 0, 0, axis_index_groups=across)]
  transfers between devices with their start and end apart: 20 -> 19, of which waited for: 11 -> 11; matrix products, arithmetic and copies ran while one was open for 0% -> 0% of each run, Pallas kernels for 3% -> 3%
where the time goes in v8:
time: 158 us; the launch traced here: 157 us
  starting transfers between devices  83.3 us (53%)
  waiting for transfers between devices  31.2 us (20%)
  blocking collectives  27.6 us (17%)
  Pallas kernels  9.19 us (6%)
  local copies, waits for them, and re-layouts  4.27 us (3%)
    ppermute x15, starting transfers between devices, shift(): return lax.ppermute(x, 'ctx', [(i, (i + by) % n) for i in range(n)])  52.2 us
    ppermute x2, starting transfers between devices, swap_cores(): lax.ppermute(x, 'ctx', [(i, i ^ 1) for i in range(lax.axis_size('ctx'))])  19.2 us
    ppermute x15, waiting for transfers between devices, shift(): return lax.ppermute(x, 'ctx', [(i, (i + by) % n) for i in range(n)])  15.5 us
    all_to_all x1, waiting for transfers between devices, per_device(): totals = lax.all_to_all(totals, 'ctx', 0, 0, axis_index_groups=across)  13.8 us
    all_to_all x1, blocking collectives, per_device(): sums = lax.all_to_all(sums, 'fsdp', 0, 0, tiled=True)  13.2 us
    pallas_call x9, Pallas kernels, call(): pl.pallas_call(kernel, out_shape=shapes, in_specs=[SMEM] * smem + [VMEM]...  9.19 us
    all_gather x1, blocking collectives, per_device(): lax.all_gather(before, 'ctx', axis=0, tiled=True, axis_index_groups=quads)  8.33 us
    all_to_all x1, starting transfers between devices, per_device(): totals = lax.all_to_all(totals, 'ctx', 0, 0, axis_index_groups=across)  7.97 us
  transfers between devices with their start and end apart: 19, of which 11 were waited for; matrix products, arithmetic and copies ran while one was open for 0% of the time, Pallas kernels for 3%

profile of v8, /device:TPU:1, one launch (start us, length us, event | category | flops | bytes accessed | tf_op | source)
XLA Modules:
  0.0 156.8 jit_solution(10815183603305810183)
XLA Ops:
  0.9 8.8 %collective-permute-start = (bf16[256,128]{1,0:T(8,128)(2,1)S(1)}, bf16[256,128]{1,0:T(8,128)(2,1)S(1)}, u32[]{:S(2)}, u32[]{:S(2)}) collective-permute-start(bf16[256,128]{1,0:T(8,128)(2,1)S(1)} %get-tuple-element.32), channel_id=1, source_target_pairs={{0,16},{16,0},{32,48},{48,32},{64,80},{80,64},{96,112},{112,96},{1... | collective-permute-start | bytes 196616 | tf_op jit(solution)/shard_map/ppermute | solution.py:42
  12.3 3.8 %all-to-all-start = ((bf16[16,512,128]{2,1,0:T(8,128)(2,1)}), bf16[16,512,128]{2,1,0:T(8,128)(2,1)S(1)}, u32[]{:S(2)}, u32[]{:S(2)}) async-start(bf16[16,512,128]{2,1,0:T(8,128)(2,1)} %broadcast_in_dim.2), calls=%async_computation | async-start | bytes 4194304 | tf_op jit(solution)/shard_map/all_to_all | solution.py:242
  16.4 1.9 %collective-permute-start.1 = (bf16[128,768]{1,0:T(8,128)(2,1)S(1)}, bf16[128,768]{1,0:T(8,128)(2,1)S(1)}, u32[]{:S(2)}, u32[]{:S(2)}) collective-permute-start(bf16[128,768]{1,0:T(8,128)(2,1)S(1)} %bitcast_dynamic-update-slice_fusion.refs_0_), channel_id=1, source_target_pairs={{0,32},{16,48},{32,64},{48,80},{64,96},{80,112},{96,128},{112,144}... | collective-permute-start | bytes 589832 | tf_op jit(solution)/shard_map/ppermute | solution.py:38
  18.3 8.8 %collective-permute-start.6 = (bf16[128,768]{1,0:T(8,128)(2,1)S(1)}, bf16[128,768]{1,0:T(8,128)(2,1)S(1)}, u32[]{:S(2)}, u32[]{:S(2)}) collective-permute-start(bf16[128,768]{1,0:T(8,128)(2,1)S(1)} %bitcast_dynamic-update-slice_fusion.refs_0_), channel_id=1, source_target_pairs={{0,480},{16,496},{32,0},{48,16},{64,32},{80,48},{96,64},{112,80},{... | collective-permute-start | bytes 589832 | tf_op jit(solution)/shard_map/ppermute | solution.py:38
  27.1 2.7 %collective-permute-done.1.refs_1_ = bf16[128,768]{1,0:T(8,128)(2,1)S(1)} collective-permute-done((bf16[128,768]{1,0:T(8,128)(2,1)S(1)}, bf16[128,768]{1,0:T(8,128)(2,1)S(1)}, u32[]{:S(2)}, u32[]{:S(2)}) %collective-permute-start.1) | collective-permute-done | bytes 196640 | tf_op jit(solution)/shard_map/ppermute | solution.py:38
  31.7 4.6 %collective-permute-start.7 = (bf16[128,768]{1,0:T(8,128)(2,1)S(1)}, bf16[128,768]{1,0:T(8,128)(2,1)S(1)}, u32[]{:S(2)}, u32[]{:S(2)}) collective-permute-start(bf16[128,768]{1,0:T(8,128)(2,1)S(1)} %collective-permute-done.6.refs_2_), channel_id=1, source_target_pairs={{0,480},{16,496},{32,0},{48,16},{64,32},{80,48},{96,64},{112,80},{... | collective-permute-start | bytes 589832 | tf_op jit(solution)/shard_map/ppermute | solution.py:38
  40.0 4.6 %collective-permute-start.8 = (bf16[128,768]{1,0:T(8,128)(2,1)S(1)}, bf16[128,768]{1,0:T(8,128)(2,1)S(1)}, u32[]{:S(2)}, u32[]{:S(2)}) collective-permute-start(bf16[128,768]{1,0:T(8,128)(2,1)S(1)} %collective-permute-done.7.refs_4_), channel_id=1, source_target_pairs={{0,480},{16,496},{32,0},{48,16},{64,32},{80,48},{96,64},{112,80},{... | collective-permute-start | bytes 589832 | tf_op jit(solution)/shard_map/ppermute | solution.py:38
  45.7 1.9 %collective-permute-start.4 = (bf16[128,768]{1,0:T(8,128)(2,1)S(1)}, bf16[128,768]{1,0:T(8,128)(2,1)S(1)}, u32[]{:S(2)}, u32[]{:S(2)}) collective-permute-start(bf16[128,768]{1,0:T(8,128)(2,1)S(1)} %collective-permute-done.3.refs_5_), channel_id=1, source_target_pairs={{0,32},{16,48},{32,64},{48,80},{64,96},{80,112},{96,128},{112,144}... | collective-permute-start | bytes 589832 | tf_op jit(solution)/shard_map/ppermute | solution.py:38
  47.7 4.9 %collective-permute-start.9 = (bf16[128,768]{1,0:T(8,128)(2,1)S(1)}, bf16[128,768]{1,0:T(8,128)(2,1)}, u32[]{:S(2)}, u32[]{:S(2)}) collective-permute-start(bf16[128,768]{1,0:T(8,128)(2,1)S(1)} %collective-permute-done.8.refs_6_), channel_id=1, source_target_pairs={{0,480},{16,496},{32,0},{48,16},{64,32},{80,48},{96,64},{112,80},{... | collective-permute-start | bytes 589832 | tf_op jit(solution)/shard_map/ppermute | solution.py:38
  53.3 1.9 %collective-permute-start.5 = (bf16[128,768]{1,0:T(8,128)(2,1)S(1)}, bf16[128,768]{1,0:T(8,128)(2,1)}, u32[]{:S(2)}, u32[]{:S(2)}) collective-permute-start(bf16[128,768]{1,0:T(8,128)(2,1)S(1)} %collective-permute-done.4.refs_7_), channel_id=1, source_target_pairs={{0,32},{16,48},{32,64},{48,80},{64,96},{80,112},{96,128},{112,144}... | collective-permute-start | bytes 589832 | tf_op jit(solution)/shard_map/ppermute | solution.py:38
  56.0 4.6 %collective-permute-start.10 = (bf16[128,768]{1,0:T(8,128)(2,1)}, bf16[128,768]{1,0:T(8,128)(2,1)}, u32[]{:S(2)}, u32[]{:S(2)}) collective-permute-start(bf16[128,768]{1,0:T(8,128)(2,1)} %collective-permute-done.9.refs_8_), channel_id=1, source_target_pairs={{0,480},{16,496},{32,0},{48,16},{64,32},{80,48},{96,64},{112,80},{... | collective-permute-start | bytes 589832 | tf_op jit(solution)/shard_map/ppermute | solution.py:38
  61.1 1.9 %collective-permute-start.11 = (bf16[128,768]{1,0:T(8,128)(2,1)}, bf16[128,768]{1,0:T(8,128)(2,1)}, u32[]{:S(2)}, u32[]{:S(2)}) collective-permute-start(bf16[128,768]{1,0:T(8,128)(2,1)} %collective-permute-done.5.refs_0_), channel_id=1, source_target_pairs={{0,32},{16,48},{32,64},{48,80},{64,96},{80,112},{96,128},{112,144}... | collective-permute-start | bytes 589832 | tf_op jit(solution)/shard_map/ppermute | solution.py:38
  63.4 5.0 %collective-permute-start.12 = (bf16[128,768]{1,0:T(8,128)(2,1)}, bf16[128,768]{1,0:T(8,128)(2,1)}, u32[]{:S(2)}, u32[]{:S(2)}) collective-permute-start(bf16[128,768]{1,0:T(8,128)(2,1)} %collective-permute-done.10.refs_1_), channel_id=1, source_target_pairs={{0,480},{16,496},{32,0},{48,16},{64,32},{80,48},{96,64},{112,80},{... | collective-permute-start | bytes 589832 | tf_op jit(solution)/shard_map/ppermute | solution.py:38
  69.4 2.1 %shard_map.73.refs_7_ = f32[512,768]{1,0:T(8,128)S(1)} custom-call(s32[1]{0:T(128)} %bitcast.1.chip_ref, bf16[16,512,128]{2,1,0:T(8,128)(2,1)S(1)} %all-to-all-done.tok_ref, bf16[128,768]{1,0:T(8,128)(2,1)S(1)} %bitcast_dynamic-update-slice_fusion.refs_0_, bf16[128,768]{1,0:T(8,128)(2,1)S(1)} %collective-permute-done.1.refs_1_, ...), custom_call_target="tpu_custom_call" | custom-call | tf_op jit(solution)/shard_map/pallas_call | solution.py:22
  71.5 1.9 %collective-permute-start.13 = (bf16[128,768]{1,0:T(8,128)(2,1)}, bf16[128,768]{1,0:T(8,128)(2,1)S(1)}, u32[]{:S(2)}, u32[]{:S(2)}) collective-permute-start(bf16[128,768]{1,0:T(8,128)(2,1)} %collective-permute-done.11.refs_2_), channel_id=1, source_target_pairs={{0,32},{16,48},{32,64},{48,80},{64,96},{80,112},{96,128},{112,144}... | collective-permute-start | bytes 589832 | tf_op jit(solution)/shard_map/ppermute | solution.py:38
  73.5 4.6 %collective-permute-start.14 = (bf16[128,768]{1,0:T(8,128)(2,1)}, bf16[128,768]{1,0:T(8,128)(2,1)S(1)}, u32[]{:S(2)}, u32[]{:S(2)}) collective-permute-start(bf16[128,768]{1,0:T(8,128)(2,1)} %collective-permute-done.12.refs_3_), channel_id=1, source_target_pairs={{0,480},{16,496},{32,0},{48,16},{64,32},{80,48},{96,64},{112,80},{... | collective-permute-start | bytes 589832 | tf_op jit(solution)/shard_map/ppermute | solution.py:38
  81.3 6.8 %collective-permute-done.15.refs_6_ = bf16[128,768]{1,0:T(8,128)(2,1)S(1)} collective-permute-done((bf16[128,768]{1,0:T(8,128)(2,1)S(1)}, bf16[128,768]{1,0:T(8,128)(2,1)S(1)}, u32[]{:S(2)}, u32[]{:S(2)}) %collective-permute-start.15) | collective-permute-done | bytes 196640 | tf_op jit(solution)/shard_map/ppermute | solution.py:38
  88.1 3.1 %shard_map.74 = (f32[256,768]{1,0:T(8,128)S(1)}, f32[256,768]{1,0:T(8,128)}) custom-call(s32[1]{0:T(128)} %bitcast.1.chip_ref, bf16[16,512,128]{2,1,0:T(8,128)(2,1)S(1)} %all-to-all-done.tok_ref, bf16[128,768]{1,0:T(8,128)(2,1)} %collective-permute-done.5.refs_0_, bf16[128,768]{1,0:T(8,128)(2,1)} %collective-permute-done.10.refs_1_, ...), custom_call_target="tpu_custom_call" | custom-call | tf_op jit(solution)/shard_map/pallas_call | solution.py:22
  91.2 10.4 %collective-permute-start.16 = (f32[256,768]{1,0:T(8,128)}, f32[256,768]{1,0:T(8,128)S(1)}, u32[]{:S(2)}, u32[]{:S(2)}) collective-permute-start(f32[256,768]{1,0:T(8,128)} %get-tuple-element.20), channel_id=1, source_target_pairs={{0,16},{16,0},{32,48},{48,32},{64,80},{80,64},{96,112},{112,96},{1... | collective-permute-start | bytes 2359304 | tf_op jit(solution)/shard_map/ppermute | solution.py:42
  104.1 6.0 %all-gather = bf16[1088,128]{1,0:T(8,128)(2,1)S(1)} all-gather(bf16[272,128]{1,0:T(8,128)(2,1)S(1)} %get-tuple-element.26), channel_id=2, replica_groups={{0,16,32,48},{64,80,96,112},{128,144,160,176},{192,208,224,240},{256,27..., dimensions={0}, use_global_device_ids=true | all-gather | bytes 348160 | tf_op jit(solution)/shard_map/all_gather | solution.py:290
  110.8 8.0 %all-to-all-start.1 = ((bf16[8,80,128]{2,1,0:T(8,128)(2,1)}), bf16[8,80,128]{2,1,0:T(8,128)(2,1)S(1)}, u32[]{:S(2)}, u32[]{:S(2)}) async-start(bf16[8,80,128]{2,1,0:T(8,128)(2,1)} %shard_map.78), calls=%async_computation.1 | async-start | bytes 327680 | tf_op jit(solution)/shard_map/all_to_all | solution.py:299
  119.7 13.8 %all-to-all-done.1.all_ref = bf16[8,80,128]{2,1,0:T(8,128)(2,1)S(1)} async-done(((bf16[8,80,128]{2,1,0:T(8,128)(2,1)}), bf16[8,80,128]{2,1,0:T(8,128)(2,1)S(1)}, u32[]{:S(2)}, u32[]{:S(2)}) %all-to-all-start.1) | async-done | bytes 163872 | tf_op jit(solution)/shard_map/all_to_all | solution.py:299
  133.6 8.3 %all_gather.11.before_ref = f32[256,128]{1,0:T(8,128)S(1)} all-gather(f32[64,128]{1,0:T(8,128)S(1)} %shard_map.79), channel_id=1, replica_groups={{0,16,32,48},{64,80,96,112},{128,144,160,176},{192,208,224,240},{256,27..., dimensions={0}, use_global_device_ids=true | all-gather | bytes 163840 | tf_op jit(solution)/shard_map/all_gather | solution.py:302
  142.5 13.2 %all_to_all.21 = f32[16,1,256]{2,1,0:T(1,128)S(1)} all-to-all(f32[16,1,256]{2,1,0:T(1,128)S(1)} %copy.8), channel_id=1, replica_groups=mesh['ctx'=32,'fsdp'=16] {'fsdp'}, dimensions={0} | all-to-all | bytes 32768 | tf_op jit(solution)/shard_map/all_to_all | solution.py:317
  (52 shorter events, 22.7 us)
Async XLA Ops:
  0.9 9.7 %collective-permute-start = (bf16[256,128]{1,0:T(8,128)(2,1)S(1)}, bf16[256,128]{1,0:T(8,128)(2,1)S(1)}, u32[]{:S(2)}, u32[]{:S(2)}) collective-permute-start(bf16[256,128]{1,0:T(8,128)(2,1)S(1)} %get-tuple-element.32), channel_id=1, source_target_pairs={{0,16},{16,0},{32,48},{48,32},{64,80},{80,64},{96,112},{112,96},{1... | collective-permute-start | bytes 196616 | tf_op jit(solution)/shard_map/ppermute | solution.py:42
  12.3 4.0 %copy-start.7 = (bf16[128,256]{1,0:T(8,128)(2,1)S(1)}, bf16[128,256]{1,0:T(8,128)(2,1)}, u32[]{:S(2)}) copy-start(bf16[128,256]{1,0:T(8,128)(2,1)} %param.9) | copy-start | bytes 196612
  12.3 56.1 %all-to-all-start = ((bf16[16,512,128]{2,1,0:T(8,128)(2,1)}), bf16[16,512,128]{2,1,0:T(8,128)(2,1)S(1)}, u32[]{:S(2)}, u32[]{:S(2)}) async-start(bf16[16,512,128]{2,1,0:T(8,128)(2,1)} %broadcast_in_dim.2), calls=%async_computation | async-start | bytes 4194304 | tf_op jit(solution)/shard_map/all_to_all | solution.py:242
  16.4 13.4 %collective-permute-start.1 = (bf16[128,768]{1,0:T(8,128)(2,1)S(1)}, bf16[128,768]{1,0:T(8,128)(2,1)S(1)}, u32[]{:S(2)}, u32[]{:S(2)}) collective-permute-start(bf16[128,768]{1,0:T(8,128)(2,1)S(1)} %bitcast_dynamic-update-slice_fusion.refs_0_), channel_id=1, source_target_pairs={{0,32},{16,48},{32,64},{48,80},{64,96},{80,112},{96,128},{112,144}... | collective-permute-start | bytes 589832 | tf_op jit(solution)/shard_map/ppermute | solution.py:38
  18.3 13.4 %collective-permute-start.6 = (bf16[128,768]{1,0:T(8,128)(2,1)S(1)}, bf16[128,768]{1,0:T(8,128)(2,1)S(1)}, u32[]{:S(2)}, u32[]{:S(2)}) collective-permute-start(bf16[128,768]{1,0:T(8,128)(2,1)S(1)} %bitcast_dynamic-update-slice_fusion.refs_0_), channel_id=1, source_target_pairs={{0,480},{16,496},{32,0},{48,16},{64,32},{80,48},{96,64},{112,80},{... | collective-permute-start | bytes 589832 | tf_op jit(solution)/shard_map/ppermute | solution.py:38
  29.8 8.3 %collective-permute-start.2 = (bf16[128,768]{1,0:T(8,128)(2,1)S(1)}, bf16[128,768]{1,0:T(8,128)(2,1)S(1)}, u32[]{:S(2)}, u32[]{:S(2)}) collective-permute-start(bf16[128,768]{1,0:T(8,128)(2,1)S(1)} %collective-permute-done.1.refs_1_), channel_id=1, source_target_pairs={{0,32},{16,48},{32,64},{48,80},{64,96},{80,112},{96,128},{112,144}... | collective-permute-start | bytes 589832 | tf_op jit(solution)/shard_map/ppermute | solution.py:38
  31.7 8.3 %collective-permute-start.7 = (bf16[128,768]{1,0:T(8,128)(2,1)S(1)}, bf16[128,768]{1,0:T(8,128)(2,1)S(1)}, u32[]{:S(2)}, u32[]{:S(2)}) collective-permute-start(bf16[128,768]{1,0:T(8,128)(2,1)S(1)} %collective-permute-done.6.refs_2_), channel_id=1, source_target_pairs={{0,480},{16,496},{32,0},{48,16},{64,32},{80,48},{96,64},{112,80},{... | collective-permute-start | bytes 589832 | tf_op jit(solution)/shard_map/ppermute | solution.py:38
  38.1 7.6 %collective-permute-start.3 = (bf16[128,768]{1,0:T(8,128)(2,1)S(1)}, bf16[128,768]{1,0:T(8,128)(2,1)S(1)}, u32[]{:S(2)}, u32[]{:S(2)}) collective-permute-start(bf16[128,768]{1,0:T(8,128)(2,1)S(1)} %collective-permute-done.2.refs_3_), channel_id=1, source_target_pairs={{0,32},{16,48},{32,64},{48,80},{64,96},{80,112},{96,128},{112,144}... | collective-permute-start | bytes 589832 | tf_op jit(solution)/shard_map/ppermute | solution.py:38
  40.0 7.6 %collective-permute-start.8 = (bf16[128,768]{1,0:T(8,128)(2,1)S(1)}, bf16[128,768]{1,0:T(8,128)(2,1)S(1)}, u32[]{:S(2)}, u32[]{:S(2)}) collective-permute-start(bf16[128,768]{1,0:T(8,128)(2,1)S(1)} %collective-permute-done.7.refs_4_), channel_id=1, source_target_pairs={{0,480},{16,496},{32,0},{48,16},{64,32},{80,48},{96,64},{112,80},{... | collective-permute-start | bytes 589832 | tf_op jit(solution)/shard_map/ppermute | solution.py:38
  45.7 7.6 %collective-permute-start.4 = (bf16[128,768]{1,0:T(8,128)(2,1)S(1)}, bf16[128,768]{1,0:T(8,128)(2,1)S(1)}, u32[]{:S(2)}, u32[]{:S(2)}) collective-permute-start(bf16[128,768]{1,0:T(8,128)(2,1)S(1)} %collective-permute-done.3.refs_5_), channel_id=1, source_target_pairs={{0,32},{16,48},{32,64},{48,80},{64,96},{80,112},{96,128},{112,144}... | collective-permute-start | bytes 589832 | tf_op jit(solution)/shard_map/ppermute | solution.py:38
  47.7 8.3 %collective-permute-start.9 = (bf16[128,768]{1,0:T(8,128)(2,1)S(1)}, bf16[128,768]{1,0:T(8,128)(2,1)}, u32[]{:S(2)}, u32[]{:S(2)}) collective-permute-start(bf16[128,768]{1,0:T(8,128)(2,1)S(1)} %collective-permute-done.8.refs_6_), channel_id=1, source_target_pairs={{0,480},{16,496},{32,0},{48,16},{64,32},{80,48},{96,64},{112,80},{... | collective-permute-start | bytes 589832 | tf_op jit(solution)/shard_map/ppermute | solution.py:38
  53.3 7.7 %collective-permute-start.5 = (bf16[128,768]{1,0:T(8,128)(2,1)S(1)}, bf16[128,768]{1,0:T(8,128)(2,1)}, u32[]{:S(2)}, u32[]{:S(2)}) collective-permute-start(bf16[128,768]{1,0:T(8,128)(2,1)S(1)} %collective-permute-done.4.refs_7_), channel_id=1, source_target_pairs={{0,32},{16,48},{32,64},{48,80},{64,96},{80,112},{96,128},{112,144}... | collective-permute-start | bytes 589832 | tf_op jit(solution)/shard_map/ppermute | solution.py:38
  56.0 7.5 %collective-permute-start.10 = (bf16[128,768]{1,0:T(8,128)(2,1)}, bf16[128,768]{1,0:T(8,128)(2,1)}, u32[]{:S(2)}, u32[]{:S(2)}) collective-permute-start(bf16[128,768]{1,0:T(8,128)(2,1)} %collective-permute-done.9.refs_8_), channel_id=1, source_target_pairs={{0,480},{16,496},{32,0},{48,16},{64,32},{80,48},{96,64},{112,80},{... | collective-permute-start | bytes 589832 | tf_op jit(solution)/shard_map/ppermute | solution.py:38
  61.1 10.5 %collective-permute-start.11 = (bf16[128,768]{1,0:T(8,128)(2,1)}, bf16[128,768]{1,0:T(8,128)(2,1)}, u32[]{:S(2)}, u32[]{:S(2)}) collective-permute-start(bf16[128,768]{1,0:T(8,128)(2,1)} %collective-permute-done.5.refs_0_), channel_id=1, source_target_pairs={{0,32},{16,48},{32,64},{48,80},{64,96},{80,112},{96,128},{112,144}... | collective-permute-start | bytes 589832 | tf_op jit(solution)/shard_map/ppermute | solution.py:38
  63.4 10.0 %collective-permute-start.12 = (bf16[128,768]{1,0:T(8,128)(2,1)}, bf16[128,768]{1,0:T(8,128)(2,1)}, u32[]{:S(2)}, u32[]{:S(2)}) collective-permute-start(bf16[128,768]{1,0:T(8,128)(2,1)} %collective-permute-done.10.refs_1_), channel_id=1, source_target_pairs={{0,480},{16,496},{32,0},{48,16},{64,32},{80,48},{96,64},{112,80},{... | collective-permute-start | bytes 589832 | tf_op jit(solution)/shard_map/ppermute | solution.py:38
  71.5 30.1 %copy-start.2 = (f32[2,256]{1,0:T(2,128)S(1)}, f32[2,256]{1,0:T(2,128)}, u32[]{:S(2)}) copy-start(f32[2,256]{1,0:T(2,128)} %decays_ref.1) | copy-start | bytes 6148
  71.5 30.1 %copy-start.4 = (s32[256]{0:T(256)S(1)}, s32[256]{0:T(256)}, u32[]{:S(2)}) copy-start(s32[256]{0:T(256)} %param.13) | copy-start | bytes 3076
  71.5 7.8 %collective-permute-start.13 = (bf16[128,768]{1,0:T(8,128)(2,1)}, bf16[128,768]{1,0:T(8,128)(2,1)S(1)}, u32[]{:S(2)}, u32[]{:S(2)}) collective-permute-start(bf16[128,768]{1,0:T(8,128)(2,1)} %collective-permute-done.11.refs_2_), channel_id=1, source_target_pairs={{0,32},{16,48},{32,64},{48,80},{64,96},{80,112},{96,128},{112,144}... | collective-permute-start | bytes 589832 | tf_op jit(solution)/shard_map/ppermute | solution.py:38
  73.5 7.8 %collective-permute-start.14 = (bf16[128,768]{1,0:T(8,128)(2,1)}, bf16[128,768]{1,0:T(8,128)(2,1)S(1)}, u32[]{:S(2)}, u32[]{:S(2)}) collective-permute-start(bf16[128,768]{1,0:T(8,128)(2,1)} %collective-permute-done.12.refs_3_), channel_id=1, source_target_pairs={{0,480},{16,496},{32,0},{48,16},{64,32},{80,48},{96,64},{112,80},{... | collective-permute-start | bytes 589832 | tf_op jit(solution)/shard_map/ppermute | solution.py:38
  79.4 8.7 %collective-permute-start.15 = (bf16[128,768]{1,0:T(8,128)(2,1)S(1)}, bf16[128,768]{1,0:T(8,128)(2,1)S(1)}, u32[]{:S(2)}, u32[]{:S(2)}) collective-permute-start(bf16[128,768]{1,0:T(8,128)(2,1)S(1)} %collective-permute-done.13.refs_4_), channel_id=1, source_target_pairs={{0,32},{16,48},{32,64},{48,80},{64,96},{80,112},{96,128},{112,144}... | collective-permute-start | bytes 589832 | tf_op jit(solution)/shard_map/ppermute | solution.py:38
  91.2 27.6 %copy-start.5 = (f32[2]{0:T(128)S(1)}, f32[2]{0:T(128)}, u32[]{:S(2)}) copy-start(f32[2]{0:T(128)} %skip_ref.1) | copy-start | bytes 28
  91.2 12.5 %collective-permute-start.16 = (f32[256,768]{1,0:T(8,128)}, f32[256,768]{1,0:T(8,128)S(1)}, u32[]{:S(2)}, u32[]{:S(2)}) collective-permute-start(f32[256,768]{1,0:T(8,128)} %get-tuple-element.20), channel_id=1, source_target_pairs={{0,16},{16,0},{32,48},{48,32},{64,80},{80,64},{96,112},{112,96},{1... | collective-permute-start | bytes 2359304 | tf_op jit(solution)/shard_map/ppermute | solution.py:42
  110.8 22.8 %all-to-all-start.1 = ((bf16[8,80,128]{2,1,0:T(8,128)(2,1)}), bf16[8,80,128]{2,1,0:T(8,128)(2,1)S(1)}, u32[]{:S(2)}, u32[]{:S(2)}) async-start(bf16[8,80,128]{2,1,0:T(8,128)(2,1)} %shard_map.78), calls=%async_computation.1 | async-start | bytes 327680 | tf_op jit(solution)/shard_map/all_to_all | solution.py:299
  118.8 36.9 %copy-start.3 = (f32[2,128]{1,0:T(2,128)S(1)}, f32[2,128]{1,0:T(2,128)}, u32[]{:S(2)}) copy-start(f32[2,128]{1,0:T(2,128)} %param.10) | copy-start | bytes 3076
  (3 other events, 5.5 us)

commit v9 on v8

--- a/solution.py
+++ b/solution.py
@@ -86,22 +86,24 @@
     if len(outs) == 1:
         outs[0][...] = acc
     else:
-        outs[0][...] = acc[: rows // 2]
-        outs[1][...] = acc[rows // 2 :]
-
-
-def partial_product(n_out, steps, chip, tok, blocks, acc):
-    shape = (tok.shape[1] // n_out, blocks[0].shape[1])
+        edge = outs[0].shape[1]
+        outs[0][...] = acc[: rows // 2, :edge]
+        outs[1][...] = acc[rows // 2 :, :edge]
+        outs[2][...] = acc[: rows // 2, edge:]
+        outs[3][...] = acc[rows // 2 :, edge:]
+
+
+def partial_product(shapes, steps, chip, tok, blocks, acc):
     got = call(
         functools.partial(partial_kernel, steps, len(acc)),
-        [(shape, F32)] * n_out,
+        [(shape, F32) for shape in shapes],
         chip,
         tok,
         *blocks,
         *acc,
         smem=1,
     )
-    return [got] if n_out == 1 else got
+    return [got] if len(shapes) == 1 else got
 
 
 def three_parts(gates):
@@ -126,8 +128,7 @@
     heads, _, width = ends_ref.shape
     n_state = maps_ref.shape[1] // 2
     n_val = heads * width
-    both = own_ref[:, : n_val + 2 * n_state] + got_ref[:, : n_val + 2 * n_state]
-    act = silu(both).astype(BF16)
+    act = silu(own_ref[...] + got_ref[...]).astype(BF16)
     values = act[:, :n_val]
     maps = act[:, n_val:]
     val_ref[...] = values
@@ -191,8 +192,7 @@
     n_state = maps_ref.shape[1] // 2
     place = place_ref[0]
     c_map = maps_ref[:, n_state:]
-    n_gate = gate_ref.shape[1] - heads * width
-    gate = (gate_ref[:, n_gate:] + got_ref[:, n_gate:]).astype(BF16).astype(F32)
+    gate = (gate_ref[...] + got_ref[...]).astype(BF16).astype(F32)
     gate = silu(gate)
     total = jnp.zeros((rows, width), F32)
     for h in range(heads):
@@ -266,9 +266,11 @@
             steps.append(-s)
             blocks.append(down)
         if s == half - 4:
-            acc = partial_product(1, steps, chip_1, tok, blocks, acc)
+            acc = partial_product([(2 * rows, block.shape[1])], steps, chip_1, tok, blocks, acc)
             steps, blocks = [], []
-    own, other = partial_product(2, steps, chip_1, tok, blocks, acc)
+    n_first = n_val + 2 * n_state
+    shapes = [(rows, n_first)] * 2 + [(rows, n_val)] * 2
+    own, other, gate_own, gate_other = partial_product(shapes, steps, chip_1, tok, blocks, acc)
     got = swap_cores(other)
 
     place, quad_place = (ctx % 4).reshape(1), (ctx // 4).reshape(1)
@@ -298,6 +300,8 @@
     )
     totals = lax.all_to_all(totals, "ctx", 0, 0, axis_index_groups=across)
     diag = call(diag_kernel, [((rows, n_val), F32)], skip, maps, values, decay, smem=1)
+    gate_other, diag = lax.optimization_barrier((gate_other, diag))
+    gate_got = swap_cores(gate_other)
     before = call(before_kernel, [((share, width), F32)], quad_place, totals, smem=1)
     before = lax.all_gather(before, "ctx", axis=0, tiled=True, axis_index_groups=quads)
 
@@ -310,8 +314,8 @@
         before,
         maps,
         cols,
-        own,
-        got,
+        gate_own,
+        gate_got,
         smem=1,
     )
     sums = lax.all_to_all(sums, "fsdp", 0, 0, tiled=True)

time: 158 us -> 157 us (level)
  waiting for transfers between devices: 31.2 us -> 28.2 us
  starting transfers between devices: 83.3 us -> 85.6 us
    ppermute x2 -> x3, starting transfers between devices: 19.2 us -> 21.6 us  [swap_cores(): lax.ppermute(x, 'ctx', [(i, i ^ 1) for i in range(lax.axis_size('ctx'))])]
    all_to_all x1, waiting for transfers between devices: 13.8 us -> 11.4 us  [per_device(): totals = lax.all_to_all(totals, 'ctx', 0, 0, axis_index_groups=across)]
  transfers between devices with their start and end apart: 19 -> 20, of which waited for: 11 -> 11; matrix products, arithmetic and copies ran while one was open for 0% -> 0% of each run, Pallas kernels for 3% -> 3%
where the time goes in v9:
time: 157 us; the launch traced here: 156 us
  starting transfers between devices  85.6 us (55%)
  waiting for transfers between devices  28.2 us (18%)
  blocking collectives  27.6 us (18%)
  Pallas kernels  8.31 us (5%)
  local copies, waits for them, and re-layouts  4.95 us (3%)
    ppermute x15, starting transfers between devices, shift(): return lax.ppermute(x, 'ctx', [(i, (i + by) % n) for i in range(n)])  52.2 us
    ppermute x3, starting transfers between devices, swap_cores(): lax.ppermute(x, 'ctx', [(i, i ^ 1) for i in range(lax.axis_size('ctx'))])  21.6 us
    ppermute x15, waiting for transfers between devices, shift(): return lax.ppermute(x, 'ctx', [(i, (i + by) % n) for i in range(n)])  15.5 us
    all_to_all x1, blocking collectives, per_device(): sums = lax.all_to_all(sums, 'fsdp', 0, 0, tiled=True)  13.2 us
    all_to_all x1, waiting for transfers between devices, per_device(): totals = lax.all_to_all(totals, 'ctx', 0, 0, axis_index_groups=across)  11.4 us
    all_gather x1, blocking collectives, per_device(): lax.all_gather(before, 'ctx', axis=0, tiled=True, axis_index_groups=quads)  8.33 us
    pallas_call x9, Pallas kernels, call(): pl.pallas_call(kernel, out_shape=shapes, in_specs=[SMEM] * smem + [VMEM]...  8.31 us
    all_to_all x1, starting transfers between devices, per_device(): totals = lax.all_to_all(totals, 'ctx', 0, 0, axis_index_groups=across)  7.97 us
  transfers between devices with their start and end apart: 20, of which 11 were waited for; matrix products, arithmetic and copies ran while one was open for 0% of the time, Pallas kernels for 3%

profile of v9, /device:TPU:1, one launch (start us, length us, event | category | flops | bytes accessed | tf_op | source)
XLA Modules:
  0.0 156.0 jit_solution(8492526722012826750)
XLA Ops:
  0.9 8.8 %collective-permute-start = (bf16[256,128]{1,0:T(8,128)(2,1)S(1)}, bf16[256,128]{1,0:T(8,128)(2,1)S(1)}, u32[]{:S(2)}, u32[]{:S(2)}) collective-permute-start(bf16[256,128]{1,0:T(8,128)(2,1)S(1)} %get-tuple-element.40), channel_id=1, source_target_pairs={{0,16},{16,0},{32,48},{48,32},{64,80},{80,64},{96,112},{112,96},{1... | collective-permute-start | bytes 196616 | tf_op jit(solution)/shard_map/ppermute | solution.py:42
  12.3 3.8 %all-to-all-start = ((bf16[16,512,128]{2,1,0:T(8,128)(2,1)}), bf16[16,512,128]{2,1,0:T(8,128)(2,1)S(1)}, u32[]{:S(2)}, u32[]{:S(2)}) async-start(bf16[16,512,128]{2,1,0:T(8,128)(2,1)} %broadcast_in_dim.2), calls=%async_computation | async-start | bytes 4194304 | tf_op jit(solution)/shard_map/all_to_all | solution.py:242
  16.4 1.9 %collective-permute-start.1 = (bf16[128,768]{1,0:T(8,128)(2,1)S(1)}, bf16[128,768]{1,0:T(8,128)(2,1)S(1)}, u32[]{:S(2)}, u32[]{:S(2)}) collective-permute-start(bf16[128,768]{1,0:T(8,128)(2,1)S(1)} %bitcast_dynamic-update-slice_fusion.refs_0_), channel_id=1, source_target_pairs={{0,32},{16,48},{32,64},{48,80},{64,96},{80,112},{96,128},{112,144}... | collective-permute-start | bytes 589832 | tf_op jit(solution)/shard_map/ppermute | solution.py:38
  18.3 8.8 %collective-permute-start.6 = (bf16[128,768]{1,0:T(8,128)(2,1)S(1)}, bf16[128,768]{1,0:T(8,128)(2,1)S(1)}, u32[]{:S(2)}, u32[]{:S(2)}) collective-permute-start(bf16[128,768]{1,0:T(8,128)(2,1)S(1)} %bitcast_dynamic-update-slice_fusion.refs_0_), channel_id=1, source_target_pairs={{0,480},{16,496},{32,0},{48,16},{64,32},{80,48},{96,64},{112,80},{... | collective-permute-start | bytes 589832 | tf_op jit(solution)/shard_map/ppermute | solution.py:38
  27.1 2.7 %collective-permute-done.1.refs_1_ = bf16[128,768]{1,0:T(8,128)(2,1)S(1)} collective-permute-done((bf16[128,768]{1,0:T(8,128)(2,1)S(1)}, bf16[128,768]{1,0:T(8,128)(2,1)S(1)}, u32[]{:S(2)}, u32[]{:S(2)}) %collective-permute-start.1) | collective-permute-done | bytes 196640 | tf_op jit(solution)/shard_map/ppermute | solution.py:38
  31.7 4.6 %collective-permute-start.7 = (bf16[128,768]{1,0:T(8,128)(2,1)S(1)}, bf16[128,768]{1,0:T(8,128)(2,1)S(1)}, u32[]{:S(2)}, u32[]{:S(2)}) collective-permute-start(bf16[128,768]{1,0:T(8,128)(2,1)S(1)} %collective-permute-done.6.refs_2_), channel_id=1, source_target_pairs={{0,480},{16,496},{32,0},{48,16},{64,32},{80,48},{96,64},{112,80},{... | collective-permute-start | bytes 589832 | tf_op jit(solution)/shard_map/ppermute | solution.py:38
  40.1 4.6 %collective-permute-start.8 = (bf16[128,768]{1,0:T(8,128)(2,1)S(1)}, bf16[128,768]{1,0:T(8,128)(2,1)S(1)}, u32[]{:S(2)}, u32[]{:S(2)}) collective-permute-start(bf16[128,768]{1,0:T(8,128)(2,1)S(1)} %collective-permute-done.7.refs_4_), channel_id=1, source_target_pairs={{0,480},{16,496},{32,0},{48,16},{64,32},{80,48},{96,64},{112,80},{... | collective-permute-start | bytes 589832 | tf_op jit(solution)/shard_map/ppermute | solution.py:38
  47.7 4.9 %collective-permute-start.9 = (bf16[128,768]{1,0:T(8,128)(2,1)S(1)}, bf16[128,768]{1,0:T(8,128)(2,1)}, u32[]{:S(2)}, u32[]{:S(2)}) collective-permute-start(bf16[128,768]{1,0:T(8,128)(2,1)S(1)} %collective-permute-done.8.refs_6_), channel_id=1, source_target_pairs={{0,480},{16,496},{32,0},{48,16},{64,32},{80,48},{96,64},{112,80},{... | collective-permute-start | bytes 589832 | tf_op jit(solution)/shard_map/ppermute | solution.py:38
  53.4 1.9 %collective-permute-start.5 = (bf16[128,768]{1,0:T(8,128)(2,1)S(1)}, bf16[128,768]{1,0:T(8,128)(2,1)}, u32[]{:S(2)}, u32[]{:S(2)}) collective-permute-start(bf16[128,768]{1,0:T(8,128)(2,1)S(1)} %collective-permute-done.4.refs_7_), channel_id=1, source_target_pairs={{0,32},{16,48},{32,64},{48,80},{64,96},{80,112},{96,128},{112,144}... | collective-permute-start | bytes 589832 | tf_op jit(solution)/shard_map/ppermute | solution.py:38
  55.9 4.6 %collective-permute-start.10 = (bf16[128,768]{1,0:T(8,128)(2,1)}, bf16[128,768]{1,0:T(8,128)(2,1)}, u32[]{:S(2)}, u32[]{:S(2)}) collective-permute-start(bf16[128,768]{1,0:T(8,128)(2,1)} %collective-permute-done.9.refs_8_), channel_id=1, source_target_pairs={{0,480},{16,496},{32,0},{48,16},{64,32},{80,48},{96,64},{112,80},{... | collective-permute-start | bytes 589832 | tf_op jit(solution)/shard_map/ppermute | solution.py:38
  61.1 1.9 %collective-permute-start.11 = (bf16[128,768]{1,0:T(8,128)(2,1)}, bf16[128,768]{1,0:T(8,128)(2,1)}, u32[]{:S(2)}, u32[]{:S(2)}) collective-permute-start(bf16[128,768]{1,0:T(8,128)(2,1)} %collective-permute-done.5.refs_0_), channel_id=1, source_target_pairs={{0,32},{16,48},{32,64},{48,80},{64,96},{80,112},{96,128},{112,144}... | collective-permute-start | bytes 589832 | tf_op jit(solution)/shard_map/ppermute | solution.py:38
  63.4 5.0 %collective-permute-start.12 = (bf16[128,768]{1,0:T(8,128)(2,1)}, bf16[128,768]{1,0:T(8,128)(2,1)}, u32[]{:S(2)}, u32[]{:S(2)}) collective-permute-start(bf16[128,768]{1,0:T(8,128)(2,1)} %collective-permute-done.10.refs_1_), channel_id=1, source_target_pairs={{0,480},{16,496},{32,0},{48,16},{64,32},{80,48},{96,64},{112,80},{... | collective-permute-start | bytes 589832 | tf_op jit(solution)/shard_map/ppermute | solution.py:38
  69.4 2.1 %shard_map.73.refs_7_ = f32[512,768]{1,0:T(8,128)S(1)} custom-call(s32[1]{0:T(128)} %bitcast.1.chip_ref, bf16[16,512,128]{2,1,0:T(8,128)(2,1)S(1)} %all-to-all-done.tok_ref, bf16[128,768]{1,0:T(8,128)(2,1)S(1)} %bitcast_dynamic-update-slice_fusion.refs_0_, bf16[128,768]{1,0:T(8,128)(2,1)S(1)} %collective-permute-done.1.refs_1_, ...), custom_call_target="tpu_custom_call" | custom-call | tf_op jit(solution)/shard_map/pallas_call | solution.py:22
  71.5 1.9 %collective-permute-start.13 = (bf16[128,768]{1,0:T(8,128)(2,1)}, bf16[128,768]{1,0:T(8,128)(2,1)S(1)}, u32[]{:S(2)}, u32[]{:S(2)}) collective-permute-start(bf16[128,768]{1,0:T(8,128)(2,1)} %collective-permute-done.11.refs_2_), channel_id=1, source_target_pairs={{0,32},{16,48},{32,64},{48,80},{64,96},{80,112},{96,128},{112,144}... | collective-permute-start | bytes 589832 | tf_op jit(solution)/shard_map/ppermute | solution.py:38
  73.5 4.6 %collective-permute-start.14 = (bf16[128,768]{1,0:T(8,128)(2,1)}, bf16[128,768]{1,0:T(8,128)(2,1)S(1)}, u32[]{:S(2)}, u32[]{:S(2)}) collective-permute-start(bf16[128,768]{1,0:T(8,128)(2,1)} %collective-permute-done.12.refs_3_), channel_id=1, source_target_pairs={{0,480},{16,496},{32,0},{48,16},{64,32},{80,48},{96,64},{112,80},{... | collective-permute-start | bytes 589832 | tf_op jit(solution)/shard_map/ppermute | solution.py:38
  81.3 6.8 %collective-permute-done.15.refs_6_ = bf16[128,768]{1,0:T(8,128)(2,1)S(1)} collective-permute-done((bf16[128,768]{1,0:T(8,128)(2,1)S(1)}, bf16[128,768]{1,0:T(8,128)(2,1)S(1)}, u32[]{:S(2)}, u32[]{:S(2)}) %collective-permute-start.15) | collective-permute-done | bytes 196640 | tf_op jit(solution)/shard_map/ppermute | solution.py:38
  88.1 2.2 %shard_map.74 = (f32[256,512]{1,0:T(8,128)S(1)}, f32[256,512]{1,0:T(8,128)S(1)}, f32[256,256]{1,0:T(8,128)S(1)}, f32[256,256]{1,0:T(8,128)S(1)}) custom-call(s32[1]{0:T(128)} %bitcast.1.chip_ref, bf16[16,512,128]{2,1,0:T(8,128)(2,1)S(1)} %all-to-all-done.tok_ref, bf16[128,768]{1,0:T(8,128)(2,1)} %collective-permute-done.5.refs_0_, ...), custom_call_target="tpu_custom_call" | custom-call | tf_op jit(solution)/shard_map/pallas_call | solution.py:22
  91.0 10.4 %collective-permute-start.16 = (f32[256,512]{1,0:T(8,128)S(1)}, f32[256,512]{1,0:T(8,128)S(1)}, u32[]{:S(2)}, u32[]{:S(2)}) collective-permute-start(f32[256,512]{1,0:T(8,128)S(1)} %get-tuple-element.25), channel_id=1, source_target_pairs={{0,16},{16,0},{32,48},{48,32},{64,80},{80,64},{96,112},{112,96},{1... | collective-permute-start | bytes 1572872 | tf_op jit(solution)/shard_map/ppermute | solution.py:42
  103.3 6.0 %all-gather = bf16[1088,128]{1,0:T(8,128)(2,1)S(1)} all-gather(bf16[272,128]{1,0:T(8,128)(2,1)S(1)} %get-tuple-element.32), channel_id=2, replica_groups={{0,16,32,48},{64,80,96,112},{128,144,160,176},{192,208,224,240},{256,27..., dimensions={0}, use_global_device_ids=true | all-gather | bytes 348160 | tf_op jit(solution)/shard_map/all_gather | solution.py:292
  110.0 8.0 %all-to-all-start.1 = ((bf16[8,80,128]{2,1,0:T(8,128)(2,1)}), bf16[8,80,128]{2,1,0:T(8,128)(2,1)S(1)}, u32[]{:S(2)}, u32[]{:S(2)}) async-start(bf16[8,80,128]{2,1,0:T(8,128)(2,1)} %shard_map.78), calls=%async_computation.1 | async-start | bytes 327680 | tf_op jit(solution)/shard_map/all_to_all | solution.py:301
  119.0 2.4 %collective-permute-start.17 = (f32[256,256]{1,0:T(8,128)S(1)}, f32[256,256]{1,0:T(8,128)S(1)}, u32[]{:S(2)}, u32[]{:S(2)}) collective-permute-start(f32[256,256]{1,0:T(8,128)S(1)} %copy-done.7), channel_id=1, source_target_pairs={{0,16},{16,0},{32,48},{48,32},{64,80},{80,64},{96,112},{112,96},{1... | collective-permute-start | bytes 786440 | tf_op jit(solution)/shard_map/ppermute | solution.py:42
  121.3 11.4 %all-to-all-done.1.all_ref = bf16[8,80,128]{2,1,0:T(8,128)(2,1)S(1)} async-done(((bf16[8,80,128]{2,1,0:T(8,128)(2,1)}), bf16[8,80,128]{2,1,0:T(8,128)(2,1)S(1)}, u32[]{:S(2)}, u32[]{:S(2)}) %all-to-all-start.1) | async-done | bytes 163872 | tf_op jit(solution)/shard_map/all_to_all | solution.py:301
  132.8 8.3 %all_gather.11.before_ref = f32[256,128]{1,0:T(8,128)S(1)} all-gather(f32[64,128]{1,0:T(8,128)S(1)} %shard_map.79), channel_id=1, replica_groups={{0,16,32,48},{64,80,96,112},{128,144,160,176},{192,208,224,240},{256,27..., dimensions={0}, use_global_device_ids=true | all-gather | bytes 163840 | tf_op jit(solution)/shard_map/all_gather | solution.py:306
  141.7 13.2 %all_to_all.21 = f32[16,1,256]{2,1,0:T(1,128)S(1)} all-to-all(f32[16,1,256]{2,1,0:T(1,128)S(1)} %copy.8), channel_id=1, replica_groups=mesh['ctx'=32,'fsdp'=16] {'fsdp'}, dimensions={0} | all-to-all | bytes 32768 | tf_op jit(solution)/shard_map/all_to_all | solution.py:321
  (58 shorter events, 24.8 us)
Async XLA Ops:
  0.9 9.7 %collective-permute-start = (bf16[256,128]{1,0:T(8,128)(2,1)S(1)}, bf16[256,128]{1,0:T(8,128)(2,1)S(1)}, u32[]{:S(2)}, u32[]{:S(2)}) collective-permute-start(bf16[256,128]{1,0:T(8,128)(2,1)S(1)} %get-tuple-element.40), channel_id=1, source_target_pairs={{0,16},{16,0},{32,48},{48,32},{64,80},{80,64},{96,112},{112,96},{1... | collective-permute-start | bytes 196616 | tf_op jit(solution)/shard_map/ppermute | solution.py:42
  12.3 56.1 %all-to-all-start = ((bf16[16,512,128]{2,1,0:T(8,128)(2,1)}), bf16[16,512,128]{2,1,0:T(8,128)(2,1)S(1)}, u32[]{:S(2)}, u32[]{:S(2)}) async-start(bf16[16,512,128]{2,1,0:T(8,128)(2,1)} %broadcast_in_dim.2), calls=%async_computation | async-start | bytes 4194304 | tf_op jit(solution)/shard_map/all_to_all | solution.py:242
  16.4 13.4 %collective-permute-start.1 = (bf16[128,768]{1,0:T(8,128)(2,1)S(1)}, bf16[128,768]{1,0:T(8,128)(2,1)S(1)}, u32[]{:S(2)}, u32[]{:S(2)}) collective-permute-start(bf16[128,768]{1,0:T(8,128)(2,1)S(1)} %bitcast_dynamic-update-slice_fusion.refs_0_), channel_id=1, source_target_pairs={{0,32},{16,48},{32,64},{48,80},{64,96},{80,112},{96,128},{112,144}... | collective-permute-start | bytes 589832 | tf_op jit(solution)/shard_map/ppermute | solution.py:38
  18.3 13.4 %collective-permute-start.6 = (bf16[128,768]{1,0:T(8,128)(2,1)S(1)}, bf16[128,768]{1,0:T(8,128)(2,1)S(1)}, u32[]{:S(2)}, u32[]{:S(2)}) collective-permute-start(bf16[128,768]{1,0:T(8,128)(2,1)S(1)} %bitcast_dynamic-update-slice_fusion.refs_0_), channel_id=1, source_target_pairs={{0,480},{16,496},{32,0},{48,16},{64,32},{80,48},{96,64},{112,80},{... | collective-permute-start | bytes 589832 | tf_op jit(solution)/shard_map/ppermute | solution.py:38
  29.8 8.3 %collective-permute-start.2 = (bf16[128,768]{1,0:T(8,128)(2,1)S(1)}, bf16[128,768]{1,0:T(8,128)(2,1)S(1)}, u32[]{:S(2)}, u32[]{:S(2)}) collective-permute-start(bf16[128,768]{1,0:T(8,128)(2,1)S(1)} %collective-permute-done.1.refs_1_), channel_id=1, source_target_pairs={{0,32},{16,48},{32,64},{48,80},{64,96},{80,112},{96,128},{112,144}... | collective-permute-start | bytes 589832 | tf_op jit(solution)/shard_map/ppermute | solution.py:38
  31.7 8.3 %collective-permute-start.7 = (bf16[128,768]{1,0:T(8,128)(2,1)S(1)}, bf16[128,768]{1,0:T(8,128)(2,1)S(1)}, u32[]{:S(2)}, u32[]{:S(2)}) collective-permute-start(bf16[128,768]{1,0:T(8,128)(2,1)S(1)} %collective-permute-done.6.refs_2_), channel_id=1, source_target_pairs={{0,480},{16,496},{32,0},{48,16},{64,32},{80,48},{96,64},{112,80},{... | collective-permute-start | bytes 589832 | tf_op jit(solution)/shard_map/ppermute | solution.py:38
  38.1 7.6 %collective-permute-start.3 = (bf16[128,768]{1,0:T(8,128)(2,1)S(1)}, bf16[128,768]{1,0:T(8,128)(2,1)S(1)}, u32[]{:S(2)}, u32[]{:S(2)}) collective-permute-start(bf16[128,768]{1,0:T(8,128)(2,1)S(1)} %collective-permute-done.2.refs_3_), channel_id=1, source_target_pairs={{0,32},{16,48},{32,64},{48,80},{64,96},{80,112},{96,128},{112,144}... | collective-permute-start | bytes 589832 | tf_op jit(solution)/shard_map/ppermute | solution.py:38
  40.1 7.6 %collective-permute-start.8 = (bf16[128,768]{1,0:T(8,128)(2,1)S(1)}, bf16[128,768]{1,0:T(8,128)(2,1)S(1)}, u32[]{:S(2)}, u32[]{:S(2)}) collective-permute-start(bf16[128,768]{1,0:T(8,128)(2,1)S(1)} %collective-permute-done.7.refs_4_), channel_id=1, source_target_pairs={{0,480},{16,496},{32,0},{48,16},{64,32},{80,48},{96,64},{112,80},{... | collective-permute-start | bytes 589832 | tf_op jit(solution)/shard_map/ppermute | solution.py:38
  45.7 7.6 %collective-permute-start.4 = (bf16[128,768]{1,0:T(8,128)(2,1)S(1)}, bf16[128,768]{1,0:T(8,128)(2,1)S(1)}, u32[]{:S(2)}, u32[]{:S(2)}) collective-permute-start(bf16[128,768]{1,0:T(8,128)(2,1)S(1)} %collective-permute-done.3.refs_5_), channel_id=1, source_target_pairs={{0,32},{16,48},{32,64},{48,80},{64,96},{80,112},{96,128},{112,144}... | collective-permute-start | bytes 589832 | tf_op jit(solution)/shard_map/ppermute | solution.py:38
  47.7 8.3 %collective-permute-start.9 = (bf16[128,768]{1,0:T(8,128)(2,1)S(1)}, bf16[128,768]{1,0:T(8,128)(2,1)}, u32[]{:S(2)}, u32[]{:S(2)}) collective-permute-start(bf16[128,768]{1,0:T(8,128)(2,1)S(1)} %collective-permute-done.8.refs_6_), channel_id=1, source_target_pairs={{0,480},{16,496},{32,0},{48,16},{64,32},{80,48},{96,64},{112,80},{... | collective-permute-start | bytes 589832 | tf_op jit(solution)/shard_map/ppermute | solution.py:38
  53.4 7.7 %collective-permute-start.5 = (bf16[128,768]{1,0:T(8,128)(2,1)S(1)}, bf16[128,768]{1,0:T(8,128)(2,1)}, u32[]{:S(2)}, u32[]{:S(2)}) collective-permute-start(bf16[128,768]{1,0:T(8,128)(2,1)S(1)} %collective-permute-done.4.refs_7_), channel_id=1, source_target_pairs={{0,32},{16,48},{32,64},{48,80},{64,96},{80,112},{96,128},{112,144}... | collective-permute-start | bytes 589832 | tf_op jit(solution)/shard_map/ppermute | solution.py:38
  55.9 7.5 %collective-permute-start.10 = (bf16[128,768]{1,0:T(8,128)(2,1)}, bf16[128,768]{1,0:T(8,128)(2,1)}, u32[]{:S(2)}, u32[]{:S(2)}) collective-permute-start(bf16[128,768]{1,0:T(8,128)(2,1)} %collective-permute-done.9.refs_8_), channel_id=1, source_target_pairs={{0,480},{16,496},{32,0},{48,16},{64,32},{80,48},{96,64},{112,80},{... | collective-permute-start | bytes 589832 | tf_op jit(solution)/shard_map/ppermute | solution.py:38
  61.1 10.5 %collective-permute-start.11 = (bf16[128,768]{1,0:T(8,128)(2,1)}, bf16[128,768]{1,0:T(8,128)(2,1)}, u32[]{:S(2)}, u32[]{:S(2)}) collective-permute-start(bf16[128,768]{1,0:T(8,128)(2,1)} %collective-permute-done.5.refs_0_), channel_id=1, source_target_pairs={{0,32},{16,48},{32,64},{48,80},{64,96},{80,112},{96,128},{112,144}... | collective-permute-start | bytes 589832 | tf_op jit(solution)/shard_map/ppermute | solution.py:38
  63.4 10.0 %collective-permute-start.12 = (bf16[128,768]{1,0:T(8,128)(2,1)}, bf16[128,768]{1,0:T(8,128)(2,1)}, u32[]{:S(2)}, u32[]{:S(2)}) collective-permute-start(bf16[128,768]{1,0:T(8,128)(2,1)} %collective-permute-done.10.refs_1_), channel_id=1, source_target_pairs={{0,480},{16,496},{32,0},{48,16},{64,32},{80,48},{96,64},{112,80},{... | collective-permute-start | bytes 589832 | tf_op jit(solution)/shard_map/ppermute | solution.py:38
  71.5 29.9 %copy-start.2 = (f32[2,256]{1,0:T(2,128)S(1)}, f32[2,256]{1,0:T(2,128)}, u32[]{:S(2)}) copy-start(f32[2,256]{1,0:T(2,128)} %decays_ref.1) | copy-start | bytes 6148
  71.5 29.9 %copy-start.4 = (s32[256]{0:T(256)S(1)}, s32[256]{0:T(256)}, u32[]{:S(2)}) copy-start(s32[256]{0:T(256)} %param.13) | copy-start | bytes 3076
  71.5 7.8 %collective-permute-start.13 = (bf16[128,768]{1,0:T(8,128)(2,1)}, bf16[128,768]{1,0:T(8,128)(2,1)S(1)}, u32[]{:S(2)}, u32[]{:S(2)}) collective-permute-start(bf16[128,768]{1,0:T(8,128)(2,1)} %collective-permute-done.11.refs_2_), channel_id=1, source_target_pairs={{0,32},{16,48},{32,64},{48,80},{64,96},{80,112},{96,128},{112,144}... | collective-permute-start | bytes 589832 | tf_op jit(solution)/shard_map/ppermute | solution.py:38
  73.5 7.8 %collective-permute-start.14 = (bf16[128,768]{1,0:T(8,128)(2,1)}, bf16[128,768]{1,0:T(8,128)(2,1)S(1)}, u32[]{:S(2)}, u32[]{:S(2)}) collective-permute-start(bf16[128,768]{1,0:T(8,128)(2,1)} %collective-permute-done.12.refs_3_), channel_id=1, source_target_pairs={{0,480},{16,496},{32,0},{48,16},{64,32},{80,48},{96,64},{112,80},{... | collective-permute-start | bytes 589832 | tf_op jit(solution)/shard_map/ppermute | solution.py:38
  79.4 8.7 %collective-permute-start.15 = (bf16[128,768]{1,0:T(8,128)(2,1)S(1)}, bf16[128,768]{1,0:T(8,128)(2,1)S(1)}, u32[]{:S(2)}, u32[]{:S(2)}) collective-permute-start(bf16[128,768]{1,0:T(8,128)(2,1)S(1)} %collective-permute-done.13.refs_4_), channel_id=1, source_target_pairs={{0,32},{16,48},{32,64},{48,80},{64,96},{80,112},{96,128},{112,144}... | collective-permute-start | bytes 589832 | tf_op jit(solution)/shard_map/ppermute | solution.py:38
  91.0 28.0 %copy-start.7 = (f32[256,256]{1,0:T(8,128)S(1)}, f32[256,256]{1,0:T(8,128)}, u32[]{:S(2)}) copy-start(f32[256,256]{1,0:T(8,128)} %copy-done.6) | copy-start | bytes 786436
  91.0 12.0 %collective-permute-start.16 = (f32[256,512]{1,0:T(8,128)S(1)}, f32[256,512]{1,0:T(8,128)S(1)}, u32[]{:S(2)}, u32[]{:S(2)}) collective-permute-start(f32[256,512]{1,0:T(8,128)S(1)} %get-tuple-element.25), channel_id=1, source_target_pairs={{0,16},{16,0},{32,48},{48,32},{64,80},{80,64},{96,112},{112,96},{1... | collective-permute-start | bytes 1572872 | tf_op jit(solution)/shard_map/ppermute | solution.py:42
  103.3 51.7 %copy-start.3 = (f32[2,128]{1,0:T(2,128)S(1)}, f32[2,128]{1,0:T(2,128)}, u32[]{:S(2)}) copy-start(f32[2,128]{1,0:T(2,128)} %param.10) | copy-start | bytes 3076
  110.0 22.8 %all-to-all-start.1 = ((bf16[8,80,128]{2,1,0:T(8,128)(2,1)}), bf16[8,80,128]{2,1,0:T(8,128)(2,1)S(1)}, u32[]{:S(2)}, u32[]{:S(2)}) async-start(bf16[8,80,128]{2,1,0:T(8,128)(2,1)} %shard_map.78), calls=%async_computation.1 | async-start | bytes 327680 | tf_op jit(solution)/shard_map/all_to_all | solution.py:301
  119.0 22.2 %collective-permute-start.17 = (f32[256,256]{1,0:T(8,128)S(1)}, f32[256,256]{1,0:T(8,128)S(1)}, u32[]{:S(2)}, u32[]{:S(2)}) collective-permute-start(f32[256,256]{1,0:T(8,128)S(1)} %copy-done.7), channel_id=1, source_target_pairs={{0,16},{16,0},{32,48},{48,32},{64,80},{80,64},{96,112},{112,96},{1... | collective-permute-start | bytes 786440 | tf_op jit(solution)/shard_map/ppermute | solution.py:42
  (6 other events, 37.2 us)

commit v10 on v6

--- a/solution.py
+++ b/solution.py
@@ -221,11 +221,8 @@
     same_core = [[2 * z + c for z in range(n_chip)] for c in range(2)]
     core_1, chip_1 = core.reshape(1), chip.reshape(1)
 
-    def mine_other(a, b):
-        return jnp.where(core == 0, a, b), jnp.where(core == 0, b, a)
-
-    tok_mine, tok_other = mine_other(tokens[:, :depth], tokens[:, depth:])
-    tok = jnp.concatenate([tok_mine, swap_cores(tok_other)], axis=0)
+    tok = jnp.concatenate([tokens, swap_cores(tokens)], axis=0)
+    tok = jnp.where(core == 0, tok[:, :depth], tok[:, depth:])
     copies = jnp.broadcast_to(tok[None], (n_fsdp,) + tok.shape)
     tok = lax.all_to_all(copies, "fsdp", 0, 0)
 

time: 154 us -> 153 us (level)
    unnamed x33 -> x34, local copies, waits for them, and re-layouts: 8 us -> 8.95 us
where the time goes in v10:
time: 153 us; the launch traced here: 152 us
  starting transfers between devices  85.6 us (56%)
  blocking collectives  37.4 us (24%)
  local copies, waits for them, and re-layouts  12.5 us (8%)
  waiting for transfers between devices  9.85 us (6%)
  Pallas kernels  6.6 us (4%)
    ppermute x15, starting transfers between devices, shift(): return lax.ppermute(x, 'ctx', [(i, (i + by) % n) for i in range(n)])  51.8 us
    ppermute x4, starting transfers between devices, swap_cores(): lax.ppermute(x, 'ctx', [(i, i ^ 1) for i in range(lax.axis_size('ctx'))])  30 us
    all_gather x1, blocking collectives, per_device(): lax.all_gather(packed, 'ctx', axis=0, axis_index_groups=same_core)  24.5 us
    all_to_all x1, blocking collectives, per_device(): sums = lax.all_to_all(sums, 'fsdp', 0, 0, tiled=True)  12.9 us
    unnamed x34, local copies, waits for them, and re-layouts  8.95 us
    ppermute x15, waiting for transfers between devices, shift(): return lax.ppermute(x, 'ctx', [(i, (i + by) % n) for i in range(n)])  8.18 us
    pallas_call x9, Pallas kernels, call(): pl.pallas_call(kernel, out_shape=shapes, in_specs=[SMEM] * smem + [VMEM]...  6.6 us
    all_to_all x1, starting transfers between devices, per_device(): tok = lax.all_to_all(copies, 'fsdp', 0, 0)  3.85 us
  transfers between devices with their start and end apart: 20, of which 8 were waited for; matrix products, arithmetic and copies ran while one was open for 1% of the time, Pallas kernels for 2%

profile of v10, /device:TPU:1, one launch (start us, length us, event | category | flops | bytes accessed | tf_op | source)
XLA Modules:
  0.0 152.4 jit_solution(7190027148895638422)
XLA Ops:
  0.0 8.8 %collective-permute-start = (bf16[256,256]{1,0:T(8,128)(2,1)}, bf16[256,256]{1,0:T(8,128)(2,1)S(1)}, u32[]{:S(2)}, u32[]{:S(2)}) collective-permute-start(bf16[256,256]{1,0:T(8,128)(2,1)} %param.7), channel_id=1, source_target_pairs={{0,16},{16,0},{32,48},{48,32},{64,80},{80,64},{96,112},{112,96},{1... | collective-permute-start | bytes 393224 | tf_op jit(solution)/shard_map/ppermute | solution.py:42
  12.5 3.8 %all-to-all-start = ((bf16[16,512,128]{2,1,0:T(8,128)(2,1)}), bf16[16,512,128]{2,1,0:T(8,128)(2,1)S(1)}, u32[]{:S(2)}, u32[]{:S(2)}) async-start(bf16[16,512,128]{2,1,0:T(8,128)(2,1)} %broadcast_in_dim.2), calls=%async_computation | async-start | bytes 4194304 | tf_op jit(solution)/shard_map/all_to_all | solution.py:227
  16.4 1.9 %collective-permute-start.7 = (bf16[128,768]{1,0:T(8,128)(2,1)S(1)}, bf16[128,768]{1,0:T(8,128)(2,1)S(1)}, u32[]{:S(2)}, u32[]{:S(2)}) collective-permute-start(bf16[128,768]{1,0:T(8,128)(2,1)S(1)} %bitcast_dynamic-update-slice_fusion.refs_0_), channel_id=1, source_target_pairs={{0,32},{16,48},{32,64},{48,80},{64,96},{80,112},{96,128},{112,144}... | collective-permute-start | bytes 589832 | tf_op jit(solution)/shard_map/ppermute | solution.py:38
  18.4 8.8 %collective-permute-start.1 = (bf16[128,768]{1,0:T(8,128)(2,1)S(1)}, bf16[128,768]{1,0:T(8,128)(2,1)S(1)}, u32[]{:S(2)}, u32[]{:S(2)}) collective-permute-start(bf16[128,768]{1,0:T(8,128)(2,1)S(1)} %bitcast_dynamic-update-slice_fusion.refs_0_), channel_id=1, source_target_pairs={{0,480},{16,496},{32,0},{48,16},{64,32},{80,48},{96,64},{112,80},{... | collective-permute-start | bytes 589832 | tf_op jit(solution)/shard_map/ppermute | solution.py:38
  27.2 3.1 %collective-permute-done.7.refs_1_ = bf16[128,768]{1,0:T(8,128)(2,1)S(1)} collective-permute-done((bf16[128,768]{1,0:T(8,128)(2,1)S(1)}, bf16[128,768]{1,0:T(8,128)(2,1)S(1)}, u32[]{:S(2)}, u32[]{:S(2)}) %collective-permute-start.7) | collective-permute-done | bytes 196640 | tf_op jit(solution)/shard_map/ppermute | solution.py:38
  30.3 1.9 %collective-permute-start.8 = (bf16[128,768]{1,0:T(8,128)(2,1)S(1)}, bf16[128,768]{1,0:T(8,128)(2,1)S(1)}, u32[]{:S(2)}, u32[]{:S(2)}) collective-permute-start(bf16[128,768]{1,0:T(8,128)(2,1)S(1)} %collective-permute-done.7.refs_1_), channel_id=1, source_target_pairs={{0,32},{16,48},{32,64},{48,80},{64,96},{80,112},{96,128},{112,144}... | collective-permute-start | bytes 589832 | tf_op jit(solution)/shard_map/ppermute | solution.py:38
  32.2 4.6 %collective-permute-start.2 = (bf16[128,768]{1,0:T(8,128)(2,1)S(1)}, bf16[128,768]{1,0:T(8,128)(2,1)S(1)}, u32[]{:S(2)}, u32[]{:S(2)}) collective-permute-start(bf16[128,768]{1,0:T(8,128)(2,1)S(1)} %collective-permute-done.1.refs_2_), channel_id=1, source_target_pairs={{0,480},{16,496},{32,0},{48,16},{64,32},{80,48},{96,64},{112,80},{... | collective-permute-start | bytes 589832 | tf_op jit(solution)/shard_map/ppermute | solution.py:38
  36.8 2.2 %collective-permute-done.8.refs_3_ = bf16[128,768]{1,0:T(8,128)(2,1)S(1)} collective-permute-done((bf16[128,768]{1,0:T(8,128)(2,1)S(1)}, bf16[128,768]{1,0:T(8,128)(2,1)S(1)}, u32[]{:S(2)}, u32[]{:S(2)}) %collective-permute-start.8) | collective-permute-done | bytes 196640 | tf_op jit(solution)/shard_map/ppermute | solution.py:38
  39.0 1.9 %collective-permute-start.9 = (bf16[128,768]{1,0:T(8,128)(2,1)S(1)}, bf16[128,768]{1,0:T(8,128)(2,1)S(1)}, u32[]{:S(2)}, u32[]{:S(2)}) collective-permute-start(bf16[128,768]{1,0:T(8,128)(2,1)S(1)} %collective-permute-done.8.refs_3_), channel_id=1, source_target_pairs={{0,32},{16,48},{32,64},{48,80},{64,96},{80,112},{96,128},{112,144}... | collective-permute-start | bytes 589832 | tf_op jit(solution)/shard_map/ppermute | solution.py:38
  40.9 4.6 %collective-permute-start.3 = (bf16[128,768]{1,0:T(8,128)(2,1)S(1)}, bf16[128,768]{1,0:T(8,128)(2,1)S(1)}, u32[]{:S(2)}, u32[]{:S(2)}) collective-permute-start(bf16[128,768]{1,0:T(8,128)(2,1)S(1)} %collective-permute-done.2.refs_4_), channel_id=1, source_target_pairs={{0,480},{16,496},{32,0},{48,16},{64,32},{80,48},{96,64},{112,80},{... | collective-permute-start | bytes 589832 | tf_op jit(solution)/shard_map/ppermute | solution.py:38
  46.6 1.9 %collective-permute-start.10 = (bf16[128,768]{1,0:T(8,128)(2,1)S(1)}, bf16[128,768]{1,0:T(8,128)(2,1)S(1)}, u32[]{:S(2)}, u32[]{:S(2)}) collective-permute-start(bf16[128,768]{1,0:T(8,128)(2,1)S(1)} %collective-permute-done.9.refs_5_), channel_id=1, source_target_pairs={{0,32},{16,48},{32,64},{48,80},{64,96},{80,112},{96,128},{112,144}... | collective-permute-start | bytes 589832 | tf_op jit(solution)/shard_map/ppermute | solution.py:38
  48.5 4.9 %collective-permute-start.4 = (bf16[128,768]{1,0:T(8,128)(2,1)S(1)}, bf16[128,768]{1,0:T(8,128)(2,1)S(1)}, u32[]{:S(2)}, u32[]{:S(2)}) collective-permute-start(bf16[128,768]{1,0:T(8,128)(2,1)S(1)} %collective-permute-done.3.refs_6_), channel_id=1, source_target_pairs={{0,480},{16,496},{32,0},{48,16},{64,32},{80,48},{96,64},{112,80},{... | collective-permute-start | bytes 589832 | tf_op jit(solution)/shard_map/ppermute | solution.py:38
  54.2 1.9 %collective-permute-start.11 = (bf16[128,768]{1,0:T(8,128)(2,1)S(1)}, bf16[128,768]{1,0:T(8,128)(2,1)S(1)}, u32[]{:S(2)}, u32[]{:S(2)}) collective-permute-start(bf16[128,768]{1,0:T(8,128)(2,1)S(1)} %collective-permute-done.10.refs_7_), channel_id=1, source_target_pairs={{0,32},{16,48},{32,64},{48,80},{64,96},{80,112},{96,128},{112,144}... | collective-permute-start | bytes 589832 | tf_op jit(solution)/shard_map/ppermute | solution.py:38
  56.8 4.6 %collective-permute-start.5 = (bf16[128,768]{1,0:T(8,128)(2,1)S(1)}, bf16[128,768]{1,0:T(8,128)(2,1)S(1)}, u32[]{:S(2)}, u32[]{:S(2)}) collective-permute-start(bf16[128,768]{1,0:T(8,128)(2,1)S(1)} %collective-permute-done.4.refs_8_), channel_id=1, source_target_pairs={{0,480},{16,496},{32,0},{48,16},{64,32},{80,48},{96,64},{112,80},{... | collective-permute-start | bytes 589832 | tf_op jit(solution)/shard_map/ppermute | solution.py:38
  62.1 1.9 %collective-permute-start.12 = (bf16[128,768]{1,0:T(8,128)(2,1)S(1)}, bf16[128,768]{1,0:T(8,128)(2,1)S(1)}, u32[]{:S(2)}, u32[]{:S(2)}) collective-permute-start(bf16[128,768]{1,0:T(8,128)(2,1)S(1)} %collective-permute-done.11.refs_9_), channel_id=1, source_target_pairs={{0,32},{16,48},{32,64},{48,80},{64,96},{80,112},{96,128},{112,144}... | collective-permute-start | bytes 589832 | tf_op jit(solution)/shard_map/ppermute | solution.py:38
  64.7 4.6 %collective-permute-start.6 = (bf16[128,768]{1,0:T(8,128)(2,1)S(1)}, bf16[128,768]{1,0:T(8,128)(2,1)}, u32[]{:S(2)}, u32[]{:S(2)}) collective-permute-start(bf16[128,768]{1,0:T(8,128)(2,1)S(1)} %collective-permute-done.5.refs_10_), channel_id=1, source_target_pairs={{0,480},{16,496},{32,0},{48,16},{64,32},{80,48},{96,64},{112,80},{... | collective-permute-start | bytes 589832 | tf_op jit(solution)/shard_map/ppermute | solution.py:38
  69.9 1.9 %collective-permute-start.13 = (bf16[128,768]{1,0:T(8,128)(2,1)S(1)}, bf16[128,768]{1,0:T(8,128)(2,1)}, u32[]{:S(2)}, u32[]{:S(2)}) collective-permute-start(bf16[128,768]{1,0:T(8,128)(2,1)S(1)} %collective-permute-done.12.refs_11_), channel_id=1, source_target_pairs={{0,32},{16,48},{32,64},{48,80},{64,96},{80,112},{96,128},{112,144}... | collective-permute-start | bytes 589832 | tf_op jit(solution)/shard_map/ppermute | solution.py:38
  72.5 4.6 %collective-permute-start.14 = (bf16[128,768]{1,0:T(8,128)(2,1)}, bf16[128,768]{1,0:T(8,128)(2,1)}, u32[]{:S(2)}, u32[]{:S(2)}) collective-permute-start(bf16[128,768]{1,0:T(8,128)(2,1)} %collective-permute-done.6.refs_0_), channel_id=1, source_target_pairs={{0,480},{16,496},{32,0},{48,16},{64,32},{80,48},{96,64},{112,80},{... | collective-permute-start | bytes 589832 | tf_op jit(solution)/shard_map/ppermute | solution.py:38
  77.7 1.9 %collective-permute-start.15 = (bf16[128,768]{1,0:T(8,128)(2,1)}, bf16[128,768]{1,0:T(8,128)(2,1)}, u32[]{:S(2)}, u32[]{:S(2)}) collective-permute-start(bf16[128,768]{1,0:T(8,128)(2,1)} %collective-permute-done.13.refs_1_), channel_id=1, source_target_pairs={{0,32},{16,48},{32,64},{48,80},{64,96},{80,112},{96,128},{112,144}... | collective-permute-start | bytes 589832 | tf_op jit(solution)/shard_map/ppermute | solution.py:38
  87.8 9.9 %collective-permute-start.16 = (f32[256,768]{1,0:T(8,128)S(1)}, f32[256,768]{1,0:T(8,128)S(1)}, u32[]{:S(2)}, u32[]{:S(2)}) collective-permute-start(f32[256,768]{1,0:T(8,128)S(1)} %get-tuple-element.21), channel_id=1, source_target_pairs={{0,16},{16,0},{32,48},{48,32},{64,80},{80,64},{96,112},{112,96},{1... | collective-permute-start | bytes 2359304 | tf_op jit(solution)/shard_map/ppermute | solution.py:42
  100.0 2.3 %collective-permute-start.17 = (f32[136,128]{1,0:T(8,128)S(1)}, f32[136,128]{1,0:T(8,128)S(1)}, u32[]{:S(2)}, u32[]{:S(2)}) collective-permute-start(f32[136,128]{1,0:T(8,128)S(1)} %get-tuple-element.28), channel_id=1, source_target_pairs={{0,16},{16,0},{32,48},{48,32},{64,80},{80,64},{96,112},{112,96},{1... | collective-permute-start | bytes 208904 | tf_op jit(solution)/shard_map/ppermute | solution.py:42
  103.2 24.5 %all-gather = bf16[2304,128]{1,0:T(8,128)(2,1)S(1)} all-gather(bf16[144,128]{1,0:T(8,128)(2,1)S(1)} %get-tuple-element.29), channel_id=2, replica_groups={{0,32,64,96,128,160,192,224,256,288,320,352,384,416,448,480},{16,48,80,..., dimensions={0}, use_global_device_ids=true | all-gather | bytes 626688 | tf_op jit(solution)/shard_map/all_gather | solution.py:272
  127.9 9.0 %collective-permute-start.18 = (f32[128,128]{1,0:T(8,128)S(1)}, f32[128,128]{1,0:T(8,128)S(1)}, u32[]{:S(2)}, u32[]{:S(2)}) collective-permute-start(f32[128,128]{1,0:T(8,128)S(1)} %get-tuple-element.32), channel_id=1, source_target_pairs={{0,16},{16,0},{32,48},{48,32},{64,80},{80,64},{96,112},{112,96},{1... | collective-permute-start | bytes 196616 | tf_op jit(solution)/shard_map/ppermute | solution.py:42
  138.4 12.9 %all_to_all.16 = f32[16,1,256]{2,1,0:T(1,128)S(1)} all-to-all(f32[16,1,256]{2,1,0:T(1,128)S(1)} %copy.8), channel_id=1, replica_groups=mesh['ctx'=32,'fsdp'=16] {'fsdp'}, dimensions={0} | all-to-all | bytes 32768 | tf_op jit(solution)/shard_map/all_to_all | solution.py:297
  (68 shorter events, 23.6 us)
Async XLA Ops:
  0.0 10.7 %collective-permute-start = (bf16[256,256]{1,0:T(8,128)(2,1)}, bf16[256,256]{1,0:T(8,128)(2,1)S(1)}, u32[]{:S(2)}, u32[]{:S(2)}) collective-permute-start(bf16[256,256]{1,0:T(8,128)(2,1)} %param.7), channel_id=1, source_target_pairs={{0,16},{16,0},{32,48},{48,32},{64,80},{80,64},{96,112},{112,96},{1... | collective-permute-start | bytes 393224 | tf_op jit(solution)/shard_map/ppermute | solution.py:42
  12.5 67.1 %all-to-all-start = ((bf16[16,512,128]{2,1,0:T(8,128)(2,1)}), bf16[16,512,128]{2,1,0:T(8,128)(2,1)S(1)}, u32[]{:S(2)}, u32[]{:S(2)}) async-start(bf16[16,512,128]{2,1,0:T(8,128)(2,1)} %broadcast_in_dim.2), calls=%async_computation | async-start | bytes 4194304 | tf_op jit(solution)/shard_map/all_to_all | solution.py:227
  16.4 13.8 %collective-permute-start.7 = (bf16[128,768]{1,0:T(8,128)(2,1)S(1)}, bf16[128,768]{1,0:T(8,128)(2,1)S(1)}, u32[]{:S(2)}, u32[]{:S(2)}) collective-permute-start(bf16[128,768]{1,0:T(8,128)(2,1)S(1)} %bitcast_dynamic-update-slice_fusion.refs_0_), channel_id=1, source_target_pairs={{0,32},{16,48},{32,64},{48,80},{64,96},{80,112},{96,128},{112,144}... | collective-permute-start | bytes 589832 | tf_op jit(solution)/shard_map/ppermute | solution.py:38
  18.4 13.8 %collective-permute-start.1 = (bf16[128,768]{1,0:T(8,128)(2,1)S(1)}, bf16[128,768]{1,0:T(8,128)(2,1)S(1)}, u32[]{:S(2)}, u32[]{:S(2)}) collective-permute-start(bf16[128,768]{1,0:T(8,128)(2,1)S(1)} %bitcast_dynamic-update-slice_fusion.refs_0_), channel_id=1, source_target_pairs={{0,480},{16,496},{32,0},{48,16},{64,32},{80,48},{96,64},{112,80},{... | collective-permute-start | bytes 589832 | tf_op jit(solution)/shard_map/ppermute | solution.py:38
  30.3 8.7 %collective-permute-start.8 = (bf16[128,768]{1,0:T(8,128)(2,1)S(1)}, bf16[128,768]{1,0:T(8,128)(2,1)S(1)}, u32[]{:S(2)}, u32[]{:S(2)}) collective-permute-start(bf16[128,768]{1,0:T(8,128)(2,1)S(1)} %collective-permute-done.7.refs_1_), channel_id=1, source_target_pairs={{0,32},{16,48},{32,64},{48,80},{64,96},{80,112},{96,128},{112,144}... | collective-permute-start | bytes 589832 | tf_op jit(solution)/shard_map/ppermute | solution.py:38
  32.2 8.7 %collective-permute-start.2 = (bf16[128,768]{1,0:T(8,128)(2,1)S(1)}, bf16[128,768]{1,0:T(8,128)(2,1)S(1)}, u32[]{:S(2)}, u32[]{:S(2)}) collective-permute-start(bf16[128,768]{1,0:T(8,128)(2,1)S(1)} %collective-permute-done.1.refs_2_), channel_id=1, source_target_pairs={{0,480},{16,496},{32,0},{48,16},{64,32},{80,48},{96,64},{112,80},{... | collective-permute-start | bytes 589832 | tf_op jit(solution)/shard_map/ppermute | solution.py:38
  39.0 7.6 %collective-permute-start.9 = (bf16[128,768]{1,0:T(8,128)(2,1)S(1)}, bf16[128,768]{1,0:T(8,128)(2,1)S(1)}, u32[]{:S(2)}, u32[]{:S(2)}) collective-permute-start(bf16[128,768]{1,0:T(8,128)(2,1)S(1)} %collective-permute-done.8.refs_3_), channel_id=1, source_target_pairs={{0,32},{16,48},{32,64},{48,80},{64,96},{80,112},{96,128},{112,144}... | collective-permute-start | bytes 589832 | tf_op jit(solution)/shard_map/ppermute | solution.py:38
  40.9 7.6 %collective-permute-start.3 = (bf16[128,768]{1,0:T(8,128)(2,1)S(1)}, bf16[128,768]{1,0:T(8,128)(2,1)S(1)}, u32[]{:S(2)}, u32[]{:S(2)}) collective-permute-start(bf16[128,768]{1,0:T(8,128)(2,1)S(1)} %collective-permute-done.2.refs_4_), channel_id=1, source_target_pairs={{0,480},{16,496},{32,0},{48,16},{64,32},{80,48},{96,64},{112,80},{... | collective-permute-start | bytes 589832 | tf_op jit(solution)/shard_map/ppermute | solution.py:38
  46.6 7.6 %collective-permute-start.10 = (bf16[128,768]{1,0:T(8,128)(2,1)S(1)}, bf16[128,768]{1,0:T(8,128)(2,1)S(1)}, u32[]{:S(2)}, u32[]{:S(2)}) collective-permute-start(bf16[128,768]{1,0:T(8,128)(2,1)S(1)} %collective-permute-done.9.refs_5_), channel_id=1, source_target_pairs={{0,32},{16,48},{32,64},{48,80},{64,96},{80,112},{96,128},{112,144}... | collective-permute-start | bytes 589832 | tf_op jit(solution)/shard_map/ppermute | solution.py:38
  48.5 8.3 %collective-permute-start.4 = (bf16[128,768]{1,0:T(8,128)(2,1)S(1)}, bf16[128,768]{1,0:T(8,128)(2,1)S(1)}, u32[]{:S(2)}, u32[]{:S(2)}) collective-permute-start(bf16[128,768]{1,0:T(8,128)(2,1)S(1)} %collective-permute-done.3.refs_6_), channel_id=1, source_target_pairs={{0,480},{16,496},{32,0},{48,16},{64,32},{80,48},{96,64},{112,80},{... | collective-permute-start | bytes 589832 | tf_op jit(solution)/shard_map/ppermute | solution.py:38
  54.2 7.8 %collective-permute-start.11 = (bf16[128,768]{1,0:T(8,128)(2,1)S(1)}, bf16[128,768]{1,0:T(8,128)(2,1)S(1)}, u32[]{:S(2)}, u32[]{:S(2)}) collective-permute-start(bf16[128,768]{1,0:T(8,128)(2,1)S(1)} %collective-permute-done.10.refs_7_), channel_id=1, source_target_pairs={{0,32},{16,48},{32,64},{48,80},{64,96},{80,112},{96,128},{112,144}... | collective-permute-start | bytes 589832 | tf_op jit(solution)/shard_map/ppermute | solution.py:38
  56.8 7.9 %collective-permute-start.5 = (bf16[128,768]{1,0:T(8,128)(2,1)S(1)}, bf16[128,768]{1,0:T(8,128)(2,1)S(1)}, u32[]{:S(2)}, u32[]{:S(2)}) collective-permute-start(bf16[128,768]{1,0:T(8,128)(2,1)S(1)} %collective-permute-done.4.refs_8_), channel_id=1, source_target_pairs={{0,480},{16,496},{32,0},{48,16},{64,32},{80,48},{96,64},{112,80},{... | collective-permute-start | bytes 589832 | tf_op jit(solution)/shard_map/ppermute | solution.py:38
  62.1 7.9 %collective-permute-start.12 = (bf16[128,768]{1,0:T(8,128)(2,1)S(1)}, bf16[128,768]{1,0:T(8,128)(2,1)S(1)}, u32[]{:S(2)}, u32[]{:S(2)}) collective-permute-start(bf16[128,768]{1,0:T(8,128)(2,1)S(1)} %collective-permute-done.11.refs_9_), channel_id=1, source_target_pairs={{0,32},{16,48},{32,64},{48,80},{64,96},{80,112},{96,128},{112,144}... | collective-permute-start | bytes 589832 | tf_op jit(solution)/shard_map/ppermute | solution.py:38
  64.7 7.8 %collective-permute-start.6 = (bf16[128,768]{1,0:T(8,128)(2,1)S(1)}, bf16[128,768]{1,0:T(8,128)(2,1)}, u32[]{:S(2)}, u32[]{:S(2)}) collective-permute-start(bf16[128,768]{1,0:T(8,128)(2,1)S(1)} %collective-permute-done.5.refs_10_), channel_id=1, source_target_pairs={{0,480},{16,496},{32,0},{48,16},{64,32},{80,48},{96,64},{112,80},{... | collective-permute-start | bytes 589832 | tf_op jit(solution)/shard_map/ppermute | solution.py:38
  69.9 7.7 %collective-permute-start.13 = (bf16[128,768]{1,0:T(8,128)(2,1)S(1)}, bf16[128,768]{1,0:T(8,128)(2,1)}, u32[]{:S(2)}, u32[]{:S(2)}) collective-permute-start(bf16[128,768]{1,0:T(8,128)(2,1)S(1)} %collective-permute-done.12.refs_11_), channel_id=1, source_target_pairs={{0,32},{16,48},{32,64},{48,80},{64,96},{80,112},{96,128},{112,144}... | collective-permute-start | bytes 589832 | tf_op jit(solution)/shard_map/ppermute | solution.py:38
  72.5 13.1 %collective-permute-start.14 = (bf16[128,768]{1,0:T(8,128)(2,1)}, bf16[128,768]{1,0:T(8,128)(2,1)}, u32[]{:S(2)}, u32[]{:S(2)}) collective-permute-start(bf16[128,768]{1,0:T(8,128)(2,1)} %collective-permute-done.6.refs_0_), channel_id=1, source_target_pairs={{0,480},{16,496},{32,0},{48,16},{64,32},{80,48},{96,64},{112,80},{... | collective-permute-start | bytes 589832 | tf_op jit(solution)/shard_map/ppermute | solution.py:38
  77.7 8.4 %collective-permute-start.15 = (bf16[128,768]{1,0:T(8,128)(2,1)}, bf16[128,768]{1,0:T(8,128)(2,1)}, u32[]{:S(2)}, u32[]{:S(2)}) collective-permute-start(bf16[128,768]{1,0:T(8,128)(2,1)} %collective-permute-done.13.refs_1_), channel_id=1, source_target_pairs={{0,32},{16,48},{32,64},{48,80},{64,96},{80,112},{96,128},{112,144}... | collective-permute-start | bytes 589832 | tf_op jit(solution)/shard_map/ppermute | solution.py:38
  85.6 12.1 %copy-start.10 = (f32[2,256]{1,0:T(2,128)S(1)}, f32[2,256]{1,0:T(2,128)}, u32[]{:S(2)}) copy-start(f32[2,256]{1,0:T(2,128)} %decays_ref.1) | copy-start | bytes 6148
  85.6 12.1 %copy-start.12 = (s32[256]{0:T(256)S(1)}, s32[256]{0:T(256)}, u32[]{:S(2)}) copy-start(s32[256]{0:T(256)} %param.13) | copy-start | bytes 3076
  87.8 49.1 %copy-start.13 = (f32[2]{0:T(128)S(1)}, f32[2]{0:T(128)}, u32[]{:S(2)}) copy-start(f32[2]{0:T(128)} %skip_ref.1) | copy-start | bytes 28
  87.8 11.8 %collective-permute-start.16 = (f32[256,768]{1,0:T(8,128)S(1)}, f32[256,768]{1,0:T(8,128)S(1)}, u32[]{:S(2)}, u32[]{:S(2)}) collective-permute-start(f32[256,768]{1,0:T(8,128)S(1)} %get-tuple-element.21), channel_id=1, source_target_pairs={{0,16},{16,0},{32,48},{48,32},{64,80},{80,64},{96,112},{112,96},{1... | collective-permute-start | bytes 2359304 | tf_op jit(solution)/shard_map/ppermute | solution.py:42
  100.0 3.2 %collective-permute-start.17 = (f32[136,128]{1,0:T(8,128)S(1)}, f32[136,128]{1,0:T(8,128)S(1)}, u32[]{:S(2)}, u32[]{:S(2)}) collective-permute-start(f32[136,128]{1,0:T(8,128)S(1)} %get-tuple-element.28), channel_id=1, source_target_pairs={{0,16},{16,0},{32,48},{48,32},{64,80},{80,64},{96,112},{112,96},{1... | collective-permute-start | bytes 208904 | tf_op jit(solution)/shard_map/ppermute | solution.py:42
  127.7 23.6 %copy-start.11 = (f32[2,128]{1,0:T(2,128)S(1)}, f32[2,128]{1,0:T(2,128)}, u32[]{:S(2)}) copy-start(f32[2,128]{1,0:T(2,128)} %param.10) | copy-start | bytes 3076
  127.9 10.0 %collective-permute-start.18 = (f32[128,128]{1,0:T(8,128)S(1)}, f32[128,128]{1,0:T(8,128)S(1)}, u32[]{:S(2)}, u32[]{:S(2)}) collective-permute-start(f32[128,128]{1,0:T(8,128)S(1)} %get-tuple-element.32), channel_id=1, source_target_pairs={{0,16},{16,0},{32,48},{48,32},{64,80},{80,64},{96,112},{112,96},{1... | collective-permute-start | bytes 196616 | tf_op jit(solution)/shard_map/ppermute | solution.py:42
  (11 other events, 11.9 us)
